TPU v7x, 32 devices: a whole 2x2x4 slice. The times are simulated.
32 devices in a mesh: sample: 2 (over y), grid: 16 (over z, x, core).
Axes of the slice: x: 2, y: 2, z: 4, core: 2. Of those that a mesh axis runs over, the one named last changes fastest.
Arguments:
- orbitals: float32 [64, 16, 32, 128], P('sample', 'grid'), parts along dimension 0, may hold values from -6 to 6
- cotangent: float32 [64, 16, 32, 128], P('sample', 'grid'), parts along dimension 0, may hold values from -6 to 6
- potential: float32 [16, 32, 128], P('grid'), may hold values from 0 to 1.5
- cheb_coef: float32 [4], replicated, may hold values from 0.3 to 1
- energy: float32 [32], replicated, may hold values from 0.5 to 2
- proj_cell: int32 [32768], P('grid'), may hold values from 0 to 4095, as said below
- proj_atom: int32 [32768], P('grid'), may hold values from 0 to 31, as said below
- proj_value: float32 [32768], P('grid'), may hold values from -0.1875 to 0.1875
Outputs:
- grad_orbitals: float32 [64, 16, 32, 128], P('sample', 'grid'), parts along dimension 0
- grad_potential: float32 [32, 32, 128], P(('sample', 'grid')), parts along dimension 0
- grad_energy: float32 [64], P(('sample', 'grid')), parts along dimension 0
There are 2 independent parts, one for each index of `sample`. A program takes and returns all parts, laid end to end along the dimension named above; an argument that names none is the same for every part. Nothing has to cross between parts.
Inputs may be any that keep to these rules, and one draw needn't show every extreme that they name: Point i lies in the grid slab of device i // 2048 of the grid axis; proj_cell[i] = x * 32 * 128 + y * 128 + z with x counted within that slab; points may repeat. `proj_atom`: atom a is homed on grid device a // 2; the atom of point i is homed on device i // 2048 or on one of its two neighbours, the devices taken as a closed loop.
All inputs are finite; a program needn't handle non-finite values.
Results may differ from a plain program's by a relative error of at most 0.00029.
Values sent between devices are 32-bit elements; how exact they have to be, the bound alone decides.
No kernel may reach another device: no remote copies, remote signals or barrier semaphores. Data moves between devices by JAX's collectives and lax.ppermute only.
A program may use at most 64 MiB of HBM per device.

v0:
```python
import jax
import jax.numpy as jnp
from jax import lax
from jax.sharding import PartitionSpec as P

spectral_center = 4.5
spectral_half = 4.5


def extended(x, sides, width):
    for axis, dim in sides:
        devices, length = (lax.axis_size(axis), x.shape[dim])
        up = [(i, (i + 1) % devices) for i in range(devices)]
        down = [(j, i) for i, j in up]
        last = lax.slice_in_dim(x, length - width, length, axis=dim)
        initial = lax.slice_in_dim(x, 0, width, axis=dim)
        before = lax.ppermute(last, axis, up)
        after = lax.ppermute(initial, axis, down)
        x = jnp.concatenate([before, x, after], axis=dim)
    return x


def per_device(orbitals, cotangent, potential, cheb_coef, energy, proj_cell, proj_atom, proj_value):
    plane_shape = orbitals.shape[1:]
    cell_count = plane_shape[0] * plane_shape[1] * plane_shape[2]
    devices = lax.axis_size("grid")
    my_index = lax.axis_index("grid")
    atoms_all = energy.shape[0]
    atom_dev = atoms_all // devices
    first_atom = (my_index + devices - 1) % devices * atom_dev
    slot_index = (proj_atom - first_atom + atoms_all) % atoms_all
    one_hot = (slot_index[:, None] == jnp.arange(3 * atom_dev, dtype=jnp.int32)[None, :]).astype(
        jnp.float32
    )
    weights = one_hot * proj_value[:, None]
    energy_near = lax.dynamic_slice_in_dim(
        jnp.concatenate([energy, energy]), first_atom, 3 * atom_dev
    )

    def combine_sums(partial_value):
        rows_count = partial_value.shape[0]
        spread_wide = jnp.zeros((rows_count, 2 * atoms_all), jnp.float32)
        spread_wide = lax.dynamic_update_slice_in_dim(spread_wide, partial_value, first_atom, 1)
        placed = spread_wide[:, :atoms_all] + spread_wide[:, atoms_all:]
        total = lax.psum(placed, "grid")
        near_coef = lax.dynamic_slice_in_dim(
            jnp.concatenate([total, total], 1), first_atom, 3 * atom_dev, 1
        )
        return near_coef

    def apply_operator(field, extra):
        rows_count = field.shape[0]
        padded = extended(field, (("grid", 1),), 1)
        beside = padded[:, 2:] + padded[:, :-2]
        beside = beside + jnp.roll(field, 1, axis=2) + jnp.roll(field, -1, axis=2)
        beside = beside + jnp.roll(field, 1, axis=3) + jnp.roll(field, -1, axis=3)
        kinetic = -0.5 * (beside - 6.0 * field)
        flat = field.reshape(rows_count, cell_count)
        picks = flat[:, proj_cell]
        if extra is not None:
            picks = jnp.concatenate(
                [picks, extra.reshape(extra.shape[0], cell_count)[:, proj_cell]], 0
            )
        partial_value = jnp.dot(
            picks, weights, precision=lax.Precision.HIGHEST, preferred_element_type=jnp.float32
        )
        near_coef = combine_sums(partial_value)
        field_coef = near_coef[:rows_count]
        spread = jnp.dot(
            field_coef * energy_near[None, :],
            weights.T,
            precision=lax.Precision.HIGHEST,
            preferred_element_type=jnp.float32,
        )
        nonlocal_part = (
            jnp.zeros((rows_count, cell_count), jnp.float32)
            .at[:, proj_cell]
            .add(spread)
            .reshape(field.shape)
        )
        result = (
            kinetic + potential[None] * field + nonlocal_part - spectral_center * field
        ) / spectral_half
        owned = near_coef[:, atom_dev : 2 * atom_dev]
        return (result, owned[:rows_count], owned[rows_count:])

    back_three = cheb_coef[3] * cotangent
    term_one, proj_zero, unused = apply_operator(orbitals, None)
    image, proj_one, unused = apply_operator(term_one, None)
    term_two = 2.0 * image - orbitals
    image, coef_three, unused = apply_operator(back_three, None)
    back_two = cheb_coef[2] * cotangent + 2.0 * image
    image, coef_two, unused = apply_operator(back_two, None)
    back_one = cheb_coef[1] * cotangent + 2.0 * image - back_three
    image, coef_one, proj_two = apply_operator(back_one, term_two)
    grad_orbitals = cheb_coef[0] * cotangent + image - back_two
    grad_potential = (
        jnp.sum(
            back_one * orbitals + 2.0 * back_two * term_one + 2.0 * back_three * term_two, axis=0
        )
        / spectral_half
    )
    grad_energy = (
        jnp.sum(
            coef_one * proj_zero + 2.0 * coef_two * proj_one + 2.0 * coef_three * proj_two, axis=0
        )
        / spectral_half
    )
    return (grad_orbitals, grad_potential, grad_energy)


def solution(mesh):
    placed = (
        P("sample", "grid", None, None),
        P("sample", "grid", None, None),
        P("grid", None, None),
        P(),
        P(),
        P("grid"),
        P("grid"),
        P("grid"),
    )
    return jax.shard_map(
        per_device,
        mesh=mesh,
        in_specs=placed,
        out_specs=(
            P("sample", "grid", None, None),
            P(("sample", "grid"), None, None),
            P(("sample", "grid")),
        ),
        check_vma=False,
    )
```

profile of v0, /device:TPU:1, one launch (start us, length us, event | category | flops | bytes accessed | tf_op | source)
XLA Modules:
  0.0 397.9 jit_solution(13894875550771868777)
XLA Ops:
  0.7 2.6 collective-permute-start.7
  6.5 2.9 collective-permute-start
  16.7 9.2 %gather_fusion = f32[2048,32]{1,0:T(8,128)} fusion(f32[32,4096]{0,1:T(8,128)} %bitcast.27, s32[2048]{0:T(1024)S(1)} %get-tuple-element.52), kind=kCustom, calls=%fused_computation | custom fusion | bytes 532480 | tf_op jit(solution)/shard_map/gather | solution.py:59
  25.9 3.6 fusion.18
  29.6 7.6 %gather_fusion.3 = f32[2048,32]{1,0:T(8,128)} fusion(f32[32,4096]{0,1:T(8,128)S(1)} %bitcast.26, s32[2048]{0:T(1024)S(1)} %get-tuple-element.52), kind=kCustom, calls=%fused_computation.3 | custom fusion | bytes 532480 | tf_op jit(solution)/shard_map/gather | solution.py:59
  37.3 3.6 fusion.10
  41.0 61.4 %all-reduce.1 = (f32[32,32]{0,1:T(8,128)S(1)}, f32[32,32]{0,1:T(8,128)S(1)}) all-reduce(f32[32,32]{0,1:T(8,128)S(1)} %slice_add_fusion.4, f32[32,32]{0,1:T(8,128)S(1)} %slice_add_fusion.2), channel_id=1, replica_groups=mesh['sample'=2,'grid'=16] {'grid'}, use_global_device_ids=true, to_apply=%region_0.1 | all-reduce | flops 2048 | bytes 16384 | tf_op jit(solution)/shard_map/psum | solution.py:45
  102.5 2.3 fusion.8
  104.8 12.5 %scatter_custom_fusion.2 = f32[32,4096]{0,1:T(8,128)S(1)} fusion(s32[2048]{0:T(1024)S(1)} %get-tuple-element.53, f32[2048,32]{1,0:T(8,128)} %fusion.8, f32[]{:T(128)} %constant.60.clone.1), kind=kCustom, calls=%fused_computation.39 | custom fusion | flops 65536 | bytes 524800 | tf_op jit(solution)/shard_map/scatter-add | solution.py:78
  118.8 2.3 fusion.16
  121.1 12.3 %scatter_custom_fusion = f32[32,4096]{0,1:T(8,128)S(1)} fusion(s32[2048]{0:T(1024)S(1)} %get-tuple-element.53, f32[2048,32]{1,0:T(8,128)} %fusion.16, f32[]{:T(128)} %constant.60.clone.1), kind=kCustom, calls=%fused_computation.43 | custom fusion | flops 65536 | bytes 524800 | tf_op jit(solution)/shard_map/scatter-add | solution.py:78
  142.2 5.0 %collective-permute-start.8 = (f32[32,1,32,128]{3,2,1,0:T(8,128)S(1)}, f32[32,1,32,128]{3,2,1,0:T(8,128)}, u32[]{:S(2)}, u32[]{:S(2)}) collective-permute-start(f32[32,1,32,128]{3,2,1,0:T(8,128)S(1)} %get-tuple-element.10), channel_id=1, source_target_pairs={{1,0},{2,1},{3,2},{4,3},{5,4},{6,5},{7,6},{8,7},{9,8},{10,9},{11,1... | collective-permute-start | bytes 1572872 | tf_op jit(solution)/shard_map/ppermute | solution.py:18
  149.8 3.0 fusion.42
  157.7 9.2 %gather_fusion.4 = f32[2048,32]{1,0:T(8,128)} fusion(f32[32,4096]{0,1:T(8,128)} %bitcast.25, s32[2048]{0:T(1024)S(1)} %get-tuple-element.52), kind=kCustom, calls=%fused_computation.4 | custom fusion | bytes 532480 | tf_op jit(solution)/shard_map/gather | solution.py:59
  166.9 3.6 fusion.6
  170.6 9.2 %gather_fusion.1 = f32[2048,32]{1,0:T(8,128)} fusion(f32[32,4096]{0,1:T(8,128)} %bitcast.28, s32[2048]{0:T(1024)S(1)} %get-tuple-element.52), kind=kCustom, calls=%fused_computation.1 | custom fusion | bytes 532480 | tf_op jit(solution)/shard_map/gather | solution.py:59
  179.8 3.6 fusion.14
  183.5 60.0 %all-reduce = (f32[32,32]{0,1:T(8,128)S(1)}, f32[32,32]{0,1:T(8,128)S(1)}) all-reduce(f32[32,32]{0,1:T(8,128)S(1)} %slice_add_fusion.1, f32[32,32]{0,1:T(8,128)S(1)} %slice_add_fusion.3), channel_id=1, replica_groups=mesh['sample'=2,'grid'=16] {'grid'}, use_global_device_ids=true, to_apply=%region_6.7 | all-reduce | flops 2048 | bytes 16384 | tf_op jit(solution)/shard_map/psum | solution.py:45
  243.5 2.3 fusion.4
  245.8 13.2 %scatter_custom_fusion.3 = f32[32,4096]{0,1:T(8,128)} fusion(s32[2048]{0:T(1024)S(1)} %get-tuple-element.53, f32[2048,32]{1,0:T(8,128)} %fusion.4, f32[]{:T(128)} %constant.60.clone.1), kind=kCustom, calls=%fused_computation.37 | custom fusion | flops 65536 | bytes 524800 | tf_op jit(solution)/shard_map/scatter-add | solution.py:78
  259.1 2.3 copy.23
  263.6 13.5 %scatter_custom_fusion.1 = f32[32,4096]{0,1:T(8,128)} fusion(s32[2048]{0:T(1024)S(1)} %get-tuple-element.53, f32[2048,32]{1,0:T(8,128)} %fusion.12, f32[]{:T(128)} %constant.60.clone.1), kind=kCustom, calls=%fused_computation.41 | custom fusion | flops 65536 | bytes 524800 | tf_op jit(solution)/shard_map/scatter-add | solution.py:78
  277.1 3.0 copy.16
  282.3 5.1 %add_reduce_fusion = (f32[32,128]{1,0:T(8,128)S(1)}, f32[32,1,32,128]{3,2,1,0:T(8,128)S(1)}, f32[32,1,32,128]{3,2,1,0:T(8,128)}) fusion(f32[32,1,32,128]{3,2,1,0:T(8,128)S(1)} %fusion.42, f32[32,1,32,128]{3,2,1,0:T(8,128)S(1)} %copy-done, f32[32,1,32,128]{3,2,1,0:T(8,128)S(1)} %copy-done.1, f32[]{:T(128)} %bitcast.3, ...), kind=kLoop, calls=%fused_computation.100 | loop fusion | flops 6418432 | bytes 10534920 | tf_op jit(solution)/shard_map/reduce_sum | solution.py:98
  289.4 7.0 %gather_fusion.2 = f32[2048,32]{1,0:T(8,128)S(1)} fusion(f32[32,4096]{0,1:T(8,128)} %bitcast.35, s32[2048]{0:T(1024)S(1)} %get-tuple-element.52), kind=kCustom, calls=%fused_computation.2 | custom fusion | bytes 532480 | tf_op jit(solution)/shard_map/gather | solution.py:59
  298.5 9.2 %gather_fusion.5 = f32[2048,32]{1,0:T(8,128)} fusion(f32[32,4096]{0,1:T(8,128)} %bitcast.30, s32[2048]{0:T(1024)S(1)} %get-tuple-element.52), kind=kCustom, calls=%fused_computation.5 | custom fusion | bytes 532480 | tf_op jit(solution)/shard_map/gather | solution.py:62
  307.7 3.9 fusion.2
  311.7 57.6 %psum.39 = f32[64,32]{0,1:T(8,128)S(1)} all-reduce(f32[64,32]{0,1:T(8,128)S(1)} %slice_add_fusion), channel_id=1, replica_groups=mesh['sample'=2,'grid'=16] {'grid'}, use_global_device_ids=true, to_apply=%region_8.9 | all-reduce | flops 2048 | bytes 16384 | tf_op jit(solution)/shard_map/psum | solution.py:45
  372.0 5.1 %collective-permute-start.4 = (f32[32,1,32,128]{3,2,1,0:T(8,128)S(1)}, f32[32,1,32,128]{3,2,1,0:T(8,128)}, u32[]{:S(2)}, u32[]{:S(2)}) collective-permute-start(f32[32,1,32,128]{3,2,1,0:T(8,128)S(1)} %get-tuple-element.8), channel_id=1, source_target_pairs={{1,0},{2,1},{3,2},{4,3},{5,4},{6,5},{7,6},{8,7},{9,8},{10,9},{11,1... | collective-permute-start | bytes 1572872 | tf_op jit(solution)/shard_map/ppermute | solution.py:18
  377.6 13.2 %scatter_custom_fusion.4 = f32[32,4096]{0,1:T(8,128)} fusion(s32[2048]{0:T(1024)S(1)} %get-tuple-element.53, f32[2048,32]{1,0:T(8,128)} %fusion, f32[]{:T(128)} %constant.60.clone.1), kind=kCustom, calls=%fused_computation.35 | custom fusion | flops 65536 | bytes 524800 | tf_op jit(solution)/shard_map/scatter-add | solution.py:78
  390.8 2.3 copy.26
  394.1 3.4 fusion.64
  (134 shorter events, 41.3 us)
Async XLA Ops:
  0.6 10.7 %copy-start = (f32[32,1,32,128]{3,2,1,0:T(8,128)S(1)}, f32[32,1,32,128]{3,2,1,0:T(8,128)}, u32[]{:S(2)}) copy-start(f32[32,1,32,128]{3,2,1,0:T(8,128)} %param.8) | copy-start | bytes 1572868
  0.6 136.4 %collective-permute-start.6 = (f32[32,1,32,128]{3,2,1,0:T(8,128)}, f32[32,1,32,128]{3,2,1,0:T(8,128)}, u32[]{:S(2)}, u32[]{:S(2)}) collective-permute-start(f32[32,1,32,128]{3,2,1,0:T(8,128)} %param.8), channel_id=1, source_target_pairs={{1,0},{2,1},{3,2},{4,3},{5,4},{6,5},{7,6},{8,7},{9,8},{10,9},{11,1... | collective-permute-start | bytes 1572872 | tf_op jit(solution)/shard_map/ppermute | solution.py:18
  0.7 136.3 %collective-permute-start.7 = (f32[32,1,32,128]{3,2,1,0:T(8,128)}, f32[32,1,32,128]{3,2,1,0:T(8,128)}, u32[]{:S(2)}, u32[]{:S(2)}) collective-permute-start(f32[32,1,32,128]{3,2,1,0:T(8,128)} %param.8), channel_id=1, source_target_pairs={{0,1},{1,2},{2,3},{3,4},{4,5},{5,6},{6,7},{7,8},{8,9},{9,10},{10,1... | collective-permute-start | bytes 1572872 | tf_op jit(solution)/shard_map/ppermute | solution.py:17
  6.5 143.2 %collective-permute-start = (f32[32,1,32,128]{3,2,1,0:T(8,128)S(1)}, f32[32,1,32,128]{3,2,1,0:T(8,128)}, u32[]{:S(2)}, u32[]{:S(2)}) collective-permute-start(f32[32,1,32,128]{3,2,1,0:T(8,128)S(1)} %broadcast_multiply_fusion.1), channel_id=1, source_target_pairs={{1,0},{2,1},{3,2},{4,3},{5,4},{6,5},{7,6},{8,7},{9,8},{10,9},{11,1... | collective-permute-start | bytes 1572872 | tf_op jit(solution)/shard_map/ppermute | solution.py:18
  9.3 140.3 %collective-permute-start.1 = (f32[32,1,32,128]{3,2,1,0:T(8,128)S(1)}, f32[32,1,32,128]{3,2,1,0:T(8,128)}, u32[]{:S(2)}, u32[]{:S(2)}) collective-permute-start(f32[32,1,32,128]{3,2,1,0:T(8,128)S(1)} %broadcast_multiply_fusion.1), channel_id=1, source_target_pairs={{0,1},{1,2},{2,3},{3,4},{4,5},{5,6},{6,7},{7,8},{8,9},{9,10},{10,1... | collective-permute-start | bytes 1572872 | tf_op jit(solution)/shard_map/ppermute | solution.py:17
  14.2 2.4 copy-start.27
  14.2 2.4 copy-start.26
  15.4 10.5 %copy-start.24 = (f32[2048]{0:T(1024)S(1)}, f32[2048]{0:T(1024)}, u32[]{:S(2)}) copy-start(f32[2048]{0:T(1024)} %param.15) | copy-start | bytes 24580
  29.5 72.9 %copy-start.28 = (f32[32]{0:T(128)S(1)}, f32[32]{0:T(128)}, u32[]{:S(2)}) copy-start(f32[32]{0:T(128)} %param.12) | copy-start | bytes 388
  121.1 13.8 %copy-start.25 = (f32[1,32,128]{2,1,0:T(8,128)S(1)}, f32[1,32,128]{2,1,0:T(8,128)}, u32[]{:S(2)}) copy-start(f32[1,32,128]{2,1,0:T(8,128)} %param.10) | copy-start | bytes 49156
  134.9 2.2 copy-start.4
  134.9 2.2 copy-start.14
  134.9 2.2 copy-start.15
  134.9 2.2 copy-start.16
  134.9 2.2 copy-start.17
  134.9 2.2 copy-start.18
  134.9 2.4 copy-start.19
  142.2 138.4 %collective-permute-start.8 = (f32[32,1,32,128]{3,2,1,0:T(8,128)S(1)}, f32[32,1,32,128]{3,2,1,0:T(8,128)}, u32[]{:S(2)}, u32[]{:S(2)}) collective-permute-start(f32[32,1,32,128]{3,2,1,0:T(8,128)S(1)} %get-tuple-element.10), channel_id=1, source_target_pairs={{1,0},{2,1},{3,2},{4,3},{5,4},{6,5},{7,6},{8,7},{9,8},{10,9},{11,1... | collective-permute-start | bytes 1572872 | tf_op jit(solution)/shard_map/ppermute | solution.py:18
  147.3 133.4 %collective-permute-start.9 = (f32[32,1,32,128]{3,2,1,0:T(8,128)S(1)}, f32[32,1,32,128]{3,2,1,0:T(8,128)}, u32[]{:S(2)}, u32[]{:S(2)}) collective-permute-start(f32[32,1,32,128]{3,2,1,0:T(8,128)S(1)} %get-tuple-element.10), channel_id=1, source_target_pairs={{0,1},{1,2},{2,3},{3,4},{4,5},{5,6},{6,7},{7,8},{8,9},{9,10},{10,1... | collective-permute-start | bytes 1572872 | tf_op jit(solution)/shard_map/ppermute | solution.py:17
  147.3 2.4 copy-start.1
  147.3 2.4 copy-start.2
  147.3 2.4 copy-start.6
  147.3 2.4 copy-start.7
  147.3 2.4 copy-start.21
  147.3 2.4 copy-start.22
  147.3 2.5 copy-start.23
  155.9 124.7 %collective-permute-start.2 = (f32[32,1,32,128]{3,2,1,0:T(8,128)S(1)}, f32[32,1,32,128]{3,2,1,0:T(8,128)}, u32[]{:S(2)}, u32[]{:S(2)}) collective-permute-start(f32[32,1,32,128]{3,2,1,0:T(8,128)S(1)} %fusion.42), channel_id=1, source_target_pairs={{1,0},{2,1},{3,2},{4,3},{5,4},{6,5},{7,6},{8,7},{9,8},{10,9},{11,1... | collective-permute-start | bytes 1572872 | tf_op jit(solution)/shard_map/ppermute | solution.py:18
  156.4 124.2 %collective-permute-start.3 = (f32[32,1,32,128]{3,2,1,0:T(8,128)S(1)}, f32[32,1,32,128]{3,2,1,0:T(8,128)}, u32[]{:S(2)}, u32[]{:S(2)}) collective-permute-start(f32[32,1,32,128]{3,2,1,0:T(8,128)S(1)} %fusion.42), channel_id=1, source_target_pairs={{0,1},{1,2},{2,3},{3,4},{4,5},{5,6},{6,7},{7,8},{8,9},{9,10},{10,1... | collective-permute-start | bytes 1572872 | tf_op jit(solution)/shard_map/ppermute | solution.py:17
  280.2 2.1 copy-start.20
  287.4 9.0 %copy-start.5 = (f32[32,1,32,128]{3,2,1,0:T(8,128)S(1)}, f32[32,1,32,128]{3,2,1,0:T(8,128)}, u32[]{:S(2)}) copy-start(f32[32,1,32,128]{3,2,1,0:T(8,128)} %get-tuple-element.9) | copy-start | bytes 1572868
  372.0 22.1 %collective-permute-start.4 = (f32[32,1,32,128]{3,2,1,0:T(8,128)S(1)}, f32[32,1,32,128]{3,2,1,0:T(8,128)}, u32[]{:S(2)}, u32[]{:S(2)}) collective-permute-start(f32[32,1,32,128]{3,2,1,0:T(8,128)S(1)} %get-tuple-element.8), channel_id=1, source_target_pairs={{1,0},{2,1},{3,2},{4,3},{5,4},{6,5},{7,6},{8,7},{9,8},{10,9},{11,1... | collective-permute-start | bytes 1572872 | tf_op jit(solution)/shard_map/ppermute | solution.py:18
  377.0 17.0 %collective-permute-start.5 = (f32[32,1,32,128]{3,2,1,0:T(8,128)S(1)}, f32[32,1,32,128]{3,2,1,0:T(8,128)}, u32[]{:S(2)}, u32[]{:S(2)}) collective-permute-start(f32[32,1,32,128]{3,2,1,0:T(8,128)S(1)} %get-tuple-element.8), channel_id=1, source_target_pairs={{0,1},{1,2},{2,3},{3,4},{4,5},{5,6},{6,7},{7,8},{8,9},{9,10},{10,1... | collective-permute-start | bytes 1572872 | tf_op jit(solution)/shard_map/ppermute | solution.py:17
  (7 other events, 10.5 us)
where the time goes:
time: 406 us; the launch traced here: 398 us
  blocking collectives  179 us (44%)
  local copies, waits for them, and re-layouts  88.9 us (22%)
  other arithmetic  81.4 us (20%)
  matrix products  29.5 us (7%)
  starting transfers between devices  17.4 us (4%)
    psum x3, blocking collectives, combine_sums(): total = lax.psum(placed, 'grid')  179 us
    scatter-add x5, other arithmetic, apply_operator(): nonlocal_part = jnp.zeros((rows_count, cell_count), jnp.float32).at[:, pr...  64.8 us
    gather x5, local copies, waits for them, and re-layouts, apply_operator(): picks = flat[:, proj_cell]  42.3 us
    dot_general x5, matrix products, apply_operator(): jnp.dot(picks, weights, precision=lax.Precision.HIGHEST, preferred_elemen...  18.1 us
    ppermute x5, starting transfers between devices, extended(): after = lax.ppermute(initial, axis, down)  13.6 us
    dot_general x5, matrix products, apply_operator(): jnp.dot(field_coef * energy_near[None, :], weights.T, precision=lax.Preci...  11.4 us
    reshape x5, local copies, waits for them, and re-layouts, apply_operator(): nonlocal_part = jnp.zeros((rows_count, cell_count), jnp.float32).at[:, pr...  10.5 us
    gather x1, local copies, waits for them, and re-layouts, apply_operator(): extra.reshape(extra.shape[0], cell_count)[:, proj_cell]  9.21 us
  transfers between devices with their start and end apart: 10, of which 0 were waited for; matrix products, arithmetic and copies ran while one was open for 41% of the time, Pallas kernels for 0%

commit v1 on v0

v1 whole, which is shorter than its diff:
```python
import functools

import jax
import jax.numpy as jnp
from jax import lax
from jax.experimental import pallas as pl
from jax.experimental.pallas import tpu as pltpu
from jax.sharding import PartitionSpec as P

spectral_center = 4.5
spectral_half = 4.5

GROUP = 4
LANES = 128
F32 = jnp.float32


def call(body, outs, *args, scratch=(), smem=(), any_args=(), any_outs=()):
    in_specs, operands = [], []
    for n, a in enumerate(args):
        if n in smem:
            in_specs.append(pl.BlockSpec(memory_space=pltpu.SMEM))
        elif n in any_args:
            in_specs.append(pl.BlockSpec(memory_space=pl.ANY))
        else:
            in_specs.append(pl.BlockSpec(memory_space=pltpu.VMEM))
            a = pltpu.with_memory_space_constraint(a, pltpu.VMEM)
        operands.append(a)
    out_shape, out_specs = [], []
    for n, shape in enumerate(outs):
        if n in any_outs:
            out_shape.append(jax.ShapeDtypeStruct(shape, F32))
            out_specs.append(pl.BlockSpec(memory_space=pl.ANY))
        else:
            out_shape.append(pltpu.VMEM(shape, F32))
            out_specs.append(pl.BlockSpec(memory_space=pltpu.VMEM))
    return pl.pallas_call(
        body,
        out_shape=out_shape,
        in_specs=in_specs,
        out_specs=out_specs,
        scratch_shapes=list(scratch),
        compiler_params=pltpu.CompilerParams(vmem_limit_bytes=16 << 20),
    )(*operands)


def lane_iota(shape):
    return lax.broadcasted_iota(jnp.int32, shape, len(shape) - 1)


def prep_kernel(devices, atoms, idx, cell, atom, value, pot, out):
    rows = cell.shape[0]
    atom_dev = atoms // devices
    shifted = atom[...] + (atoms - (idx[0] - 1) * atom_dev)
    shifted = jnp.where(shifted >= 2 * atoms, shifted - 2 * atoms, shifted)
    slot = jnp.where(shifted >= atoms, shifted - atoms, shifted)
    out[0:rows, :] = cell[...].astype(F32)
    out[rows : 2 * rows, :] = slot.astype(F32)
    out[2 * rows : 3 * rows, :] = value[...]
    out[3 * rows :, :] = pot[...]


def pack_kernel(rows, idx, field, *refs):
    outs, sems = refs[:GROUP], refs[GROUP]
    k = lax.rem(idx[0], GROUP)
    copies = []
    for j in range(GROUP):
        first = pl.multiple_of((k ^ j) * rows, rows)
        copies.append(
            pltpu.make_async_copy(field.at[pl.ds(first, rows)], outs[j], sems.at[j])
        )
    for copy in copies:
        copy.start()
    for copy in copies:
        copy.wait()


def dense_kernel(ny, slots, idx, *refs):
    ins, out = refs[:GROUP], refs[GROUP]
    k = lax.rem(idx[0], GROUP)
    rows = (ins[0].shape[0] - ny) // 3
    count = rows * LANES
    place = lax.broadcasted_iota(jnp.int32, (ny * 8, count), 0)
    column = lax.broadcasted_iota(jnp.int32, (LANES, count), 0)
    for j in range(GROUP):
        src = ins[j]
        flat = lambda part: jnp.concatenate(
            [src[part * rows + r : part * rows + r + 1, :] for r in range(rows)], axis=1
        )
        cell = flat(0).astype(jnp.int32)
        slot = flat(1).astype(jnp.int32)
        value = flat(2)
        code = (cell // LANES) * 8 + slot
        z = cell % LANES
        left = jnp.where(place == code, 1.0, 0.0).astype(jnp.bfloat16)
        hit = column == z
        high = value.astype(jnp.bfloat16).astype(F32)
        rest = value - high
        middle = rest.astype(jnp.bfloat16).astype(F32)
        low = rest - middle
        dense = None
        for piece in (low, middle, high):
            right = jnp.where(hit, piece, 0.0).astype(jnp.bfloat16)
            term = lax.dot_general(
                left, right, (((1,), (1,)), ((), ())), preferred_element_type=F32
            )
            dense = term if dense is None else dense + term
        first = pl.multiple_of((k ^ j) * ny, ny)
        out[pl.ds(first, ny)] = dense.reshape(ny, 8, LANES)
        pot = (src[3 * rows :, :] - (spectral_center - 3.0)) * (1.0 / spectral_half)
        out[pl.ds(first, ny), slots : slots + 1, :] = pot.reshape(ny, 1, LANES)


def edge_tiles(tile, width, shift):
    lane = lane_iota(tile.shape)
    above = jnp.where(lane < width, pltpu.roll(tile, LANES - shift, 1), 0.0)
    below = jnp.where((lane >= shift) & (lane < shift + width), pltpu.roll(tile, shift, 1), 0.0)
    return above, below


def coef_tile(sums, slots, atom_dev):
    atoms = (GROUP + 2) * atom_dev
    lane = lane_iota((8, LANES))
    tile = jnp.zeros((8, LANES), F32)
    for t in range(atoms):
        total = None
        for p in range(GROUP):
            slot = t - p * atom_dev
            if 0 <= slot < slots:
                total = sums[p][slot] if total is None else total + sums[p][slot]
        tile = jnp.where(lane == t, jnp.sum(total, axis=1, keepdims=True), tile)
    return tile


def relay_kernel(ny, atom_dev, idx, *refs):
    slots = 3 * atom_dev
    ins, (dense, field, tile_out, up, down, sums) = refs[:GROUP], refs[GROUP:]
    k = lax.rem(idx[0], GROUP)
    un = 8
    for j in range(GROUP):
        p = k ^ j
        src = ins[j]

        def body(yb, accs, src=src, p=p):
            accs = list(accs)
            for yy in range(un):
                y = yb * un + yy
                v = src[pl.ds(y, 8, stride=ny), :]
                row = p * ny + y
                field[row] = v
                for s in range(slots):
                    accs[s] = accs[s] + v * dense[row, s : s + 1, :]
            return tuple(accs)

        zero = jnp.zeros((8, LANES), F32)
        accs = lax.fori_loop(0, ny // un, body, (zero,) * slots)
        for s in range(slots):
            sums[p * slots + s] = accs[s]
    parts = [[sums[p * slots + s] for s in range(slots)] for p in range(GROUP)]
    tile = coef_tile(parts, slots, atom_dev)
    tile_out[...] = tile
    above, below = edge_tiles(tile, 2 * atom_dev, GROUP * atom_dev)
    up[ny] = above
    down[ny] = below
    up[0:ny] = field[(GROUP - 1) * ny : GROUP * ny]
    down[0:ny] = field[0:ny]


def step_kernel(kind, ny, devices, atoms, *refs):
    atom_dev = atoms // devices
    slots = 3 * atom_dev
    refs = list(refs)
    take = lambda count: [refs.pop(0) for _ in range(count)]
    idx, cheb, energy, dense, field, tile_in, below, above = take(8)
    if kind == "b1":
        (other,) = take(1)
    elif kind == "t2":
        other, full_zero, b1, tile_b1, b2, tile_b2, cot, full_cot = take(8)
    elif kind == "out":
        other, cot = take(2)
    if kind in ("b2", "t1"):
        new, tile_out, up, down, full_out = refs
    elif kind == "b1":
        new, tile_out, up, down = refs
    elif kind == "t2":
        gp, e_out, e_up, e_down = refs
    else:
        (new,) = refs

    full = tile_in[...] + below[ny] + above[ny]
    if kind in ("b2", "t1"):
        full_out[...] = full
    c0, c1, c2, c3 = [cheb[n] for n in range(4)]
    one = jnp.float32(1.0)
    keep, scale, mix = {
        "t1": (None, one, None),
        "t2": (None, 2.0 * one, -one),
        "b2": (c2, 2.0 * c3, None),
        "b1": (None, 2.0 * one, c1 - c3),
        "out": (None, one, -one),
    }[kind]
    first_atom = lax.rem((idx[0] // GROUP) * GROUP + devices - 1, devices) * atom_dev
    spread = []
    for t in range((GROUP + 2) * atom_dev):
        e = energy[lax.rem(first_atom + t, atoms)] * (scale * (1.0 / spectral_half))
        spread.append(jnp.broadcast_to(full[:, t : t + 1], (8, LANES)) * e)
    side = scale * (-0.5 / spectral_half)
    un = 8
    sums = []
    for p in range(GROUP):

        def body(yb, accs, p=p):
            accs = list(accs)
            rows = []
            for yy in range(un):
                y = yb * un + yy
                row = p * ny + y
                v = field[row]
                later = field[p * ny + lax.rem(y + 1, ny)]
                earlier = field[p * ny + lax.rem(y + ny - 1, ny)]
                under = field[row - ny] if p > 0 else below[y]
                over = field[row + ny] if p < GROUP - 1 else above[y]
                beside = (later + earlier) + (under + over)
                beside = beside + (pltpu.roll(v, 1, 1) + pltpu.roll(v, LANES - 1, 1))
                pot = dense[row, slots : slots + 1, :] * scale
                if keep is not None:
                    pot = pot + keep
                weights = [dense[row, s : s + 1, :] for s in range(slots)]
                a = spread[p * atom_dev] * weights[0]
                for s in range(1, slots):
                    a = a + spread[p * atom_dev + s] * weights[s]
                x = v * pot + beside * side + a
                if mix is not None:
                    x = x + other[row] * mix
                if kind == "out":
                    x = x + cot[row] * c0
                    new[pl.ds(p * 8 * ny + y, 8, stride=ny), :] = x
                elif kind == "t2":
                    g = b1[row] * other[row] + 2.0 * (b2[row] * v)
                    g = g + (2.0 * c3) * (cot[row] * x)
                    rows.append(jnp.sum(g, axis=0, keepdims=True))
                else:
                    new[row] = x
                if kind != "out":
                    for s in range(slots):
                        accs[s] = accs[s] + x * weights[s]
            if kind == "t2":
                start = pl.multiple_of(p * ny + yb * un, un)
                gp[pl.ds(start, un), :] = jnp.concatenate(rows, axis=0) * (1.0 / spectral_half)
            return tuple(accs)

        zero = jnp.zeros((8, LANES), F32)
        init = () if kind == "out" else (zero,) * slots
        sums.append(lax.fori_loop(0, ny // un, body, init))
    if kind == "out":
        return
    tile = coef_tile(sums, slots, atom_dev)
    if kind == "t2":
        e = tile_b1[...] * full_zero[...] + 2.0 * (tile_b2[...] * full)
        e = e + (2.0 * c3) * (full_cot[...] * tile)
        e = jnp.sum(e, axis=0, keepdims=True) * (1.0 / spectral_half)
        e = jnp.broadcast_to(e, (8, LANES))
        e_out[...] = e
        lane = lane_iota(e.shape)
        shift = GROUP * atom_dev
        own = (lane >= atom_dev) & (lane < shift + atom_dev)
        e_up[...] = jnp.where(own, pltpu.roll(e, LANES - shift, 1), 0.0)
        e_down[...] = jnp.where(own, pltpu.roll(e, shift, 1), 0.0)
        return
    tile_out[...] = tile
    over, under = edge_tiles(tile, 2 * atom_dev, GROUP * atom_dev)
    up[ny] = over
    down[ny] = under
    up[0:ny] = new[(GROUP - 1) * ny : GROUP * ny]
    down[0:ny] = new[0:ny]


def sums_kernel(ny, idx, gp, e, e_below, e_above, *outs):
    k = lax.rem(idx[0], GROUP)
    total = e[...] + e_below[...] + e_above[...]
    for j in range(GROUP):
        first = pl.multiple_of((k ^ j) * ny, ny)
        outs[j][0:ny, :] = gp[pl.ds(first, ny), :]
        outs[j][ny:, :] = total


def final_kernel(ny, atom_dev, idx, *refs):
    blocks, parts = refs[:GROUP], refs[GROUP : 2 * GROUP]
    out, gp, e_out, sems = refs[2 * GROUP :]
    k = lax.rem(idx[0], GROUP)
    rows = 8 * ny
    copies = []
    for j in range(GROUP):
        own = pl.ds(pl.multiple_of(k * rows, rows), rows)
        src = blocks[0].at[own] if j == 0 else blocks[j]
        first = pl.multiple_of((k ^ j) * rows, rows)
        copies.append(pltpu.make_async_copy(src, out.at[pl.ds(first, rows)], sems.at[j]))
    for copy in copies:
        copy.start()
    total = (parts[0][...] + parts[1][...]) + (parts[2][...] + parts[3][...])
    gp[...] = total[0:ny]
    e = total[ny:]
    picked = e
    for n in range(GROUP):
        picked = jnp.where(k == n, pltpu.roll(e, LANES - (n + 1) * atom_dev, 1), picked)
    e_out[...] = picked
    for copy in copies:
        copy.wait()


def per_device(orbitals, cotangent, potential, cheb_coef, energy, proj_cell, proj_atom, proj_value):
    orb, _, ny, nz = orbitals.shape
    devices = lax.axis_size("grid")
    slabs = devices // GROUP
    atoms = energy.shape[0]
    atom_dev = atoms // devices
    points = proj_cell.shape[0] // LANES
    assert orb == 8 * GROUP and nz == LANES and devices % GROUP == 0
    idx = lax.axis_index("grid").astype(jnp.int32).reshape(1)
    block = 8 * ny
    plane = GROUP * ny

    def near(x, j):
        return lax.ppermute(x, "grid", [(a, a ^ j) for a in range(devices)])

    to_above = [
        (GROUP * s + m, GROUP * ((s + 1) % slabs) + m) for s in range(slabs) for m in range(GROUP)
    ]
    to_below = [(b, a) for a, b in to_above]

    def halo(up, down):
        return lax.ppermute(up, "grid", to_above), lax.ppermute(down, "grid", to_below)

    def gather(blocks):
        return [blocks[0]] + [near(blocks[j], j) for j in range(1, GROUP)]

    (points_own,) = call(
        functools.partial(prep_kernel, devices, atoms),
        [(3 * points + ny, LANES)],
        idx,
        proj_cell.reshape(points, LANES),
        proj_atom.reshape(points, LANES),
        proj_value.reshape(points, LANES),
        potential.reshape(ny, LANES),
        smem=(0,),
    )
    points_all = [points_own] + [near(points_own, j) for j in range(1, GROUP)]

    def pack(field):
        return call(
            functools.partial(pack_kernel, block),
            [(block, LANES)] * GROUP,
            idx,
            field.reshape(orb * ny, LANES),
            scratch=[pltpu.SemaphoreType.DMA((GROUP,))],
            smem=(0,),
            any_args=(1,),
        )

    cot_blocks = gather(pack(cotangent))
    orb_blocks = gather(pack(orbitals))
    (dense,) = call(
        functools.partial(dense_kernel, ny, 3 * atom_dev),
        [(plane, 8, LANES)],
        idx,
        *points_all,
        smem=(0,),
    )
    field_shape, tile_shape, edge_shape = (plane, 8, LANES), (8, LANES), (ny + 1, 8, LANES)

    def relay(blocks):
        return call(
            functools.partial(relay_kernel, ny, atom_dev),
            [field_shape, tile_shape, edge_shape, edge_shape],
            idx,
            *blocks,
            dense,
            scratch=[pltpu.VMEM((GROUP * 3 * atom_dev, 8, LANES), F32)],
            smem=(0,),
        )

    def step(kind, outs, *args):
        return call(
            functools.partial(step_kernel, kind, ny, devices, atoms),
            outs,
            idx,
            cheb_coef,
            energy,
            dense,
            *args,
            smem=(0, 1, 2),
        )

    chain = [field_shape, tile_shape, edge_shape, edge_shape]
    cot, tile_cot, up, down = relay(cot_blocks)
    cot_halo = halo(up, down)
    zero, tile_zero, up, down = relay(orb_blocks)
    zero_halo = halo(up, down)
    b2, tile_b2, up, down, full_cot = step("b2", chain + [tile_shape], cot, tile_cot, *cot_halo)
    b2_halo = halo(up, down)
    t1, tile_t1, up, down, full_zero = step("t1", chain + [tile_shape], zero, tile_zero, *zero_halo)
    t1_halo = halo(up, down)
    b1, tile_b1, up, down = step("b1", chain, b2, tile_b2, *b2_halo, cot)
    b1_halo = halo(up, down)
    gp, e, e_up, e_down = step(
        "t2",
        [(plane, LANES)] + [tile_shape] * 3,
        t1,
        tile_t1,
        *t1_halo,
        zero,
        full_zero,
        b1,
        tile_b1,
        b2,
        tile_b2,
        cot,
        full_cot,
    )
    sums = gather(
        call(
            functools.partial(sums_kernel, ny),
            [(ny + 8, LANES)] * GROUP,
            idx,
            gp,
            e,
            *halo(e_up, e_down),
            smem=(0,),
        )
    )
    (image,) = step("out", [(GROUP * block, LANES)], b1, tile_b1, *b1_halo, b2, cot)
    member = lax.rem(idx[0], GROUP)
    blocks = [image] + [
        near(lax.dynamic_slice_in_dim(image, (member ^ j) * block, block, 0), j)
        for j in range(1, GROUP)
    ]
    out, gp, e = call(
        functools.partial(final_kernel, ny, atom_dev),
        [(orb * ny, LANES), (ny, LANES), tile_shape],
        idx,
        *blocks,
        *sums,
        scratch=[pltpu.SemaphoreType.DMA((GROUP,))],
        smem=(0,),
        any_outs=(0,),
    )
    return out.reshape(orbitals.shape), gp.reshape(potential.shape), e[0, :atom_dev]


def solution(mesh):
    placed = (
        P("sample", "grid", None, None),
        P("sample", "grid", None, None),
        P("grid", None, None),
        P(),
        P(),
        P("grid"),
        P("grid"),
        P("grid"),
    )
    return jax.shard_map(
        per_device,
        mesh=mesh,
        in_specs=placed,
        out_specs=(
            P("sample", "grid", None, None),
            P(("sample", "grid"), None, None),
            P(("sample", "grid")),
        ),
        check_vma=False,
    )
```

time: 406 us -> 82.3 us (0.20); the launches traced: 398 us -> 81.9 us
  blocking collectives: 179 us -> 0 us
  local copies, waits for them, and re-layouts: 88.9 us -> 2.88 us
  other arithmetic: 81.4 us -> 0 us
  matrix products: 29.5 us -> 0 us
  Pallas kernels: 0 us -> 20.8 us
  waiting for transfers between devices: 0.03 us -> 20.6 us
  starting transfers between devices: 17.4 us -> 36.8 us
    psum x3 -> x0, blocking collectives: 179 us -> none  [combine_sums(): total = lax.psum(placed, 'grid')]
    scatter-add x5 -> x0, other arithmetic: 64.8 us -> none  [apply_operator(): nonlocal_part = jnp.zeros((rows_count, cell_count), jnp.float32).at[:, pr...]
    gather x6 -> x0, local copies, waits for them, and re-layouts: 51.5 us -> none  [the longest x5 42.3 us: apply_operator(): picks = flat[:, proj_cell]]
    dot_general x10 -> x0, matrix products: 29.5 us -> none  [the longest x5 18.1 us: apply_operator(): jnp.dot(picks, weights, precision=lax.Precision.HIGHEST, preferred_elemen...]
    pallas_call x0 -> x13, Pallas kernels: none -> 20.8 us  [call(): pl.pallas_call(body, out_shape=out_shape, in_specs=in_specs, out_specs=ou...]
    ppermute x10 -> x27, waiting for transfers between devices: 0.03 us -> 20.6 us  [the longest x15 13.8 us: near(): return lax.ppermute(x, 'grid', [(a, a ^ j) for a in range(devices)])]
    ppermute x10 -> x27, starting transfers between devices: 17.4 us -> 36.8 us  [the longest x6 17 us: halo(): lax.ppermute(down, 'grid', to_below)]
    slice x21 -> x0, local copies, waits for them, and re-layouts: 13.6 us -> none  [the longest x10 7.66 us: apply_operator(): beside = beside + jnp.roll(field, 1, axis=3) + jnp.roll(field, -1, axis=3)]
  transfers between devices with their start and end apart: 10 -> 27, of which waited for: 0 -> 9; matrix products, arithmetic and copies ran while one was open for 41% -> 0% of each run, Pallas kernels for 0% -> 20%
where the time goes in v1:
time: 82.3 us; the launch traced here: 81.9 us
  starting transfers between devices  36.8 us (45%)
  Pallas kernels  20.8 us (25%)
  waiting for transfers between devices  20.6 us (25%)
  local copies, waits for them, and re-layouts  2.88 us (3%)
    pallas_call x13, Pallas kernels, call(): pl.pallas_call(body, out_shape=out_shape, in_specs=in_specs, out_specs=ou...  20.8 us
    ppermute x6, starting transfers between devices, halo(): lax.ppermute(down, 'grid', to_below)  17 us
    ppermute x15, starting transfers between devices, near(): return lax.ppermute(x, 'grid', [(a, a ^ j) for a in range(devices)])  16.9 us
    ppermute x15, waiting for transfers between devices, near(): return lax.ppermute(x, 'grid', [(a, a ^ j) for a in range(devices)])  13.8 us
    ppermute x6, waiting for transfers between devices, halo(): lax.ppermute(up, 'grid', to_above)  4.64 us
    ppermute x6, starting transfers between devices, halo(): lax.ppermute(up, 'grid', to_above)  2.96 us
    unnamed x17, local copies, waits for them, and re-layouts  2.33 us
    ppermute x6, waiting for transfers between devices, halo(): lax.ppermute(down, 'grid', to_below)  2.14 us
  transfers between devices with their start and end apart: 27, of which 9 were waited for; matrix products, arithmetic and copies ran while one was open for 0% of the time, Pallas kernels for 20%

profile of v1, /device:TPU:1, one launch (start us, length us, event | category | flops | bytes accessed | tf_op | source)
XLA Modules:
  0.0 81.9 jit_solution(5084899749154466189)
XLA Ops:
  0.6 1.0 %copy-done = f32[32,1,32,128]{3,2,1,0:T(8,128)S(1)} copy-done((f32[32,1,32,128]{3,2,1,0:T(8,128)S(1)}, f32[32,1,32,128]{3,2,1,0:T(8,128)}, u32[]{:S(2)}) %copy-start) | copy-done | bytes 524312
  2.5 2.7 %collective-permute-start.4 = (f32[256,128]{1,0:T(8,128)S(1)}, f32[256,128]{1,0:T(8,128)S(1)}, u32[]{:S(2)}, u32[]{:S(2)}) collective-permute-start(f32[256,128]{1,0:T(8,128)S(1)} %get-tuple-element.46), channel_id=1, source_target_pairs={{0,2},{1,3},{2,0},{3,1},{4,6},{5,7},{6,4},{7,5},{8,10},{9,11},{10,... | collective-permute-start | bytes 393224 | tf_op jit(solution)/shard_map/ppermute | solution.py:324
  5.7 1.4 %collective-permute-start.1 = (f32[80,128]{1,0:T(8,128)S(1)}, f32[80,128]{1,0:T(8,128)S(1)}, u32[]{:S(2)}, u32[]{:S(2)}) collective-permute-start(f32[80,128]{1,0:T(8,128)S(1)} %shard_map.103.refs_0_), channel_id=1, source_target_pairs={{0,2},{1,3},{2,0},{3,1},{4,6},{5,7},{6,4},{7,5},{8,10},{9,11},{10,... | collective-permute-start | bytes 122888 | tf_op jit(solution)/shard_map/ppermute | solution.py:324
  7.2 1.1 %collective-permute-start.2 = (f32[80,128]{1,0:T(8,128)S(1)}, f32[80,128]{1,0:T(8,128)S(1)}, u32[]{:S(2)}, u32[]{:S(2)}) collective-permute-start(f32[80,128]{1,0:T(8,128)S(1)} %shard_map.103.refs_0_), channel_id=1, source_target_pairs={{0,3},{1,2},{2,1},{3,0},{4,7},{5,6},{6,5},{7,4},{8,11},{9,10},{10,... | collective-permute-start | bytes 122888 | tf_op jit(solution)/shard_map/ppermute | solution.py:324
  8.3 4.4 %collective-permute-done.1.refs_2_ = f32[80,128]{1,0:T(8,128)S(1)} collective-permute-done((f32[80,128]{1,0:T(8,128)S(1)}, f32[80,128]{1,0:T(8,128)S(1)}, u32[]{:S(2)}, u32[]{:S(2)}) %collective-permute-start.1) | collective-permute-done | bytes 40992 | tf_op jit(solution)/shard_map/ppermute | solution.py:324
  13.5 4.0 %shard_map.104.refs_4_.refs_3_ = f32[128,8,128]{2,1,0:T(8,128)S(1)} custom-call(s32[1]{0:T(128)} %bitcast.idx.refs_0_, f32[80,128]{1,0:T(8,128)S(1)} %shard_map.103.refs_0_, f32[80,128]{1,0:T(8,128)S(1)} %collective-permute-done.refs_1_, f32[80,128]{1,0:T(8,128)S(1)} %collective-permute-done.1.refs_2_, f32[80,128]{1,0:T(8,128)S(1)} %collective-permute-done.2.refs_3_), custom_call_target="tpu_custom_call" | custom-call | tf_op jit(solution)/shard_map/pallas_call | solution.py:37
  18.3 1.5 %collective-permute-start.6 = (f32[33,8,128]{2,1,0:T(8,128)S(1)}, f32[33,8,128]{2,1,0:T(8,128)S(1)}, u32[]{:S(2)}, u32[]{:S(2)}) collective-permute-start(f32[33,8,128]{2,1,0:T(8,128)S(1)} %get-tuple-element.50), channel_id=1, source_target_pairs={{0,4},{1,5},{2,6},{3,7},{4,8},{5,9},{6,10},{7,11},{8,12},{9,13},{1... | collective-permute-start | bytes 405512 | tf_op jit(solution)/shard_map/ppermute | solution.py:332
  19.8 2.1 %collective-permute-start.7 = (f32[33,8,128]{2,1,0:T(8,128)S(1)}, f32[33,8,128]{2,1,0:T(8,128)S(1)}, u32[]{:S(2)}, u32[]{:S(2)}) collective-permute-start(f32[33,8,128]{2,1,0:T(8,128)S(1)} %get-tuple-element.51), channel_id=1, source_target_pairs={{4,0},{5,1},{6,2},{7,3},{8,4},{9,5},{10,6},{11,7},{12,8},{13,9},{1... | collective-permute-start | bytes 405512 | tf_op jit(solution)/shard_map/ppermute | solution.py:332
  21.9 3.6 %collective-permute-done.6.refs_6_ = f32[33,8,128]{2,1,0:T(8,128)S(1)} collective-permute-done((f32[33,8,128]{2,1,0:T(8,128)S(1)}, f32[33,8,128]{2,1,0:T(8,128)S(1)}, u32[]{:S(2)}, u32[]{:S(2)}) %collective-permute-start.6) | collective-permute-done | bytes 135200 | tf_op jit(solution)/shard_map/ppermute | solution.py:332
  25.5 2.1 %collective-permute-done.7.refs_7_ = f32[33,8,128]{2,1,0:T(8,128)S(1)} collective-permute-done((f32[33,8,128]{2,1,0:T(8,128)S(1)}, f32[33,8,128]{2,1,0:T(8,128)S(1)}, u32[]{:S(2)}, u32[]{:S(2)}) %collective-permute-start.7) | collective-permute-done | bytes 135200 | tf_op jit(solution)/shard_map/ppermute | solution.py:332
  28.3 2.3 %shard_map.107 = (f32[128,8,128]{2,1,0:T(8,128)S(1)}, f32[8,128]{1,0:T(8,128)S(1)}, f32[33,8,128]{2,1,0:T(8,128)S(1)}, f32[33,8,128]{2,1,0:T(8,128)S(1)}, f32[8,128]{1,0:T(8,128)S(1)}) custom-call(s32[1]{0:T(128)} %bitcast.idx.refs_0_, f32[4]{0:T(128)S(1)} %copy-done.3, f32[32]{0:T(128)S(1)} %copy-done.4, f32[128,8,128]{2,1,0:T(8,128)S(1)} %shard_map.104.refs_4_.refs_3_, ...), custom_call_target="tpu_custom_call" | custom-call | tf_op jit(solution)/shard_map/pallas_call | solution.py:37
  30.7 1.4 %collective-permute-start.8 = (f32[33,8,128]{2,1,0:T(8,128)S(1)}, f32[33,8,128]{2,1,0:T(8,128)S(1)}, u32[]{:S(2)}, u32[]{:S(2)}) collective-permute-start(f32[33,8,128]{2,1,0:T(8,128)S(1)} %get-tuple-element.54), channel_id=1, source_target_pairs={{0,4},{1,5},{2,6},{3,7},{4,8},{5,9},{6,10},{7,11},{8,12},{9,13},{1... | collective-permute-start | bytes 405512 | tf_op jit(solution)/shard_map/ppermute | solution.py:332
  32.1 1.9 %collective-permute-start.9 = (f32[33,8,128]{2,1,0:T(8,128)S(1)}, f32[33,8,128]{2,1,0:T(8,128)S(1)}, u32[]{:S(2)}, u32[]{:S(2)}) collective-permute-start(f32[33,8,128]{2,1,0:T(8,128)S(1)} %get-tuple-element.55), channel_id=1, source_target_pairs={{4,0},{5,1},{6,2},{7,3},{8,4},{9,5},{10,6},{11,7},{12,8},{13,9},{1... | collective-permute-start | bytes 405512 | tf_op jit(solution)/shard_map/ppermute | solution.py:332
  34.6 1.7 %collective-permute-start.15 = (f32[256,128]{1,0:T(8,128)S(1)}, f32[256,128]{1,0:T(8,128)S(1)}, u32[]{:S(2)}, u32[]{:S(2)}) collective-permute-start(f32[256,128]{1,0:T(8,128)S(1)} %get-tuple-element.61), channel_id=1, source_target_pairs={{0,1},{1,0},{2,3},{3,2},{4,5},{5,4},{6,7},{7,6},{8,9},{9,8},{10,11... | collective-permute-start | bytes 393224 | tf_op jit(solution)/shard_map/ppermute | solution.py:324
  36.3 1.2 %collective-permute-start.16 = (f32[256,128]{1,0:T(8,128)S(1)}, f32[256,128]{1,0:T(8,128)S(1)}, u32[]{:S(2)}, u32[]{:S(2)}) collective-permute-start(f32[256,128]{1,0:T(8,128)S(1)} %get-tuple-element.62), channel_id=1, source_target_pairs={{0,2},{1,3},{2,0},{3,1},{4,6},{5,7},{6,4},{7,5},{8,10},{9,11},{10,... | collective-permute-start | bytes 393224 | tf_op jit(solution)/shard_map/ppermute | solution.py:324
  38.0 3.4 %collective-permute-done.16.refs_2_ = f32[256,128]{1,0:T(8,128)S(1)} collective-permute-done((f32[256,128]{1,0:T(8,128)S(1)}, f32[256,128]{1,0:T(8,128)S(1)}, u32[]{:S(2)}, u32[]{:S(2)}) %collective-permute-start.16) | collective-permute-done | bytes 131104 | tf_op jit(solution)/shard_map/ppermute | solution.py:324
  41.4 3.0 %collective-permute-done.17.refs_3_ = f32[256,128]{1,0:T(8,128)S(1)} collective-permute-done((f32[256,128]{1,0:T(8,128)S(1)}, f32[256,128]{1,0:T(8,128)S(1)}, u32[]{:S(2)}, u32[]{:S(2)}) %collective-permute-start.17) | collective-permute-done | bytes 131104 | tf_op jit(solution)/shard_map/ppermute | solution.py:324
  44.4 1.3 %shard_map.111 = (f32[128,8,128]{2,1,0:T(8,128)S(1)}, f32[8,128]{1,0:T(8,128)S(1)}, f32[33,8,128]{2,1,0:T(8,128)}, f32[33,8,128]{2,1,0:T(8,128)S(1)}) custom-call(s32[1]{0:T(128)} %bitcast.idx.refs_0_, f32[256,128]{1,0:T(8,128)S(1)} %get-tuple-element.60.refs_0_, f32[256,128]{1,0:T(8,128)S(1)} %collective-permute-done.15.refs_1_, ...), custom_call_target="tpu_custom_call" | custom-call | tf_op jit(solution)/shard_map/pallas_call | solution.py:37
  45.7 3.3 %collective-permute-start.19 = (f32[33,8,128]{2,1,0:T(8,128)S(1)}, f32[33,8,128]{2,1,0:T(8,128)S(1)}, u32[]{:S(2)}, u32[]{:S(2)}) collective-permute-start(f32[33,8,128]{2,1,0:T(8,128)S(1)} %get-tuple-element.67), channel_id=1, source_target_pairs={{4,0},{5,1},{6,2},{7,3},{8,4},{9,5},{10,6},{11,7},{12,8},{13,9},{1... | collective-permute-start | bytes 405512 | tf_op jit(solution)/shard_map/ppermute | solution.py:332
  49.0 3.0 %shard_map.108 = (f32[128,8,128]{2,1,0:T(8,128)S(1)}, f32[8,128]{1,0:T(8,128)S(1)}, f32[33,8,128]{2,1,0:T(8,128)}, f32[33,8,128]{2,1,0:T(8,128)S(1)}) custom-call(s32[1]{0:T(128)} %bitcast.idx.refs_0_, f32[4]{0:T(128)S(1)} %copy-done.3, f32[32]{0:T(128)S(1)} %copy-done.4, f32[128,8,128]{2,1,0:T(8,128)S(1)} %shard_map.104.refs_4_.refs_3_, ...), custom_call_target="tpu_custom_call" | custom-call | tf_op jit(solution)/shard_map/pallas_call | solution.py:37
  52.0 3.3 %collective-permute-start.11 = (f32[33,8,128]{2,1,0:T(8,128)S(1)}, f32[33,8,128]{2,1,0:T(8,128)S(1)}, u32[]{:S(2)}, u32[]{:S(2)}) collective-permute-start(f32[33,8,128]{2,1,0:T(8,128)S(1)} %get-tuple-element.59), channel_id=1, source_target_pairs={{4,0},{5,1},{6,2},{7,3},{8,4},{9,5},{10,6},{11,7},{12,8},{13,9},{1... | collective-permute-start | bytes 405512 | tf_op jit(solution)/shard_map/ppermute | solution.py:332
  55.3 2.3 %shard_map.112 = (f32[128,8,128]{2,1,0:T(8,128)S(1)}, f32[8,128]{1,0:T(8,128)S(1)}, f32[33,8,128]{2,1,0:T(8,128)S(1)}, f32[33,8,128]{2,1,0:T(8,128)S(1)}, f32[8,128]{1,0:T(8,128)S(1)}) custom-call(s32[1]{0:T(128)} %bitcast.idx.refs_0_, f32[4]{0:T(128)S(1)} %copy-done.3, f32[32]{0:T(128)S(1)} %copy-done.4, f32[128,8,128]{2,1,0:T(8,128)S(1)} %shard_map.104.refs_4_.refs_3_, ...), custom_call_target="tpu_custom_call" | custom-call | tf_op jit(solution)/shard_map/pallas_call | solution.py:37
  57.6 3.3 %collective-permute-start.21 = (f32[33,8,128]{2,1,0:T(8,128)S(1)}, f32[33,8,128]{2,1,0:T(8,128)S(1)}, u32[]{:S(2)}, u32[]{:S(2)}) collective-permute-start(f32[33,8,128]{2,1,0:T(8,128)S(1)} %get-tuple-element.71), channel_id=1, source_target_pairs={{4,0},{5,1},{6,2},{7,3},{8,4},{9,5},{10,6},{11,7},{12,8},{13,9},{1... | collective-permute-start | bytes 405512 | tf_op jit(solution)/shard_map/ppermute | solution.py:332
  60.9 2.2 %shard_map.109.refs_0_ = f32[1024,128]{1,0:T(8,128)S(1)} custom-call(s32[1]{0:T(128)} %bitcast.idx.refs_0_, f32[4]{0:T(128)S(1)} %copy-done.3, f32[32]{0:T(128)S(1)} %copy-done.4, f32[128,8,128]{2,1,0:T(8,128)S(1)} %shard_map.104.refs_4_.refs_3_, f32[128,8,128]{2,1,0:T(8,128)S(1)} %get-tuple-element.56.refs_4_.refs_10_, ...), custom_call_target="tpu_custom_call" | custom-call | tf_op jit(solution)/shard_map/pallas_call | solution.py:37
  63.1 2.0 %collective-permute-start.12 = (f32[256,128]{1,0:T(8,128)S(1)}, f32[256,128]{1,0:T(8,128)S(1)}, u32[]{:S(2)}, u32[]{:S(2)}) collective-permute-start(f32[256,128]{1,0:T(8,128)S(1)} %get-tuple-element.90), channel_id=1, source_target_pairs={{0,1},{1,0},{2,3},{3,2},{4,5},{5,4},{6,7},{7,6},{8,9},{9,8},{10,11... | collective-permute-start | bytes 393224 | tf_op jit(solution)/shard_map/ppermute | solution.py:324
  65.1 1.2 %collective-permute-start.13 = (f32[256,128]{1,0:T(8,128)S(1)}, f32[256,128]{1,0:T(8,128)S(1)}, u32[]{:S(2)}, u32[]{:S(2)}) collective-permute-start(f32[256,128]{1,0:T(8,128)S(1)} %get-tuple-element.89), channel_id=1, source_target_pairs={{0,2},{1,3},{2,0},{3,1},{4,6},{5,7},{6,4},{7,5},{8,10},{9,11},{10,... | collective-permute-start | bytes 393224 | tf_op jit(solution)/shard_map/ppermute | solution.py:324
  66.8 2.7 %shard_map.113 = (f32[128,128]{1,0:T(8,128)S(1)}, f32[8,128]{1,0:T(8,128)S(1)}, f32[8,128]{1,0:T(8,128)S(1)}, f32[8,128]{1,0:T(8,128)S(1)}) custom-call(s32[1]{0:T(128)} %bitcast.idx.refs_0_, f32[4]{0:T(128)S(1)} %copy-done.3, f32[32]{0:T(128)S(1)} %copy-done.4, f32[128,8,128]{2,1,0:T(8,128)S(1)} %shard_map.104.refs_4_.refs_3_, ...), custom_call_target="tpu_custom_call" | custom-call | tf_op jit(solution)/shard_map/pallas_call | solution.py:37
  69.5 3.3 %collective-permute-start.23 = (f32[8,128]{1,0:T(8,128)S(1)}, f32[8,128]{1,0:T(8,128)S(1)}, u32[]{:S(2)}, u32[]{:S(2)}) collective-permute-start(f32[8,128]{1,0:T(8,128)S(1)} %get-tuple-element.77), channel_id=1, source_target_pairs={{4,0},{5,1},{6,2},{7,3},{8,4},{9,5},{10,6},{11,7},{12,8},{13,9},{1... | collective-permute-start | bytes 12296 | tf_op jit(solution)/shard_map/ppermute | solution.py:332
  73.8 1.7 %collective-permute-start.24 = (f32[40,128]{1,0:T(8,128)S(1)}, f32[40,128]{1,0:T(8,128)S(1)}, u32[]{:S(2)}, u32[]{:S(2)}) collective-permute-start(f32[40,128]{1,0:T(8,128)S(1)} %get-tuple-element.79), channel_id=1, source_target_pairs={{0,1},{1,0},{2,3},{3,2},{4,5},{5,4},{6,7},{7,6},{8,9},{9,8},{10,11... | collective-permute-start | bytes 61448 | tf_op jit(solution)/shard_map/ppermute | solution.py:324
  75.4 1.2 %collective-permute-start.25 = (f32[40,128]{1,0:T(8,128)S(1)}, f32[40,128]{1,0:T(8,128)S(1)}, u32[]{:S(2)}, u32[]{:S(2)}) collective-permute-start(f32[40,128]{1,0:T(8,128)S(1)} %get-tuple-element.80), channel_id=1, source_target_pairs={{0,2},{1,3},{2,0},{3,1},{4,6},{5,7},{6,4},{7,5},{8,10},{9,11},{10,... | collective-permute-start | bytes 61448 | tf_op jit(solution)/shard_map/ppermute | solution.py:324
  76.7 1.1 %collective-permute-start.26 = (f32[40,128]{1,0:T(8,128)S(1)}, f32[40,128]{1,0:T(8,128)S(1)}, u32[]{:S(2)}, u32[]{:S(2)}) collective-permute-start(f32[40,128]{1,0:T(8,128)S(1)} %get-tuple-element.81), channel_id=1, source_target_pairs={{0,3},{1,2},{2,1},{3,0},{4,7},{5,6},{6,5},{7,4},{8,11},{9,10},{10,... | collective-permute-start | bytes 61448 | tf_op jit(solution)/shard_map/ppermute | solution.py:324
  78.1 1.8 %collective-permute-done.26.refs_7_ = f32[40,128]{1,0:T(8,128)S(1)} collective-permute-done((f32[40,128]{1,0:T(8,128)S(1)}, f32[40,128]{1,0:T(8,128)S(1)}, u32[]{:S(2)}, u32[]{:S(2)}) %collective-permute-start.26) | collective-permute-done | bytes 20512 | tf_op jit(solution)/shard_map/ppermute | solution.py:324
  (54 shorter events, 8.6 us)
Async XLA Ops:
  1.7 3.6 %copy-start.2 = (f32[1,32,128]{2,1,0:T(8,128)S(1)}, f32[1,32,128]{2,1,0:T(8,128)}, u32[]{:S(2)}) copy-start(f32[1,32,128]{2,1,0:T(8,128)} %param.10) | copy-start | bytes 49156
  1.7 3.6 %copy-start.6 = (s32[2048]{0:T(1024)S(1)}, s32[2048]{0:T(1024)}, u32[]{:S(2)}) copy-start(s32[2048]{0:T(1024)} %param.14) | copy-start | bytes 24580
  1.7 3.6 %copy-start.7 = (f32[2048]{0:T(1024)S(1)}, f32[2048]{0:T(1024)}, u32[]{:S(2)}) copy-start(f32[2048]{0:T(1024)} %param.15) | copy-start | bytes 24580
  2.4 2.9 %copy-start.5 = (s32[2048]{0:T(1024)S(1)}, s32[2048]{0:T(1024)}, u32[]{:S(2)}) copy-start(s32[2048]{0:T(1024)} %param.13) | copy-start | bytes 24580
  2.4 15.2 %collective-permute-start.3 = (f32[256,128]{1,0:T(8,128)S(1)}, f32[256,128]{1,0:T(8,128)S(1)}, u32[]{:S(2)}, u32[]{:S(2)}) collective-permute-start(f32[256,128]{1,0:T(8,128)S(1)} %get-tuple-element.45), channel_id=1, source_target_pairs={{0,1},{1,0},{2,3},{3,2},{4,5},{5,4},{6,7},{7,6},{8,9},{9,8},{10,11... | collective-permute-start | bytes 393224 | tf_op jit(solution)/shard_map/ppermute | solution.py:324
  2.5 15.0 %collective-permute-start.4 = (f32[256,128]{1,0:T(8,128)S(1)}, f32[256,128]{1,0:T(8,128)S(1)}, u32[]{:S(2)}, u32[]{:S(2)}) collective-permute-start(f32[256,128]{1,0:T(8,128)S(1)} %get-tuple-element.46), channel_id=1, source_target_pairs={{0,2},{1,3},{2,0},{3,1},{4,6},{5,7},{6,4},{7,5},{8,10},{9,11},{10,... | collective-permute-start | bytes 393224 | tf_op jit(solution)/shard_map/ppermute | solution.py:324
  5.2 12.4 %collective-permute-start.5 = (f32[256,128]{1,0:T(8,128)S(1)}, f32[256,128]{1,0:T(8,128)S(1)}, u32[]{:S(2)}, u32[]{:S(2)}) collective-permute-start(f32[256,128]{1,0:T(8,128)S(1)} %get-tuple-element.47), channel_id=1, source_target_pairs={{0,3},{1,2},{2,1},{3,0},{4,7},{5,6},{6,5},{7,4},{8,11},{9,10},{10,... | collective-permute-start | bytes 393224 | tf_op jit(solution)/shard_map/ppermute | solution.py:324
  5.3 1.9 %collective-permute-start = (f32[80,128]{1,0:T(8,128)S(1)}, f32[80,128]{1,0:T(8,128)S(1)}, u32[]{:S(2)}, u32[]{:S(2)}) collective-permute-start(f32[80,128]{1,0:T(8,128)S(1)} %shard_map.103.refs_0_), channel_id=1, source_target_pairs={{0,1},{1,0},{2,3},{3,2},{4,5},{5,4},{6,7},{7,6},{8,9},{9,8},{10,11... | collective-permute-start | bytes 122888 | tf_op jit(solution)/shard_map/ppermute | solution.py:324
  5.7 7.0 %collective-permute-start.1 = (f32[80,128]{1,0:T(8,128)S(1)}, f32[80,128]{1,0:T(8,128)S(1)}, u32[]{:S(2)}, u32[]{:S(2)}) collective-permute-start(f32[80,128]{1,0:T(8,128)S(1)} %shard_map.103.refs_0_), channel_id=1, source_target_pairs={{0,2},{1,3},{2,0},{3,1},{4,6},{5,7},{6,4},{7,5},{8,10},{9,11},{10,... | collective-permute-start | bytes 122888 | tf_op jit(solution)/shard_map/ppermute | solution.py:324
  7.2 6.4 %collective-permute-start.2 = (f32[80,128]{1,0:T(8,128)S(1)}, f32[80,128]{1,0:T(8,128)S(1)}, u32[]{:S(2)}, u32[]{:S(2)}) collective-permute-start(f32[80,128]{1,0:T(8,128)S(1)} %shard_map.103.refs_0_), channel_id=1, source_target_pairs={{0,3},{1,2},{2,1},{3,0},{4,7},{5,6},{6,5},{7,4},{8,11},{9,10},{10,... | collective-permute-start | bytes 122888 | tf_op jit(solution)/shard_map/ppermute | solution.py:324
  18.3 7.2 %collective-permute-start.6 = (f32[33,8,128]{2,1,0:T(8,128)S(1)}, f32[33,8,128]{2,1,0:T(8,128)S(1)}, u32[]{:S(2)}, u32[]{:S(2)}) collective-permute-start(f32[33,8,128]{2,1,0:T(8,128)S(1)} %get-tuple-element.50), channel_id=1, source_target_pairs={{0,4},{1,5},{2,6},{3,7},{4,8},{5,9},{6,10},{7,11},{8,12},{9,13},{1... | collective-permute-start | bytes 405512 | tf_op jit(solution)/shard_map/ppermute | solution.py:332
  19.8 7.8 %collective-permute-start.7 = (f32[33,8,128]{2,1,0:T(8,128)S(1)}, f32[33,8,128]{2,1,0:T(8,128)S(1)}, u32[]{:S(2)}, u32[]{:S(2)}) collective-permute-start(f32[33,8,128]{2,1,0:T(8,128)S(1)} %get-tuple-element.51), channel_id=1, source_target_pairs={{4,0},{5,1},{6,2},{7,3},{8,4},{9,5},{10,6},{11,7},{12,8},{13,9},{1... | collective-permute-start | bytes 405512 | tf_op jit(solution)/shard_map/ppermute | solution.py:332
  28.3 5.6 %copy-start.1 = (f32[32,1,32,128]{3,2,1,0:T(8,128)S(1)}, f32[32,1,32,128]{3,2,1,0:T(8,128)}, u32[]{:S(2)}) copy-start(f32[32,1,32,128]{3,2,1,0:T(8,128)} %param.8) | copy-start | bytes 1572868
  30.7 18.3 %collective-permute-start.8 = (f32[33,8,128]{2,1,0:T(8,128)S(1)}, f32[33,8,128]{2,1,0:T(8,128)S(1)}, u32[]{:S(2)}, u32[]{:S(2)}) collective-permute-start(f32[33,8,128]{2,1,0:T(8,128)S(1)} %get-tuple-element.54), channel_id=1, source_target_pairs={{0,4},{1,5},{2,6},{3,7},{4,8},{5,9},{6,10},{7,11},{8,12},{9,13},{1... | collective-permute-start | bytes 405512 | tf_op jit(solution)/shard_map/ppermute | solution.py:332
  32.1 16.9 %collective-permute-start.9 = (f32[33,8,128]{2,1,0:T(8,128)S(1)}, f32[33,8,128]{2,1,0:T(8,128)S(1)}, u32[]{:S(2)}, u32[]{:S(2)}) collective-permute-start(f32[33,8,128]{2,1,0:T(8,128)S(1)} %get-tuple-element.55), channel_id=1, source_target_pairs={{4,0},{5,1},{6,2},{7,3},{8,4},{9,5},{10,6},{11,7},{12,8},{13,9},{1... | collective-permute-start | bytes 405512 | tf_op jit(solution)/shard_map/ppermute | solution.py:332
  34.6 3.4 %collective-permute-start.15 = (f32[256,128]{1,0:T(8,128)S(1)}, f32[256,128]{1,0:T(8,128)S(1)}, u32[]{:S(2)}, u32[]{:S(2)}) collective-permute-start(f32[256,128]{1,0:T(8,128)S(1)} %get-tuple-element.61), channel_id=1, source_target_pairs={{0,1},{1,0},{2,3},{3,2},{4,5},{5,4},{6,7},{7,6},{8,9},{9,8},{10,11... | collective-permute-start | bytes 393224 | tf_op jit(solution)/shard_map/ppermute | solution.py:324
  36.3 5.1 %collective-permute-start.16 = (f32[256,128]{1,0:T(8,128)S(1)}, f32[256,128]{1,0:T(8,128)S(1)}, u32[]{:S(2)}, u32[]{:S(2)}) collective-permute-start(f32[256,128]{1,0:T(8,128)S(1)} %get-tuple-element.62), channel_id=1, source_target_pairs={{0,2},{1,3},{2,0},{3,1},{4,6},{5,7},{6,4},{7,5},{8,10},{9,11},{10,... | collective-permute-start | bytes 393224 | tf_op jit(solution)/shard_map/ppermute | solution.py:324
  37.6 6.8 %collective-permute-start.17 = (f32[256,128]{1,0:T(8,128)S(1)}, f32[256,128]{1,0:T(8,128)S(1)}, u32[]{:S(2)}, u32[]{:S(2)}) collective-permute-start(f32[256,128]{1,0:T(8,128)S(1)} %get-tuple-element.63), channel_id=1, source_target_pairs={{0,3},{1,2},{2,1},{3,0},{4,7},{5,6},{6,5},{7,4},{8,11},{9,10},{10,... | collective-permute-start | bytes 393224 | tf_op jit(solution)/shard_map/ppermute | solution.py:324
  45.7 9.6 %collective-permute-start.18 = (f32[33,8,128]{2,1,0:T(8,128)}, f32[33,8,128]{2,1,0:T(8,128)S(1)}, u32[]{:S(2)}, u32[]{:S(2)}) collective-permute-start(f32[33,8,128]{2,1,0:T(8,128)} %get-tuple-element.66), channel_id=1, source_target_pairs={{0,4},{1,5},{2,6},{3,7},{4,8},{5,9},{6,10},{7,11},{8,12},{9,13},{1... | collective-permute-start | bytes 405512 | tf_op jit(solution)/shard_map/ppermute | solution.py:332
  45.7 9.6 %collective-permute-start.19 = (f32[33,8,128]{2,1,0:T(8,128)S(1)}, f32[33,8,128]{2,1,0:T(8,128)S(1)}, u32[]{:S(2)}, u32[]{:S(2)}) collective-permute-start(f32[33,8,128]{2,1,0:T(8,128)S(1)} %get-tuple-element.67), channel_id=1, source_target_pairs={{4,0},{5,1},{6,2},{7,3},{8,4},{9,5},{10,6},{11,7},{12,8},{13,9},{1... | collective-permute-start | bytes 405512 | tf_op jit(solution)/shard_map/ppermute | solution.py:332
  52.0 8.9 %collective-permute-start.10 = (f32[33,8,128]{2,1,0:T(8,128)}, f32[33,8,128]{2,1,0:T(8,128)S(1)}, u32[]{:S(2)}, u32[]{:S(2)}) collective-permute-start(f32[33,8,128]{2,1,0:T(8,128)} %get-tuple-element.58), channel_id=1, source_target_pairs={{0,4},{1,5},{2,6},{3,7},{4,8},{5,9},{6,10},{7,11},{8,12},{9,13},{1... | collective-permute-start | bytes 405512 | tf_op jit(solution)/shard_map/ppermute | solution.py:332
  52.0 8.9 %collective-permute-start.11 = (f32[33,8,128]{2,1,0:T(8,128)S(1)}, f32[33,8,128]{2,1,0:T(8,128)S(1)}, u32[]{:S(2)}, u32[]{:S(2)}) collective-permute-start(f32[33,8,128]{2,1,0:T(8,128)S(1)} %get-tuple-element.59), channel_id=1, source_target_pairs={{4,0},{5,1},{6,2},{7,3},{8,4},{9,5},{10,6},{11,7},{12,8},{13,9},{1... | collective-permute-start | bytes 405512 | tf_op jit(solution)/shard_map/ppermute | solution.py:332
  57.6 9.2 %collective-permute-start.20 = (f32[33,8,128]{2,1,0:T(8,128)S(1)}, f32[33,8,128]{2,1,0:T(8,128)S(1)}, u32[]{:S(2)}, u32[]{:S(2)}) collective-permute-start(f32[33,8,128]{2,1,0:T(8,128)S(1)} %get-tuple-element.70), channel_id=1, source_target_pairs={{0,4},{1,5},{2,6},{3,7},{4,8},{5,9},{6,10},{7,11},{8,12},{9,13},{1... | collective-permute-start | bytes 405512 | tf_op jit(solution)/shard_map/ppermute | solution.py:332
  57.6 9.2 %collective-permute-start.21 = (f32[33,8,128]{2,1,0:T(8,128)S(1)}, f32[33,8,128]{2,1,0:T(8,128)S(1)}, u32[]{:S(2)}, u32[]{:S(2)}) collective-permute-start(f32[33,8,128]{2,1,0:T(8,128)S(1)} %get-tuple-element.71), channel_id=1, source_target_pairs={{4,0},{5,1},{6,2},{7,3},{8,4},{9,5},{10,6},{11,7},{12,8},{13,9},{1... | collective-permute-start | bytes 405512 | tf_op jit(solution)/shard_map/ppermute | solution.py:332
  63.1 16.8 %collective-permute-start.12 = (f32[256,128]{1,0:T(8,128)S(1)}, f32[256,128]{1,0:T(8,128)S(1)}, u32[]{:S(2)}, u32[]{:S(2)}) collective-permute-start(f32[256,128]{1,0:T(8,128)S(1)} %get-tuple-element.90), channel_id=1, source_target_pairs={{0,1},{1,0},{2,3},{3,2},{4,5},{5,4},{6,7},{7,6},{8,9},{9,8},{10,11... | collective-permute-start | bytes 393224 | tf_op jit(solution)/shard_map/ppermute | solution.py:324
  65.1 14.8 %collective-permute-start.13 = (f32[256,128]{1,0:T(8,128)S(1)}, f32[256,128]{1,0:T(8,128)S(1)}, u32[]{:S(2)}, u32[]{:S(2)}) collective-permute-start(f32[256,128]{1,0:T(8,128)S(1)} %get-tuple-element.89), channel_id=1, source_target_pairs={{0,2},{1,3},{2,0},{3,1},{4,6},{5,7},{6,4},{7,5},{8,10},{9,11},{10,... | collective-permute-start | bytes 393224 | tf_op jit(solution)/shard_map/ppermute | solution.py:324
  66.3 13.6 %collective-permute-start.14 = (f32[256,128]{1,0:T(8,128)S(1)}, f32[256,128]{1,0:T(8,128)S(1)}, u32[]{:S(2)}, u32[]{:S(2)}) collective-permute-start(f32[256,128]{1,0:T(8,128)S(1)} %get-tuple-element.88), channel_id=1, source_target_pairs={{0,3},{1,2},{2,1},{3,0},{4,7},{5,6},{6,5},{7,4},{8,11},{9,10},{10,... | collective-permute-start | bytes 393224 | tf_op jit(solution)/shard_map/ppermute | solution.py:324
  69.5 4.3 %collective-permute-start.22 = (f32[8,128]{1,0:T(8,128)S(1)}, f32[8,128]{1,0:T(8,128)S(1)}, u32[]{:S(2)}, u32[]{:S(2)}) collective-permute-start(f32[8,128]{1,0:T(8,128)S(1)} %get-tuple-element.76), channel_id=1, source_target_pairs={{0,4},{1,5},{2,6},{3,7},{4,8},{5,9},{6,10},{7,11},{8,12},{9,13},{1... | collective-permute-start | bytes 12296 | tf_op jit(solution)/shard_map/ppermute | solution.py:332
  69.5 4.3 %collective-permute-start.23 = (f32[8,128]{1,0:T(8,128)S(1)}, f32[8,128]{1,0:T(8,128)S(1)}, u32[]{:S(2)}, u32[]{:S(2)}) collective-permute-start(f32[8,128]{1,0:T(8,128)S(1)} %get-tuple-element.77), channel_id=1, source_target_pairs={{4,0},{5,1},{6,2},{7,3},{8,4},{9,5},{10,6},{11,7},{12,8},{13,9},{1... | collective-permute-start | bytes 12296 | tf_op jit(solution)/shard_map/ppermute | solution.py:332
  73.8 2.9 %collective-permute-start.24 = (f32[40,128]{1,0:T(8,128)S(1)}, f32[40,128]{1,0:T(8,128)S(1)}, u32[]{:S(2)}, u32[]{:S(2)}) collective-permute-start(f32[40,128]{1,0:T(8,128)S(1)} %get-tuple-element.79), channel_id=1, source_target_pairs={{0,1},{1,0},{2,3},{3,2},{4,5},{5,4},{6,7},{7,6},{8,9},{9,8},{10,11... | collective-permute-start | bytes 61448 | tf_op jit(solution)/shard_map/ppermute | solution.py:324
  75.4 2.6 %collective-permute-start.25 = (f32[40,128]{1,0:T(8,128)S(1)}, f32[40,128]{1,0:T(8,128)S(1)}, u32[]{:S(2)}, u32[]{:S(2)}) collective-permute-start(f32[40,128]{1,0:T(8,128)S(1)} %get-tuple-element.80), channel_id=1, source_target_pairs={{0,2},{1,3},{2,0},{3,1},{4,6},{5,7},{6,4},{7,5},{8,10},{9,11},{10,... | collective-permute-start | bytes 61448 | tf_op jit(solution)/shard_map/ppermute | solution.py:324
  76.7 3.2 %collective-permute-start.26 = (f32[40,128]{1,0:T(8,128)S(1)}, f32[40,128]{1,0:T(8,128)S(1)}, u32[]{:S(2)}, u32[]{:S(2)}) collective-permute-start(f32[40,128]{1,0:T(8,128)S(1)} %get-tuple-element.81), channel_id=1, source_target_pairs={{0,3},{1,2},{2,1},{3,0},{4,7},{5,6},{6,5},{7,4},{8,11},{9,10},{10,... | collective-permute-start | bytes 61448 | tf_op jit(solution)/shard_map/ppermute | solution.py:324
  (3 other events, 2.4 us)

commit v2 on v1

v2 whole, which is shorter than its diff:
```python
import functools

import jax
import jax.numpy as jnp
from jax import lax
from jax.experimental import pallas as pl
from jax.experimental.pallas import tpu as pltpu
from jax.sharding import PartitionSpec as P

spectral_center = 4.5
spectral_half = 4.5

GROUP = 4
LANES = 128
F32 = jnp.float32


def call(body, outs, *args, micros, scratch=(), smem=(), hbm_args=(), hbm_outs=(), smem_outs=()):
    in_specs, operands = [], []
    for n, a in enumerate(args):
        if n in smem:
            in_specs.append(pl.BlockSpec(memory_space=pltpu.SMEM))
        elif n in hbm_args:
            in_specs.append(pl.BlockSpec(memory_space=pltpu.HBM))
            a = pltpu.with_memory_space_constraint(a, pltpu.HBM)
        else:
            in_specs.append(pl.BlockSpec(memory_space=pltpu.VMEM))
            a = pltpu.with_memory_space_constraint(a, pltpu.VMEM)
        operands.append(a)
    out_shape, out_specs = [], []
    for n, shape in enumerate(outs):
        if n in hbm_outs:
            out_shape.append(jax.ShapeDtypeStruct(shape, F32))
            out_specs.append(pl.BlockSpec(memory_space=pltpu.HBM))
        elif n in smem_outs:
            out_shape.append(jax.ShapeDtypeStruct(shape, F32))
            out_specs.append(pl.BlockSpec(memory_space=pltpu.SMEM))
        else:
            out_shape.append(pltpu.VMEM(shape, F32))
            out_specs.append(pl.BlockSpec(memory_space=pltpu.VMEM))
    return pl.pallas_call(
        body,
        out_shape=out_shape,
        in_specs=in_specs,
        out_specs=out_specs,
        scratch_shapes=list(scratch),
        compiler_params=pltpu.CompilerParams(vmem_limit_bytes=16 << 20),
        cost_estimate=pl.CostEstimate(
            flops=int(micros * 1e6), bytes_accessed=int(micros * 3.69e6), transcendentals=0
        ),
    )(*operands)


def lane_iota(shape):
    return lax.broadcasted_iota(jnp.int32, shape, len(shape) - 1)


def prep_kernel(devices, atoms, idx, cheb, energy, cell, atom, value, pot, cot, orb, *refs):
    consts, blocks, (box, sems, box_sems) = refs[0], refs[1:-3], refs[-3:]
    rows = blocks[GROUP].shape[0]
    count, ny = cell.shape[0], pot.shape[0]
    atom_dev = atoms // devices
    k = lax.rem(idx[0], GROUP)
    small = [
        pltpu.make_async_copy(src, box.at[n], box_sems.at[n])
        for n, src in enumerate((cell, atom))
    ]
    copies = []
    for j in range(GROUP):
        first = pl.multiple_of((k ^ j) * rows, rows)
        for n, (src, length) in enumerate(
            (
                (cot.at[pl.ds(first, rows)], (0, rows)),
                (value, (rows, count)),
                (pot, (rows + count, ny)),
            )
        ):
            copies.append(
                pltpu.make_async_copy(src, blocks[j].at[pl.ds(*length)], sems.at[4 * j + n])
            )
    for j in range(GROUP):
        first = pl.multiple_of((k ^ j) * rows, rows)
        copies.append(
            pltpu.make_async_copy(orb.at[pl.ds(first, rows)], blocks[GROUP + j], sems.at[4 * j + 3])
        )
    for copy in small + copies:
        copy.start()
    first_atom = (idx[0] - k - 1) * atom_dev
    for t in range((GROUP + 2) * atom_dev):
        a = first_atom + t
        a = jnp.where(a < 0, a + atoms, jnp.where(a >= atoms, a - atoms, a))
        consts[t : t + 1, :] = jnp.full((1, LANES), energy[a] * (1.0 / spectral_half), F32)
    for n in range(4):
        at = (GROUP + 2) * atom_dev + n
        consts[at : at + 1, :] = jnp.full((1, LANES), cheb[n], F32)
    for copy in small:
        copy.wait()
    shifted = box[1] + (atoms - (idx[0] - 1) * atom_dev)
    shifted = jnp.where(shifted >= 2 * atoms, shifted - 2 * atoms, shifted)
    slot = jnp.where(shifted >= atoms, shifted - atoms, shifted)
    for j in range(GROUP):
        at = rows + count + ny
        blocks[j][at : at + count, :] = box[0].astype(F32)
        blocks[j][at + count : at + 2 * count, :] = slot.astype(F32)
    for copy in copies:
        copy.wait()


def fill_dense(ny, slots, k, ins, out):
    block = 8 * ny
    rows = (ins[0].shape[0] - block - ny) // 3
    rest = block + rows + ny
    half = jnp.bfloat16
    place = lax.broadcasted_iota(jnp.int32, (ny * 8, LANES), 0).astype(F32).astype(half)
    column = lax.broadcasted_iota(jnp.int32, (LANES, LANES), 0).astype(F32).astype(half)
    one, none = jnp.ones((), half), jnp.zeros((), half)
    for j in range(GROUP):
        src = ins[j]
        cell = src[rest : rest + rows, :]
        line = jnp.floor(cell * (1.0 / LANES))
        z = (cell - line * LANES).astype(half)
        code = (line * 8 + src[rest + rows : rest + 2 * rows, :]).astype(half)
        value = src[block : block + rows, :]
        high = value.astype(half)
        low = (value - high.astype(F32)).astype(half)
        left, right = [], []
        for r in range(rows):
            left.append(jnp.where(place == code[r : r + 1, :], one, none))
            hit = column == z[r : r + 1, :]
            right.append(
                jnp.concatenate(
                    [jnp.where(hit, piece[r : r + 1, :], none) for piece in (high, low)], axis=0
                )
            )
        both = lax.dot_general(
            jnp.concatenate(left, axis=1),
            jnp.concatenate(right, axis=1),
            (((1,), (1,)), ((), ())),
            preferred_element_type=F32,
        )
        dense = both[:, :LANES] + both[:, LANES:]
        first = pl.multiple_of((k ^ j) * ny, ny)
        out[pl.ds(first, ny)] = dense.reshape(ny, 8, LANES)
        pot = (src[block + rows : rest, :] - (spectral_center - 3.0)) * (1.0 / spectral_half)
        out[pl.ds(first, ny), slots : slots + 1, :] = pot.reshape(ny, 1, LANES)


def edge_tiles(tile, width, shift):
    lane = lane_iota(tile.shape)
    above = jnp.where(lane < width, pltpu.roll(tile, LANES - shift, 1), 0.0)
    below = jnp.where((lane >= shift) & (lane < shift + width), pltpu.roll(tile, shift, 1), 0.0)
    return above, below


def coef_tile(sums, slots, atom_dev):
    atoms = (GROUP + 2) * atom_dev
    lane = lane_iota((8, LANES))
    tile = jnp.zeros((8, LANES), F32)
    for t in range(atoms):
        total = None
        for p in range(GROUP):
            slot = t - p * atom_dev
            if 0 <= slot < slots:
                total = sums[p][slot] if total is None else total + sums[p][slot]
        tile = jnp.where(lane == t, jnp.sum(total, axis=1, keepdims=True), tile)
    return tile


def relay_kernel(ny, atom_dev, first, idx, *refs):
    slots = 3 * atom_dev
    ins, (dense, field, tile_out, up, down, sums) = refs[:GROUP], refs[GROUP:]
    k = lax.rem(idx[0], GROUP)
    if first:
        fill_dense(ny, slots, k, ins, dense)
    un = 8
    for j in range(GROUP):
        p = k ^ j
        src = ins[j]

        def body(yb, accs, src=src, p=p):
            accs = list(accs)
            for yy in range(un):
                y = yb * un + yy
                v = src[pl.ds(y, 8, stride=ny), :]
                row = p * ny + y
                field[row] = v
                for s in range(slots):
                    accs[s] = accs[s] + v * dense[row, s : s + 1, :]
            return tuple(accs)

        zero = jnp.zeros((8, LANES), F32)
        accs = lax.fori_loop(0, ny // un, body, (zero,) * slots)
        for s in range(slots):
            sums[p * slots + s] = accs[s]
    parts = [[sums[p * slots + s] for s in range(slots)] for p in range(GROUP)]
    tile = coef_tile(parts, slots, atom_dev)
    tile_out[...] = tile
    above, below = edge_tiles(tile, 2 * atom_dev, GROUP * atom_dev)
    up[ny] = above
    down[ny] = below
    up[0:ny] = field[(GROUP - 1) * ny : GROUP * ny]
    down[0:ny] = field[0:ny]


def step_kernel(kind, ny, devices, atoms, *refs):
    atom_dev = atoms // devices
    slots = 3 * atom_dev
    refs = list(refs)
    take = lambda count: [refs.pop(0) for _ in range(count)]
    consts, dense, field, tile_in, below, above = take(6)
    zsum = refs.pop()
    if kind == "b1":
        (other,) = take(1)
    elif kind == "t2":
        other, full_zero, b1, tile_b1, b2, tile_b2, cot, full_cot = take(8)
    elif kind == "out":
        other, cot, gp, e, e_below, e_above = take(6)
    if kind in ("b2", "t1"):
        new, tile_out, up, down, full_out = refs
    elif kind == "b1":
        new, tile_out, up, down = refs
    elif kind == "t2":
        gp, e_out, e_up, e_down = refs
    else:
        (new,) = refs

    full = tile_in[...] + below[ny] + above[ny]
    if kind in ("b2", "t1"):
        full_out[...] = full
    near = (GROUP + 2) * atom_dev
    c0, c1, c2, c3 = [consts[near + n : near + n + 1, :] for n in range(4)]
    keep, scale, mix = {
        "t1": (None, 1.0, None),
        "t2": (None, 2.0, -1.0),
        "b2": (c2, 2.0 * c3, None),
        "b1": (None, 2.0, c1 - c3),
        "out": (None, 1.0, -1.0),
    }[kind]
    spread = []
    for t in range(near):
        coupling = consts[t : t + 1, :] * scale
        spread.append(jnp.broadcast_to(full[:, t : t + 1], (8, LANES)) * coupling)
    side = scale * (-0.5 / spectral_half)
    un = 32
    sums = []
    part = 9 * ny + 8
    lane, line = (lax.broadcasted_iota(jnp.int32, (2 * LANES, LANES), d) for d in (1, 0))
    apart = (lane - line) % LANES
    turn = jnp.where((apart == 1) | (apart == LANES - 1), 1.0, 0.0).astype(jnp.bfloat16)
    for p in range(GROUP):
        flat = field[p * ny : (p + 1) * ny].reshape(8 * ny, LANES)
        high = flat.astype(jnp.bfloat16)
        low = (flat - high.astype(F32)).astype(jnp.bfloat16)
        zsum[p * ny : (p + 1) * ny] = jnp.dot(
            jnp.concatenate([high, low], axis=1), turn, preferred_element_type=F32
        ).reshape(ny, 8, LANES)
    for p in range(GROUP):

        def body(yb, accs, p=p):
            accs = list(accs)
            rows = []
            first = yb * un
            before = p * ny + jnp.where(first == 0, ny - 1, first - 1)
            after = p * ny + jnp.where(first == ny - un, 0, first + un)
            lines = [field[before]] + [field[p * ny + first + yy] for yy in range(un)] + [field[after]]
            for yy in range(un):
                y = first + yy
                row = p * ny + y
                earlier, v, later = lines[yy : yy + 3]
                under = field[row - ny] if p > 0 else below[y]
                over = field[row + ny] if p < GROUP - 1 else above[y]
                beside = (later + earlier) + (under + over)
                beside = beside + zsum[row]
                pot = dense[row, slots : slots + 1, :] * scale
                if keep is not None:
                    pot = pot + keep
                weights = [dense[row, s : s + 1, :] for s in range(slots)]
                a = [spread[p * atom_dev + s] * weights[s] for s in range(slots)]
                while len(a) > 1:
                    a = [sum(a[n : n + 2][1:], a[n]) for n in range(0, len(a), 2)]
                a = a[0]
                x = v * pot + beside * side + a
                if mix is not None:
                    x = x + other[row] * mix
                if kind == "out":
                    x = x + cot[row] * c0
                    new[pl.ds(p * part + y, 8, stride=ny), :] = x
                elif kind == "t2":
                    g = b1[row] * other[row] + 2.0 * (b2[row] * v)
                    g = g + (2.0 * c3) * (cot[row] * x)
                    rows.append(jnp.sum(g, axis=0, keepdims=True))
                else:
                    new[row] = x
                if kind != "out":
                    for s in range(slots):
                        accs[s] = accs[s] + x * weights[s]
            if kind == "t2":
                start = pl.multiple_of(p * ny + yb * un, un)
                gp[pl.ds(start, un), :] = jnp.concatenate(rows, axis=0) * (1.0 / spectral_half)
            return tuple(accs)

        zero = jnp.zeros((8, LANES), F32)
        init = () if kind == "out" else (zero,) * slots
        sums.append(lax.fori_loop(0, ny // un, body, init))
    if kind == "out":
        total = e[...] + e_below[...] + e_above[...]
        for p in range(GROUP):
            rest = p * part + 8 * ny
            new[rest : rest + ny, :] = gp[p * ny : (p + 1) * ny, :]
            new[rest + ny : rest + ny + 8, :] = total
        return
    tile = coef_tile(sums, slots, atom_dev)
    if kind == "t2":
        e = tile_b1[...] * full_zero[...] + 2.0 * (tile_b2[...] * full)
        e = e + (2.0 * c3) * (full_cot[...] * tile)
        e = jnp.sum(e, axis=0, keepdims=True) * (1.0 / spectral_half)
        e = jnp.broadcast_to(e, (8, LANES))
        e_out[...] = e
        lane = lane_iota(e.shape)
        shift = GROUP * atom_dev
        own = (lane >= atom_dev) & (lane < shift + atom_dev)
        e_up[...] = jnp.where(own, pltpu.roll(e, LANES - shift, 1), 0.0)
        e_down[...] = jnp.where(own, pltpu.roll(e, shift, 1), 0.0)
        return
    tile_out[...] = tile
    over, under = edge_tiles(tile, 2 * atom_dev, GROUP * atom_dev)
    up[ny] = over
    down[ny] = under
    up[0:ny] = new[(GROUP - 1) * ny : GROUP * ny]
    down[0:ny] = new[0:ny]


def final_kernel(ny, atom_dev, idx, *refs):
    blocks, (out, gp_out, e_out, gp, sems) = refs[:GROUP], refs[GROUP:]
    k = lax.rem(idx[0], GROUP)
    rows = 8 * ny
    copies, parts = [], []
    for j in range(GROUP):
        start = pl.multiple_of(k * (rows + ny + 8), 8) if j == 0 else 0
        first = pl.multiple_of((k ^ j) * rows, rows)
        copies.append(
            pltpu.make_async_copy(
                blocks[j].at[pl.ds(start, rows)], out.at[pl.ds(first, rows)], sems.at[j]
            )
        )
        parts.append(blocks[j][pl.ds(start + rows, ny + 8), :])
    for copy in copies:
        copy.start()
    total = (parts[0] + parts[1]) + (parts[2] + parts[3])
    gp[...] = total[0:ny]
    last = pltpu.make_async_copy(gp, gp_out, sems.at[GROUP])
    last.start()
    e = total[ny : ny + 1]
    lane = lane_iota(e.shape)
    for n in range(atom_dev):
        e_out[n] = jnp.sum(jnp.where(lane == (k + 1) * atom_dev + n, e, 0.0))
    for copy in copies + [last]:
        copy.wait()


def per_device(orbitals, cotangent, potential, cheb_coef, energy, proj_cell, proj_atom, proj_value):
    orb, _, ny, nz = orbitals.shape
    devices = lax.axis_size("grid")
    slabs = devices // GROUP
    atoms = energy.shape[0]
    atom_dev = atoms // devices
    points = proj_cell.shape[0] // LANES
    assert orb == 8 * GROUP and nz == LANES and devices % GROUP == 0
    idx = lax.axis_index("grid").astype(jnp.int32).reshape(1)
    block = 8 * ny
    plane = GROUP * ny

    def near(x, j):
        return lax.ppermute(x, "grid", [(a, a ^ j) for a in range(devices)])

    to_above = [
        (GROUP * s + m, GROUP * ((s + 1) % slabs) + m) for s in range(slabs) for m in range(GROUP)
    ]
    to_below = [(b, a) for a, b in to_above]

    def halo(up, down):
        return lax.ppermute(up, "grid", to_above), lax.ppermute(down, "grid", to_below)

    def gather(blocks):
        return [blocks[0]] + [near(blocks[j], j) for j in range(1, GROUP)]

    consts, *blocks = call(
        functools.partial(prep_kernel, devices, atoms),
        [(-(-(GROUP * atom_dev + 2 * atom_dev + 4) // 8) * 8, LANES)]
        + [(block + 3 * points + ny, LANES)] * GROUP
        + [(block, LANES)] * GROUP,
        idx,
        cheb_coef,
        energy,
        proj_cell.reshape(points, LANES),
        proj_atom.reshape(points, LANES),
        proj_value.reshape(points, LANES),
        potential.reshape(ny, LANES),
        cotangent.reshape(orb * ny, LANES),
        orbitals.reshape(orb * ny, LANES),
        micros=1.2,
        scratch=[
            pltpu.VMEM((2, points, LANES), jnp.int32),
            pltpu.SemaphoreType.DMA((4 * GROUP,)),
            pltpu.SemaphoreType.DMA((2,)),
        ],
        smem=(0, 1, 2),
        hbm_args=(3, 4, 5, 6, 7, 8),
    )
    cot_blocks = gather(blocks[:GROUP])
    orb_blocks = gather(blocks[GROUP:])
    field_shape, tile_shape, edge_shape = (plane, 8, LANES), (8, LANES), (ny + 1, 8, LANES)
    chain = [field_shape, tile_shape, edge_shape, edge_shape]

    def relay(first, blocks, *args):
        return call(
            functools.partial(relay_kernel, ny, atom_dev, first),
            ([field_shape] if first else []) + chain,
            idx,
            *blocks,
            *args,
            micros=2.0 if first else 0.7,
            scratch=[pltpu.VMEM((GROUP * 3 * atom_dev, 8, LANES), F32)],
            smem=(0,),
        )

    def step(kind, outs, *args):
        return call(
            functools.partial(step_kernel, kind, ny, devices, atoms),
            outs,
            consts,
            dense,
            *args,
            micros=1.5,
            scratch=[pltpu.VMEM(field_shape, F32)],
        )

    dense, cot, tile_cot, up, down = relay(True, cot_blocks)
    cot_halo = halo(up, down)
    zero, tile_zero, up, down = relay(False, orb_blocks, dense)
    zero_halo = halo(up, down)
    b2, tile_b2, up, down, full_cot = step("b2", chain + [tile_shape], cot, tile_cot, *cot_halo)
    b2_halo = halo(up, down)
    t1, tile_t1, up, down, full_zero = step("t1", chain + [tile_shape], zero, tile_zero, *zero_halo)
    t1_halo = halo(up, down)
    b1, tile_b1, up, down = step("b1", chain, b2, tile_b2, *b2_halo, cot)
    b1_halo = halo(up, down)
    gp, e, e_up, e_down = step(
        "t2",
        [(plane, LANES)] + [tile_shape] * 3,
        t1,
        tile_t1,
        *t1_halo,
        zero,
        full_zero,
        b1,
        tile_b1,
        b2,
        tile_b2,
        cot,
        full_cot,
    )
    (image,) = step(
        "out",
        [(GROUP * (block + ny + 8), LANES)],
        b1,
        tile_b1,
        *b1_halo,
        b2,
        cot,
        gp,
        e,
        *halo(e_up, e_down),
    )
    member, part = lax.rem(idx[0], GROUP), block + ny + 8
    images = [image] + [
        near(lax.dynamic_slice_in_dim(image, (member ^ j) * part, part, 0), j)
        for j in range(1, GROUP)
    ]
    out, gp, e = call(
        functools.partial(final_kernel, ny, atom_dev),
        [(orb * ny, LANES), (ny, LANES), (atom_dev,)],
        idx,
        *images,
        micros=1.0,
        scratch=[pltpu.VMEM((ny, LANES), F32), pltpu.SemaphoreType.DMA((GROUP + 1,))],
        smem=(0,),
        hbm_outs=(0, 1),
        smem_outs=(2,),
    )
    return out.reshape(orbitals.shape), gp.reshape(potential.shape), e


def solution(mesh):
    placed = (
        P("sample", "grid", None, None),
        P("sample", "grid", None, None),
        P("grid", None, None),
        P(),
        P(),
        P("grid"),
        P("grid"),
        P("grid"),
    )
    return jax.shard_map(
        per_device,
        mesh=mesh,
        in_specs=placed,
        out_specs=(
            P("sample", "grid", None, None),
            P(("sample", "grid"), None, None),
            P(("sample", "grid")),
        ),
        check_vma=False,
    )
```

time: 82.3 us -> 63.6 us (0.77)
  Pallas kernels: 20.8 us -> 11 us
  starting transfers between devices: 36.8 us -> 28.8 us
  local copies, waits for them, and re-layouts: 2.88 us -> 0.71 us
  waiting for transfers between devices: 20.6 us -> 22.1 us
    pallas_call x13 -> x9, Pallas kernels: 20.8 us -> 11 us  [call(): pl.pallas_call(body, out_shape=out_shape, in_specs=in_specs, out_specs=ou...]
    ppermute x15 -> x9, starting transfers between devices: 16.9 us -> 8.38 us  [near(): return lax.ppermute(x, 'grid', [(a, a ^ j) for a in range(devices)])]
    ppermute x6, starting transfers between devices: 2.96 us -> 8.55 us  [halo(): lax.ppermute(up, 'grid', to_above)]
    ppermute x6, starting transfers between devices: 17 us -> 11.8 us  [halo(): lax.ppermute(down, 'grid', to_below)]
    ppermute x6, waiting for transfers between devices: 2.14 us -> 6.57 us  [halo(): lax.ppermute(down, 'grid', to_below)]
    ppermute x6, waiting for transfers between devices: 4.64 us -> 1.91 us  [halo(): lax.ppermute(up, 'grid', to_above)]
    unnamed x17 -> x4, local copies, waits for them, and re-layouts: 2.33 us -> 0.66 us
    ppermute x15 -> x9, waiting for transfers between devices: 13.8 us -> 13.6 us  [near(): return lax.ppermute(x, 'grid', [(a, a ^ j) for a in range(devices)])]
  transfers between devices with their start and end apart: 27 -> 21, of which waited for: 9 -> 9; matrix products, arithmetic and copies ran while one was open for 0% -> 0% of each run, Pallas kernels for 20% -> 11%
where the time goes in v2:
time: 63.6 us; the launch traced here: 63.3 us
  starting transfers between devices  28.8 us (45%)
  waiting for transfers between devices  22.1 us (35%)
  Pallas kernels  11 us (17%)
  local copies, waits for them, and re-layouts  0.71 us (1%)
  between operations  0.7 us (1%)
    ppermute x9, waiting for transfers between devices, near(): return lax.ppermute(x, 'grid', [(a, a ^ j) for a in range(devices)])  13.6 us
    ppermute x6, starting transfers between devices, halo(): lax.ppermute(down, 'grid', to_below)  11.8 us
    pallas_call x9, Pallas kernels, call(): pl.pallas_call(body, out_shape=out_shape, in_specs=in_specs, out_specs=ou...  11 us
    ppermute x6, starting transfers between devices, halo(): lax.ppermute(up, 'grid', to_above)  8.55 us
    ppermute x9, starting transfers between devices, near(): return lax.ppermute(x, 'grid', [(a, a ^ j) for a in range(devices)])  8.38 us
    ppermute x6, waiting for transfers between devices, halo(): lax.ppermute(down, 'grid', to_below)  6.57 us
    ppermute x6, waiting for transfers between devices, halo(): lax.ppermute(up, 'grid', to_above)  1.91 us
  transfers between devices with their start and end apart: 21, of which 9 were waited for; matrix products, arithmetic and copies ran while one was open for 0% of the time, Pallas kernels for 11%

profile of v2, /device:TPU:1, one launch (start us, length us, event | category | flops | bytes accessed | tf_op | source)
XLA Modules:
  0.0 63.3 jit_solution(1396100375491314187)
XLA Ops:
  1.3 2.1 %shard_map.103 = (f32[16,128]{1,0:T(8,128)S(1)}, f32[336,128]{1,0:T(8,128)S(1)}, f32[336,128]{1,0:T(8,128)S(1)}, f32[336,128]{1,0:T(8,128)S(1)}, f32[336,128]{1,...) custom-call(s32[1]{0:T(128)} %bitcast.idx, ...), custom_call_target="tpu_custom_call" | custom-call | flops 1200000 | bytes 4428000 | tf_op jit(solution)/shard_map/pallas_call | solution.py:41
  3.5 2.7 %collective-permute-start.1 = (f32[336,128]{1,0:T(8,128)S(1)}, f32[336,128]{1,0:T(8,128)S(1)}, u32[]{:S(2)}, u32[]{:S(2)}) collective-permute-start(f32[336,128]{1,0:T(8,128)S(1)} %get-tuple-element.45), channel_id=1, source_target_pairs={{0,2},{1,3},{2,0},{3,1},{4,6},{5,7},{6,4},{7,5},{8,10},{9,11},{10,... | collective-permute-start | bytes 516104 | tf_op jit(solution)/shard_map/ppermute | solution.py:374
  6.2 1.7 %collective-permute-start.10 = (f32[256,128]{1,0:T(8,128)S(1)}, f32[256,128]{1,0:T(8,128)S(1)}, u32[]{:S(2)}, u32[]{:S(2)}) collective-permute-start(f32[256,128]{1,0:T(8,128)S(1)} %get-tuple-element.62), channel_id=1, source_target_pairs={{0,2},{1,3},{2,0},{3,1},{4,6},{5,7},{6,4},{7,5},{8,10},{9,11},{10,... | collective-permute-start | bytes 393224 | tf_op jit(solution)/shard_map/ppermute | solution.py:374
  8.4 2.5 %collective-permute-done.1.refs_2_ = f32[336,128]{1,0:T(8,128)S(1)} collective-permute-done((f32[336,128]{1,0:T(8,128)S(1)}, f32[336,128]{1,0:T(8,128)S(1)}, u32[]{:S(2)}, u32[]{:S(2)}) %collective-permute-start.1) | collective-permute-done | bytes 172064 | tf_op jit(solution)/shard_map/ppermute | solution.py:374
  10.9 3.9 %collective-permute-done.2.refs_3_ = f32[336,128]{1,0:T(8,128)S(1)} collective-permute-done((f32[336,128]{1,0:T(8,128)S(1)}, f32[336,128]{1,0:T(8,128)S(1)}, u32[]{:S(2)}, u32[]{:S(2)}) %collective-permute-start.2) | collective-permute-done | bytes 172064 | tf_op jit(solution)/shard_map/ppermute | solution.py:374
  14.8 2.0 %shard_map.104 = (f32[128,8,128]{2,1,0:T(8,128)S(1)}, f32[128,8,128]{2,1,0:T(8,128)S(1)}, f32[8,128]{1,0:T(8,128)S(1)}, f32[33,8,128]{2,1,0:T(8,128)S(1)}, f32[33,8,128]{2,1,0:T(8,128)S(1)}) custom-call(s32[1]{0:T(128)} %bitcast.idx, f32[336,128]{1,0:T(8,128)S(1)} %get-tuple-element.43.refs_0_, f32[336,128]{1,0:T(8,128)S(1)} %collective-permute-done.refs_1_, ...), custom_call_target="tpu_custom_call" | custom-call | flops 2000000 | bytes 7380000 | tf_op jit(solution)/shard_map/pallas_call | solution.py:41
  16.8 1.8 %collective-permute-start.3 = (f32[33,8,128]{2,1,0:T(8,128)S(1)}, f32[33,8,128]{2,1,0:T(8,128)S(1)}, u32[]{:S(2)}, u32[]{:S(2)}) collective-permute-start(f32[33,8,128]{2,1,0:T(8,128)S(1)} %get-tuple-element.50), channel_id=1, source_target_pairs={{0,4},{1,5},{2,6},{3,7},{4,8},{5,9},{6,10},{7,11},{8,12},{9,13},{1... | collective-permute-start | bytes 405512 | tf_op jit(solution)/shard_map/ppermute | solution.py:382
  18.5 2.1 %collective-permute-start.4 = (f32[33,8,128]{2,1,0:T(8,128)S(1)}, f32[33,8,128]{2,1,0:T(8,128)S(1)}, u32[]{:S(2)}, u32[]{:S(2)}) collective-permute-start(f32[33,8,128]{2,1,0:T(8,128)S(1)} %get-tuple-element.51), channel_id=1, source_target_pairs={{4,0},{5,1},{6,2},{7,3},{8,4},{9,5},{10,6},{11,7},{12,8},{13,9},{1... | collective-permute-start | bytes 405512 | tf_op jit(solution)/shard_map/ppermute | solution.py:382
  21.3 1.3 %collective-permute-start.12 = (f32[33,8,128]{2,1,0:T(8,128)S(1)}, f32[33,8,128]{2,1,0:T(8,128)S(1)}, u32[]{:S(2)}, u32[]{:S(2)}) collective-permute-start(f32[33,8,128]{2,1,0:T(8,128)S(1)} %get-tuple-element.66), channel_id=1, source_target_pairs={{0,4},{1,5},{2,6},{3,7},{4,8},{5,9},{6,10},{7,11},{8,12},{9,13},{1... | collective-permute-start | bytes 405512 | tf_op jit(solution)/shard_map/ppermute | solution.py:382
  22.7 2.1 %collective-permute-start.13 = (f32[33,8,128]{2,1,0:T(8,128)S(1)}, f32[33,8,128]{2,1,0:T(8,128)S(1)}, u32[]{:S(2)}, u32[]{:S(2)}) collective-permute-start(f32[33,8,128]{2,1,0:T(8,128)S(1)} %get-tuple-element.67), channel_id=1, source_target_pairs={{4,0},{5,1},{6,2},{7,3},{8,4},{9,5},{10,6},{11,7},{12,8},{13,9},{1... | collective-permute-start | bytes 405512 | tf_op jit(solution)/shard_map/ppermute | solution.py:382
  24.8 1.8 %collective-permute-done.4.refs_5_ = f32[33,8,128]{2,1,0:T(8,128)S(1)} collective-permute-done((f32[33,8,128]{2,1,0:T(8,128)S(1)}, f32[33,8,128]{2,1,0:T(8,128)S(1)}, u32[]{:S(2)}, u32[]{:S(2)}) %collective-permute-start.4) | collective-permute-done | bytes 135200 | tf_op jit(solution)/shard_map/ppermute | solution.py:382
  26.6 0.9 %shard_map.105 = (f32[128,8,128]{2,1,0:T(8,128)S(1)}, f32[8,128]{1,0:T(8,128)S(1)}, f32[33,8,128]{2,1,0:T(8,128)S(1)}, f32[33,8,128]{2,1,0:T(8,128)S(1)}, f32[8,128]{1,0:T(8,128)S(1)}) custom-call(f32[16,128]{1,0:T(8,128)S(1)} %get-tuple-element.42.refs_0_, f32[128,8,128]{2,1,0:T(8,128)S(1)} %get-tuple-element.47.refs_1_.refs_4_, ...), custom_call_target="tpu_custom_call" | custom-call | flops 1500000 | bytes 5535000 | tf_op jit(solution)/shard_map/pallas_call | solution.py:41
  27.6 1.3 %collective-permute-start.5 = (f32[33,8,128]{2,1,0:T(8,128)S(1)}, f32[33,8,128]{2,1,0:T(8,128)S(1)}, u32[]{:S(2)}, u32[]{:S(2)}) collective-permute-start(f32[33,8,128]{2,1,0:T(8,128)S(1)} %get-tuple-element.54), channel_id=1, source_target_pairs={{0,4},{1,5},{2,6},{3,7},{4,8},{5,9},{6,10},{7,11},{8,12},{9,13},{1... | collective-permute-start | bytes 405512 | tf_op jit(solution)/shard_map/ppermute | solution.py:382
  28.8 2.0 %collective-permute-start.6 = (f32[33,8,128]{2,1,0:T(8,128)S(1)}, f32[33,8,128]{2,1,0:T(8,128)S(1)}, u32[]{:S(2)}, u32[]{:S(2)}) collective-permute-start(f32[33,8,128]{2,1,0:T(8,128)S(1)} %get-tuple-element.55), channel_id=1, source_target_pairs={{4,0},{5,1},{6,2},{7,3},{8,4},{9,5},{10,6},{11,7},{12,8},{13,9},{1... | collective-permute-start | bytes 405512 | tf_op jit(solution)/shard_map/ppermute | solution.py:382
  30.8 1.5 %collective-permute-done.13.refs_5_ = f32[33,8,128]{2,1,0:T(8,128)S(1)} collective-permute-done((f32[33,8,128]{2,1,0:T(8,128)S(1)}, f32[33,8,128]{2,1,0:T(8,128)S(1)}, u32[]{:S(2)}, u32[]{:S(2)}) %collective-permute-start.13) | collective-permute-done | bytes 135200 | tf_op jit(solution)/shard_map/ppermute | solution.py:382
  32.4 0.9 %shard_map.108 = (f32[128,8,128]{2,1,0:T(8,128)S(1)}, f32[8,128]{1,0:T(8,128)S(1)}, f32[33,8,128]{2,1,0:T(8,128)S(1)}, f32[33,8,128]{2,1,0:T(8,128)S(1)}, f32[8,128]{1,0:T(8,128)S(1)}) custom-call(f32[16,128]{1,0:T(8,128)S(1)} %get-tuple-element.42.refs_0_, f32[128,8,128]{2,1,0:T(8,128)S(1)} %get-tuple-element.47.refs_1_.refs_4_, ...), custom_call_target="tpu_custom_call" | custom-call | flops 1500000 | bytes 5535000 | tf_op jit(solution)/shard_map/pallas_call | solution.py:41
  33.3 1.3 %collective-permute-start.14 = (f32[33,8,128]{2,1,0:T(8,128)S(1)}, f32[33,8,128]{2,1,0:T(8,128)S(1)}, u32[]{:S(2)}, u32[]{:S(2)}) collective-permute-start(f32[33,8,128]{2,1,0:T(8,128)S(1)} %get-tuple-element.70), channel_id=1, source_target_pairs={{0,4},{1,5},{2,6},{3,7},{4,8},{5,9},{6,10},{7,11},{8,12},{9,13},{1... | collective-permute-start | bytes 405512 | tf_op jit(solution)/shard_map/ppermute | solution.py:382
  34.5 2.0 %collective-permute-start.15 = (f32[33,8,128]{2,1,0:T(8,128)S(1)}, f32[33,8,128]{2,1,0:T(8,128)S(1)}, u32[]{:S(2)}, u32[]{:S(2)}) collective-permute-start(f32[33,8,128]{2,1,0:T(8,128)S(1)} %get-tuple-element.71), channel_id=1, source_target_pairs={{4,0},{5,1},{6,2},{7,3},{8,4},{9,5},{10,6},{11,7},{12,8},{13,9},{1... | collective-permute-start | bytes 405512 | tf_op jit(solution)/shard_map/ppermute | solution.py:382
  36.6 1.6 %collective-permute-done.6.refs_5_ = f32[33,8,128]{2,1,0:T(8,128)S(1)} collective-permute-done((f32[33,8,128]{2,1,0:T(8,128)S(1)}, f32[33,8,128]{2,1,0:T(8,128)S(1)}, u32[]{:S(2)}, u32[]{:S(2)}) %collective-permute-start.6) | collective-permute-done | bytes 135200 | tf_op jit(solution)/shard_map/ppermute | solution.py:382
  38.2 0.9 %shard_map.106 = (f32[128,8,128]{2,1,0:T(8,128)S(1)}, f32[8,128]{1,0:T(8,128)S(1)}, f32[33,8,128]{2,1,0:T(8,128)S(1)}, f32[33,8,128]{2,1,0:T(8,128)S(1)}) custom-call(f32[16,128]{1,0:T(8,128)S(1)} %get-tuple-element.42.refs_0_, f32[128,8,128]{2,1,0:T(8,128)S(1)} %get-tuple-element.47.refs_1_.refs_4_, ...), custom_call_target="tpu_custom_call" | custom-call | flops 1500000 | bytes 5535000 | tf_op jit(solution)/shard_map/pallas_call | solution.py:41
  39.1 1.5 %collective-permute-start.7 = (f32[33,8,128]{2,1,0:T(8,128)S(1)}, f32[33,8,128]{2,1,0:T(8,128)S(1)}, u32[]{:S(2)}, u32[]{:S(2)}) collective-permute-start(f32[33,8,128]{2,1,0:T(8,128)S(1)} %get-tuple-element.58), channel_id=1, source_target_pairs={{0,4},{1,5},{2,6},{3,7},{4,8},{5,9},{6,10},{7,11},{8,12},{9,13},{1... | collective-permute-start | bytes 405512 | tf_op jit(solution)/shard_map/ppermute | solution.py:382
  40.6 1.8 %collective-permute-start.8 = (f32[33,8,128]{2,1,0:T(8,128)S(1)}, f32[33,8,128]{2,1,0:T(8,128)S(1)}, u32[]{:S(2)}, u32[]{:S(2)}) collective-permute-start(f32[33,8,128]{2,1,0:T(8,128)S(1)} %get-tuple-element.59), channel_id=1, source_target_pairs={{4,0},{5,1},{6,2},{7,3},{8,4},{9,5},{10,6},{11,7},{12,8},{13,9},{1... | collective-permute-start | bytes 405512 | tf_op jit(solution)/shard_map/ppermute | solution.py:382
  42.4 1.6 %collective-permute-done.15.refs_5_ = f32[33,8,128]{2,1,0:T(8,128)S(1)} collective-permute-done((f32[33,8,128]{2,1,0:T(8,128)S(1)}, f32[33,8,128]{2,1,0:T(8,128)S(1)}, u32[]{:S(2)}, u32[]{:S(2)}) %collective-permute-start.15) | collective-permute-done | bytes 135200 | tf_op jit(solution)/shard_map/ppermute | solution.py:382
  44.0 1.2 %shard_map.109 = (f32[128,128]{1,0:T(8,128)S(1)}, f32[8,128]{1,0:T(8,128)S(1)}, f32[8,128]{1,0:T(8,128)S(1)}, f32[8,128]{1,0:T(8,128)S(1)}) custom-call(f32[16,128]{1,0:T(8,128)S(1)} %get-tuple-element.42.refs_0_, f32[128,8,128]{2,1,0:T(8,128)S(1)} %get-tuple-element.47.refs_1_.refs_4_, f32[128,8,128]{2,1,0:T(8,128)S(1)} %get-tuple-element.68.refs_2_, ...), custom_call_target="tpu_custom_call" | custom-call | flops 1500000 | bytes 5535000 | tf_op jit(solution)/shard_map/pallas_call | solution.py:41
  45.2 1.4 %collective-permute-start.16 = (f32[8,128]{1,0:T(8,128)S(1)}, f32[8,128]{1,0:T(8,128)S(1)}, u32[]{:S(2)}, u32[]{:S(2)}) collective-permute-start(f32[8,128]{1,0:T(8,128)S(1)} %get-tuple-element.76), channel_id=1, source_target_pairs={{0,4},{1,5},{2,6},{3,7},{4,8},{5,9},{6,10},{7,11},{8,12},{9,13},{1... | collective-permute-start | bytes 12296 | tf_op jit(solution)/shard_map/ppermute | solution.py:382
  46.6 1.8 %collective-permute-start.17 = (f32[8,128]{1,0:T(8,128)S(1)}, f32[8,128]{1,0:T(8,128)S(1)}, u32[]{:S(2)}, u32[]{:S(2)}) collective-permute-start(f32[8,128]{1,0:T(8,128)S(1)} %get-tuple-element.77), channel_id=1, source_target_pairs={{4,0},{5,1},{6,2},{7,3},{8,4},{9,5},{10,6},{11,7},{12,8},{13,9},{1... | collective-permute-start | bytes 12296 | tf_op jit(solution)/shard_map/ppermute | solution.py:382
  48.5 1.9 %collective-permute-done.16.refs_10_ = f32[8,128]{1,0:T(8,128)S(1)} collective-permute-done((f32[8,128]{1,0:T(8,128)S(1)}, f32[8,128]{1,0:T(8,128)S(1)}, u32[]{:S(2)}, u32[]{:S(2)}) %collective-permute-start.16) | collective-permute-done | bytes 4128 | tf_op jit(solution)/shard_map/ppermute | solution.py:382
  51.3 1.7 %collective-permute-start.18 = (f32[296,128]{1,0:T(8,128)S(1)}, f32[296,128]{1,0:T(8,128)S(1)}, u32[]{:S(2)}, u32[]{:S(2)}) collective-permute-start(f32[296,128]{1,0:T(8,128)S(1)} %get-tuple-element.86), channel_id=1, source_target_pairs={{0,1},{1,0},{2,3},{3,2},{4,5},{5,4},{6,7},{7,6},{8,9},{9,8},{10,11... | collective-permute-start | bytes 454664 | tf_op jit(solution)/shard_map/ppermute | solution.py:374
  53.0 1.2 %collective-permute-start.19 = (f32[296,128]{1,0:T(8,128)S(1)}, f32[296,128]{1,0:T(8,128)S(1)}, u32[]{:S(2)}, u32[]{:S(2)}) collective-permute-start(f32[296,128]{1,0:T(8,128)S(1)} %get-tuple-element.85), channel_id=1, source_target_pairs={{0,2},{1,3},{2,0},{3,1},{4,6},{5,7},{6,4},{7,5},{8,10},{9,11},{10,... | collective-permute-start | bytes 454664 | tf_op jit(solution)/shard_map/ppermute | solution.py:374
  54.7 3.8 %collective-permute-done.19.refs_2_ = f32[296,128]{1,0:T(8,128)S(1)} collective-permute-done((f32[296,128]{1,0:T(8,128)S(1)}, f32[296,128]{1,0:T(8,128)S(1)}, u32[]{:S(2)}, u32[]{:S(2)}) %collective-permute-start.19) | collective-permute-done | bytes 151584 | tf_op jit(solution)/shard_map/ppermute | solution.py:374
  58.5 3.4 %collective-permute-done.20.refs_3_ = f32[296,128]{1,0:T(8,128)S(1)} collective-permute-done((f32[296,128]{1,0:T(8,128)S(1)}, f32[296,128]{1,0:T(8,128)S(1)}, u32[]{:S(2)}, u32[]{:S(2)}) %collective-permute-start.20) | collective-permute-done | bytes 151584 | tf_op jit(solution)/shard_map/ppermute | solution.py:374
  61.9 1.3 %shard_map.111 = (f32[1024,128]{1,0:T(8,128)}, f32[32,128]{1,0:T(8,128)}, f32[2]{0:T(128)}) custom-call(s32[1]{0:T(128)} %bitcast.idx, f32[1184,128]{1,0:T(8,128)S(1)} %shard_map.110.refs_0_, f32[296,128]{1,0:T(8,128)S(1)} %collective-permute-done.18.refs_1_, f32[296,128]{1,0:T(8,128)S(1)} %collective-permute-done.19.refs_2_, ...), custom_call_target="tpu_custom_call" | custom-call | flops 1000000 | bytes 3690000 | tf_op jit(solution)/shard_map/pallas_call | solution.py:41
  (24 shorter events, 3.4 us)
Async XLA Ops:
  0.6 0.7 %copy-start = (f32[4]{0:T(128)S(1)}, f32[4]{0:T(128)}, u32[]{:S(2)}) copy-start(f32[4]{0:T(128)} %cheb.1) | copy-start | bytes 52
  0.6 0.7 %copy-start.1 = (f32[32]{0:T(128)S(1)}, f32[32]{0:T(128)}, u32[]{:S(2)}) copy-start(f32[32]{0:T(128)} %energy.1) | copy-start | bytes 388
  3.4 4.8 %collective-permute-start = (f32[336,128]{1,0:T(8,128)S(1)}, f32[336,128]{1,0:T(8,128)S(1)}, u32[]{:S(2)}, u32[]{:S(2)}) collective-permute-start(f32[336,128]{1,0:T(8,128)S(1)} %get-tuple-element.44), channel_id=1, source_target_pairs={{0,1},{1,0},{2,3},{3,2},{4,5},{5,4},{6,7},{7,6},{8,9},{9,8},{10,11... | collective-permute-start | bytes 516104 | tf_op jit(solution)/shard_map/ppermute | solution.py:374
  3.5 7.3 %collective-permute-start.1 = (f32[336,128]{1,0:T(8,128)S(1)}, f32[336,128]{1,0:T(8,128)S(1)}, u32[]{:S(2)}, u32[]{:S(2)}) collective-permute-start(f32[336,128]{1,0:T(8,128)S(1)} %get-tuple-element.45), channel_id=1, source_target_pairs={{0,2},{1,3},{2,0},{3,1},{4,6},{5,7},{6,4},{7,5},{8,10},{9,11},{10,... | collective-permute-start | bytes 516104 | tf_op jit(solution)/shard_map/ppermute | solution.py:374
  6.2 8.6 %collective-permute-start.2 = (f32[336,128]{1,0:T(8,128)S(1)}, f32[336,128]{1,0:T(8,128)S(1)}, u32[]{:S(2)}, u32[]{:S(2)}) collective-permute-start(f32[336,128]{1,0:T(8,128)S(1)} %get-tuple-element.46), channel_id=1, source_target_pairs={{0,3},{1,2},{2,1},{3,0},{4,7},{5,6},{6,5},{7,4},{8,11},{9,10},{10,... | collective-permute-start | bytes 516104 | tf_op jit(solution)/shard_map/ppermute | solution.py:374
  6.2 14.4 %collective-permute-start.10 = (f32[256,128]{1,0:T(8,128)S(1)}, f32[256,128]{1,0:T(8,128)S(1)}, u32[]{:S(2)}, u32[]{:S(2)}) collective-permute-start(f32[256,128]{1,0:T(8,128)S(1)} %get-tuple-element.62), channel_id=1, source_target_pairs={{0,2},{1,3},{2,0},{3,1},{4,6},{5,7},{6,4},{7,5},{8,10},{9,11},{10,... | collective-permute-start | bytes 393224 | tf_op jit(solution)/shard_map/ppermute | solution.py:374
  7.9 12.7 %collective-permute-start.11 = (f32[256,128]{1,0:T(8,128)S(1)}, f32[256,128]{1,0:T(8,128)S(1)}, u32[]{:S(2)}, u32[]{:S(2)}) collective-permute-start(f32[256,128]{1,0:T(8,128)S(1)} %get-tuple-element.63), channel_id=1, source_target_pairs={{0,3},{1,2},{2,1},{3,0},{4,7},{5,6},{6,5},{7,4},{8,11},{9,10},{10,... | collective-permute-start | bytes 393224 | tf_op jit(solution)/shard_map/ppermute | solution.py:374
  8.2 12.4 %collective-permute-start.9 = (f32[256,128]{1,0:T(8,128)S(1)}, f32[256,128]{1,0:T(8,128)S(1)}, u32[]{:S(2)}, u32[]{:S(2)}) collective-permute-start(f32[256,128]{1,0:T(8,128)S(1)} %get-tuple-element.61), channel_id=1, source_target_pairs={{0,1},{1,0},{2,3},{3,2},{4,5},{5,4},{6,7},{7,6},{8,9},{9,8},{10,11... | collective-permute-start | bytes 393224 | tf_op jit(solution)/shard_map/ppermute | solution.py:374
  16.8 8.0 %collective-permute-start.3 = (f32[33,8,128]{2,1,0:T(8,128)S(1)}, f32[33,8,128]{2,1,0:T(8,128)S(1)}, u32[]{:S(2)}, u32[]{:S(2)}) collective-permute-start(f32[33,8,128]{2,1,0:T(8,128)S(1)} %get-tuple-element.50), channel_id=1, source_target_pairs={{0,4},{1,5},{2,6},{3,7},{4,8},{5,9},{6,10},{7,11},{8,12},{9,13},{1... | collective-permute-start | bytes 405512 | tf_op jit(solution)/shard_map/ppermute | solution.py:382
  18.5 8.1 %collective-permute-start.4 = (f32[33,8,128]{2,1,0:T(8,128)S(1)}, f32[33,8,128]{2,1,0:T(8,128)S(1)}, u32[]{:S(2)}, u32[]{:S(2)}) collective-permute-start(f32[33,8,128]{2,1,0:T(8,128)S(1)} %get-tuple-element.51), channel_id=1, source_target_pairs={{4,0},{5,1},{6,2},{7,3},{8,4},{9,5},{10,6},{11,7},{12,8},{13,9},{1... | collective-permute-start | bytes 405512 | tf_op jit(solution)/shard_map/ppermute | solution.py:382
  21.3 9.5 %collective-permute-start.12 = (f32[33,8,128]{2,1,0:T(8,128)S(1)}, f32[33,8,128]{2,1,0:T(8,128)S(1)}, u32[]{:S(2)}, u32[]{:S(2)}) collective-permute-start(f32[33,8,128]{2,1,0:T(8,128)S(1)} %get-tuple-element.66), channel_id=1, source_target_pairs={{0,4},{1,5},{2,6},{3,7},{4,8},{5,9},{6,10},{7,11},{8,12},{9,13},{1... | collective-permute-start | bytes 405512 | tf_op jit(solution)/shard_map/ppermute | solution.py:382
  22.7 9.7 %collective-permute-start.13 = (f32[33,8,128]{2,1,0:T(8,128)S(1)}, f32[33,8,128]{2,1,0:T(8,128)S(1)}, u32[]{:S(2)}, u32[]{:S(2)}) collective-permute-start(f32[33,8,128]{2,1,0:T(8,128)S(1)} %get-tuple-element.67), channel_id=1, source_target_pairs={{4,0},{5,1},{6,2},{7,3},{8,4},{9,5},{10,6},{11,7},{12,8},{13,9},{1... | collective-permute-start | bytes 405512 | tf_op jit(solution)/shard_map/ppermute | solution.py:382
  27.6 9.0 %collective-permute-start.5 = (f32[33,8,128]{2,1,0:T(8,128)S(1)}, f32[33,8,128]{2,1,0:T(8,128)S(1)}, u32[]{:S(2)}, u32[]{:S(2)}) collective-permute-start(f32[33,8,128]{2,1,0:T(8,128)S(1)} %get-tuple-element.54), channel_id=1, source_target_pairs={{0,4},{1,5},{2,6},{3,7},{4,8},{5,9},{6,10},{7,11},{8,12},{9,13},{1... | collective-permute-start | bytes 405512 | tf_op jit(solution)/shard_map/ppermute | solution.py:382
  28.8 9.4 %collective-permute-start.6 = (f32[33,8,128]{2,1,0:T(8,128)S(1)}, f32[33,8,128]{2,1,0:T(8,128)S(1)}, u32[]{:S(2)}, u32[]{:S(2)}) collective-permute-start(f32[33,8,128]{2,1,0:T(8,128)S(1)} %get-tuple-element.55), channel_id=1, source_target_pairs={{4,0},{5,1},{6,2},{7,3},{8,4},{9,5},{10,6},{11,7},{12,8},{13,9},{1... | collective-permute-start | bytes 405512 | tf_op jit(solution)/shard_map/ppermute | solution.py:382
  33.3 9.1 %collective-permute-start.14 = (f32[33,8,128]{2,1,0:T(8,128)S(1)}, f32[33,8,128]{2,1,0:T(8,128)S(1)}, u32[]{:S(2)}, u32[]{:S(2)}) collective-permute-start(f32[33,8,128]{2,1,0:T(8,128)S(1)} %get-tuple-element.70), channel_id=1, source_target_pairs={{0,4},{1,5},{2,6},{3,7},{4,8},{5,9},{6,10},{7,11},{8,12},{9,13},{1... | collective-permute-start | bytes 405512 | tf_op jit(solution)/shard_map/ppermute | solution.py:382
  34.5 9.4 %collective-permute-start.15 = (f32[33,8,128]{2,1,0:T(8,128)S(1)}, f32[33,8,128]{2,1,0:T(8,128)S(1)}, u32[]{:S(2)}, u32[]{:S(2)}) collective-permute-start(f32[33,8,128]{2,1,0:T(8,128)S(1)} %get-tuple-element.71), channel_id=1, source_target_pairs={{4,0},{5,1},{6,2},{7,3},{8,4},{9,5},{10,6},{11,7},{12,8},{13,9},{1... | collective-permute-start | bytes 405512 | tf_op jit(solution)/shard_map/ppermute | solution.py:382
  39.1 11.3 %collective-permute-start.7 = (f32[33,8,128]{2,1,0:T(8,128)S(1)}, f32[33,8,128]{2,1,0:T(8,128)S(1)}, u32[]{:S(2)}, u32[]{:S(2)}) collective-permute-start(f32[33,8,128]{2,1,0:T(8,128)S(1)} %get-tuple-element.58), channel_id=1, source_target_pairs={{0,4},{1,5},{2,6},{3,7},{4,8},{5,9},{6,10},{7,11},{8,12},{9,13},{1... | collective-permute-start | bytes 405512 | tf_op jit(solution)/shard_map/ppermute | solution.py:382
  40.6 9.8 %collective-permute-start.8 = (f32[33,8,128]{2,1,0:T(8,128)S(1)}, f32[33,8,128]{2,1,0:T(8,128)S(1)}, u32[]{:S(2)}, u32[]{:S(2)}) collective-permute-start(f32[33,8,128]{2,1,0:T(8,128)S(1)} %get-tuple-element.59), channel_id=1, source_target_pairs={{4,0},{5,1},{6,2},{7,3},{8,4},{9,5},{10,6},{11,7},{12,8},{13,9},{1... | collective-permute-start | bytes 405512 | tf_op jit(solution)/shard_map/ppermute | solution.py:382
  45.2 5.2 %collective-permute-start.16 = (f32[8,128]{1,0:T(8,128)S(1)}, f32[8,128]{1,0:T(8,128)S(1)}, u32[]{:S(2)}, u32[]{:S(2)}) collective-permute-start(f32[8,128]{1,0:T(8,128)S(1)} %get-tuple-element.76), channel_id=1, source_target_pairs={{0,4},{1,5},{2,6},{3,7},{4,8},{5,9},{6,10},{7,11},{8,12},{9,13},{1... | collective-permute-start | bytes 12296 | tf_op jit(solution)/shard_map/ppermute | solution.py:382
  46.6 3.7 %collective-permute-start.17 = (f32[8,128]{1,0:T(8,128)S(1)}, f32[8,128]{1,0:T(8,128)S(1)}, u32[]{:S(2)}, u32[]{:S(2)}) collective-permute-start(f32[8,128]{1,0:T(8,128)S(1)} %get-tuple-element.77), channel_id=1, source_target_pairs={{4,0},{5,1},{6,2},{7,3},{8,4},{9,5},{10,6},{11,7},{12,8},{13,9},{1... | collective-permute-start | bytes 12296 | tf_op jit(solution)/shard_map/ppermute | solution.py:382
  51.3 3.4 %collective-permute-start.18 = (f32[296,128]{1,0:T(8,128)S(1)}, f32[296,128]{1,0:T(8,128)S(1)}, u32[]{:S(2)}, u32[]{:S(2)}) collective-permute-start(f32[296,128]{1,0:T(8,128)S(1)} %get-tuple-element.86), channel_id=1, source_target_pairs={{0,1},{1,0},{2,3},{3,2},{4,5},{5,4},{6,7},{7,6},{8,9},{9,8},{10,11... | collective-permute-start | bytes 454664 | tf_op jit(solution)/shard_map/ppermute | solution.py:374
  53.0 5.5 %collective-permute-start.19 = (f32[296,128]{1,0:T(8,128)S(1)}, f32[296,128]{1,0:T(8,128)S(1)}, u32[]{:S(2)}, u32[]{:S(2)}) collective-permute-start(f32[296,128]{1,0:T(8,128)S(1)} %get-tuple-element.85), channel_id=1, source_target_pairs={{0,2},{1,3},{2,0},{3,1},{4,6},{5,7},{6,4},{7,5},{8,10},{9,11},{10,... | collective-permute-start | bytes 454664 | tf_op jit(solution)/shard_map/ppermute | solution.py:374
  54.2 7.7 %collective-permute-start.20 = (f32[296,128]{1,0:T(8,128)S(1)}, f32[296,128]{1,0:T(8,128)S(1)}, u32[]{:S(2)}, u32[]{:S(2)}) collective-permute-start(f32[296,128]{1,0:T(8,128)S(1)} %get-tuple-element.84), channel_id=1, source_target_pairs={{0,3},{1,2},{2,1},{3,0},{4,7},{5,6},{6,5},{7,4},{8,11},{9,10},{10,... | collective-permute-start | bytes 454664 | tf_op jit(solution)/shard_map/ppermute | solution.py:374

commit v3 on v2

v3 whole, which is shorter than its diff:
```python
import functools

import jax
import jax.numpy as jnp
from jax import lax
from jax.experimental import pallas as pl
from jax.experimental.pallas import tpu as pltpu
from jax.sharding import PartitionSpec as P

spectral_center = 4.5
spectral_half = 4.5

GROUP = 4
SLAB = 2
NEAR = SLAB + 2
LANES = 128
F32 = jnp.float32


def call(body, outs, *args, micros, scratch=(), smem=(), hbm_args=(), hbm_outs=(), smem_outs=()):
    in_specs, operands = [], []
    for n, a in enumerate(args):
        if n in smem:
            in_specs.append(pl.BlockSpec(memory_space=pltpu.SMEM))
        elif n in hbm_args:
            in_specs.append(pl.BlockSpec(memory_space=pltpu.HBM))
            a = pltpu.with_memory_space_constraint(a, pltpu.HBM)
        else:
            in_specs.append(pl.BlockSpec(memory_space=pltpu.VMEM))
            a = pltpu.with_memory_space_constraint(a, pltpu.VMEM)
        operands.append(a)
    out_shape, out_specs = [], []
    for n, shape in enumerate(outs):
        if n in hbm_outs:
            out_shape.append(jax.ShapeDtypeStruct(shape, F32))
            out_specs.append(pl.BlockSpec(memory_space=pltpu.HBM))
        elif n in smem_outs:
            out_shape.append(jax.ShapeDtypeStruct(shape, F32))
            out_specs.append(pl.BlockSpec(memory_space=pltpu.SMEM))
        else:
            out_shape.append(pltpu.VMEM(shape, F32))
            out_specs.append(pl.BlockSpec(memory_space=pltpu.VMEM))
    return pl.pallas_call(
        body,
        out_shape=out_shape,
        in_specs=in_specs,
        out_specs=out_specs,
        scratch_shapes=list(scratch),
        compiler_params=pltpu.CompilerParams(vmem_limit_bytes=16 << 20),
        cost_estimate=pl.CostEstimate(
            flops=int(micros * 1e6), bytes_accessed=int(micros * 3.69e6), transcendentals=0
        ),
    )(*operands)


def lane_iota(shape):
    return lax.broadcasted_iota(jnp.int32, shape, len(shape) - 1)


def prep_kernel(devices, atoms, idx, cheb, energy, cell, atom, value, pot, cot, *refs):
    consts, blocks = refs[0], refs[1:3]
    box, cheb_box, energy_box, value_box, pot_box, sems = refs[3:]
    count, ny = cell.shape[0], pot.shape[0]
    rows = blocks[0].shape[0] - 3 * count - ny
    atom_dev = atoms // devices
    k = lax.rem(idx[0], GROUP)
    moves = [(cell, box.at[0]), (atom, box.at[1]), (cheb, cheb_box), (energy, energy_box)]
    moves += [(value, value_box), (pot, pot_box)]
    for n in range(2):
        first = pl.multiple_of((lax.rem(k, 2) ^ (1 - n)) * rows, rows)
        moves.append((cot.at[pl.ds(first, rows)], blocks[n].at[pl.ds(0, rows)]))
    copies = [
        pltpu.make_async_copy(src, dst, sems.at[n]) for n, (src, dst) in enumerate(moves)
    ]
    for copy in copies[::-1]:
        copy.start()
    for copy in copies[:6]:
        copy.wait()
    up = lax.rem(k, 2) == 1
    first_plane = idx[0] - k + lax.rem(k, 2) * SLAB - 1
    for t in range(NEAR * atom_dev):
        h, r = t // atom_dev, t % atom_dev
        a = (first_plane + jnp.where(up, h, NEAR - 1 - h)) * atom_dev + r
        a = jnp.where(a < 0, a + atoms, jnp.where(a >= atoms, a - atoms, a))
        consts[t : t + 1, :] = jnp.full((1, LANES), energy_box[a] * (1.0 / spectral_half), F32)
    for n in range(4):
        at = NEAR * atom_dev + n
        consts[at : at + 1, :] = jnp.full((1, LANES), cheb_box[n], F32)
    shifted = box[1] + (atoms - (idx[0] - 1) * atom_dev)
    shifted = jnp.where(shifted >= 2 * atoms, shifted - 2 * atoms, shifted)
    slot = jnp.where(shifted >= atoms, shifted - atoms, shifted)
    home = jnp.where(slot >= 2 * atom_dev, 2, jnp.where(slot >= atom_dev, 1, 0))
    slot = jnp.where(k >= 2, slot, slot + (2 - 2 * home) * atom_dev)
    for block in blocks:
        at = rows
        for part in (value_box[...], pot_box[...], box[0].astype(F32), slot.astype(F32)):
            block[at : at + part.shape[0], :] = part
            at += part.shape[0]
    for copy in copies[6:]:
        copy.wait()


def pack_kernel(idx, field, *refs):
    blocks, sems = refs[:2], refs[2]
    rows = blocks[0].shape[0]
    k = lax.rem(idx[0], GROUP)
    copies = []
    for n in range(2):
        first = pl.multiple_of((lax.rem(k, 2) ^ (1 - n)) * rows, rows)
        copies.append(
            pltpu.make_async_copy(field.at[pl.ds(first, rows)], blocks[n], sems.at[n])
        )
    for copy in copies:
        copy.start()
    for copy in copies:
        copy.wait()


def first_place(k):
    return jnp.where((k == 1) | (k == 2), 1, 0)


def fill_dense(ny, slots, block, places, ins, out):
    rows = (ins[0].shape[0] - block - ny) // 3
    rest = block + rows + ny
    half = jnp.bfloat16
    place = lax.broadcasted_iota(jnp.int32, (ny * 8, LANES), 0).astype(F32).astype(half)
    column = lax.broadcasted_iota(jnp.int32, (LANES, LANES), 0).astype(F32).astype(half)
    one, none = jnp.ones((), half), jnp.zeros((), half)
    for p, src in zip(places, ins):
        cell = src[rest : rest + rows, :]
        line = jnp.floor(cell * (1.0 / LANES))
        z = (cell - line * LANES).astype(half)
        code = (line * 8 + src[rest + rows : rest + 2 * rows, :]).astype(half)
        value = src[block : block + rows, :]
        high = value.astype(half)
        low = (value - high.astype(F32)).astype(half)
        left, right = [], []
        for r in range(rows):
            left.append(jnp.where(place == code[r : r + 1, :], one, none))
            hit = column == z[r : r + 1, :]
            right.append(
                jnp.concatenate(
                    [jnp.where(hit, piece[r : r + 1, :], none) for piece in (high, low)], axis=0
                )
            )
        both = lax.dot_general(
            jnp.concatenate(left, axis=1),
            jnp.concatenate(right, axis=1),
            (((1,), (1,)), ((), ())),
            preferred_element_type=F32,
        )
        dense = both[:, :LANES] + both[:, LANES:]
        first = pl.multiple_of(p * ny, ny)
        out[pl.ds(first, ny)] = dense.reshape(ny, 8, LANES)
        pot = (src[block + rows : rest, :] - (spectral_center - 3.0)) * (1.0 / spectral_half)
        out[pl.ds(first, ny), slots : slots + 1, :] = pot.reshape(ny, 1, LANES)


def edge_tiles(tile, atom_dev):
    lane = lane_iota(tile.shape)
    earlier, later = pltpu.roll(tile, atom_dev, 1), pltpu.roll(tile, LANES - atom_dev, 1)
    turned = jnp.where(lax.rem(lane, 2 * atom_dev) < atom_dev, later, earlier)
    inner = jnp.where(lane < 2 * atom_dev, turned, 0.0)
    outer = jnp.where((lane >= 2 * atom_dev) & (lane < 4 * atom_dev), turned, 0.0)
    return inner, outer


def coef_tile(sums, slots, atom_dev):
    shape = sums[0][0].shape
    lane = lane_iota(shape)
    tile = jnp.zeros(shape, F32)
    for t in range(NEAR * atom_dev):
        total = None
        for p in range(SLAB):
            slot = t - p * atom_dev
            if 0 <= slot < slots:
                total = sums[p][slot] if total is None else total + sums[p][slot]
        tile = jnp.where(lane == t, jnp.sum(total, axis=1, keepdims=True), tile)
    return tile


def put_edges(ny, atom_dev, field, tile, inner, outer):
    inner[ny], outer[ny] = edge_tiles(tile, atom_dev)
    inner[0:ny] = field[0:ny]
    outer[0:ny] = field[ny : 2 * ny]


def relay_kernel(ny, orb, atom_dev, first, idx, *refs):
    slots = 3 * atom_dev
    ins, (dense, field, tile_out, inner, outer, sums) = refs[:2], refs[2:]
    place = first_place(lax.rem(idx[0], GROUP))
    places = (place, 1 - place)
    if first:
        fill_dense(ny, slots, orb * ny, places, ins, dense)
    un = 8
    for p, src in zip(places, ins):

        def body(yb, accs, src=src, p=p):
            accs = list(accs)
            for yy in range(un):
                y = yb * un + yy
                v = src[pl.ds(y, orb, stride=ny), :]
                row = p * ny + y
                field[row] = v
                for s in range(slots):
                    accs[s] = accs[s] + v * dense[row, s : s + 1, :]
            return tuple(accs)

        zero = jnp.zeros((orb, LANES), F32)
        accs = lax.fori_loop(0, ny // un, body, (zero,) * slots)
        for s in range(slots):
            sums[p * slots + s] = accs[s]
    parts = [[sums[p * slots + s] for s in range(slots)] for p in range(SLAB)]
    tile = coef_tile(parts, slots, atom_dev)
    tile_out[...] = tile
    put_edges(ny, atom_dev, field, tile, inner, outer)


def step_kernel(kind, ny, atom_dev, *refs):
    slots = 3 * atom_dev
    refs = list(refs)
    zsum = refs.pop()
    take = lambda count: [refs.pop(0) for _ in range(count)]
    consts, dense, field, tile_in, inside, outside = take(6)
    if kind == "b1":
        (other,) = take(1)
    elif kind == "t2":
        other, full_zero, b1, tile_b1, b2, tile_b2, cot, full_cot = take(8)
    elif kind == "out":
        other, cot, gp, e, e_inside, e_outside = take(6)
    if kind in ("b2", "t1"):
        new, tile_out, inner, outer, full_out = refs
    elif kind == "b1":
        new, tile_out, inner, outer = refs
    elif kind == "t2":
        gp, e_out, e_inner, e_outer = refs
    else:
        (new,) = refs
    orb = field.shape[1]
    full = tile_in[...] + inside[ny] + outside[ny]
    if kind in ("b2", "t1"):
        full_out[...] = full
    near = NEAR * atom_dev
    c0, c1, c2, c3 = [consts[near + n : near + n + 1, :] for n in range(4)]
    keep, scale, mix = {
        "t1": (None, 1.0, None),
        "t2": (None, 2.0, -1.0),
        "b2": (c2, 2.0 * c3, None),
        "b1": (None, 2.0, c1 - c3),
        "out": (None, 1.0, -1.0),
    }[kind]
    spread = []
    for t in range(near):
        coupling = consts[t : t + 1, :] * scale
        spread.append(jnp.broadcast_to(full[:, t : t + 1], (orb, LANES)) * coupling)
    side = scale * (-0.5 / spectral_half)
    sums = []
    part = (orb + 1) * ny + 8
    lane, line = (lax.broadcasted_iota(jnp.int32, (2 * LANES, LANES), d) for d in (1, 0))
    apart = (lane - line) % LANES
    turn = jnp.where((apart == 1) | (apart == LANES - 1), 1.0, 0.0).astype(jnp.bfloat16)
    for p in range(SLAB):
        flat = field[p * ny : (p + 1) * ny].reshape(orb * ny, LANES)
        high = flat.astype(jnp.bfloat16)
        low = (flat - high.astype(F32)).astype(jnp.bfloat16)
        zsum[p * ny : (p + 1) * ny] = jnp.dot(
            jnp.concatenate([high, low], axis=1), turn, preferred_element_type=F32
        ).reshape(ny, orb, LANES)
    un = ny
    for p in range(SLAB):

        def body(yb, accs, p=p):
            accs = list(accs)
            rows = []
            first = yb * un
            before = p * ny + jnp.where(first == 0, ny - 1, first - 1)
            after = p * ny + jnp.where(first == ny - un, 0, first + un)
            lines = [field[before]] + [field[p * ny + first + yy] for yy in range(un)]
            lines.append(field[after])
            for yy in range(un):
                y = first + yy
                row = p * ny + y
                earlier, v, later = lines[yy : yy + 3]
                beyond = (outside if p else inside)[y] + field[(1 - p) * ny + y]
                beside = (later + earlier) + (beyond + zsum[row])
                pot = dense[row, slots : slots + 1, :] * scale
                if keep is not None:
                    pot = pot + keep
                weights = [dense[row, s : s + 1, :] for s in range(slots)]
                a = [spread[p * atom_dev + s] * weights[s] for s in range(slots)]
                while len(a) > 1:
                    a = [sum(a[n + 1 : n + 2], a[n]) for n in range(0, len(a), 2)]
                x = v * pot + beside * side + a[0]
                if mix is not None:
                    x = x + other[row] * mix
                if kind == "out":
                    x = x + cot[row] * c0
                    new[pl.ds(p * part + y, orb, stride=ny), :] = x
                elif kind == "t2":
                    g = b1[row] * other[row] + 2.0 * (b2[row] * v)
                    g = g + (2.0 * c3) * (cot[row] * x)
                    rows.append(jnp.sum(g, axis=0, keepdims=True))
                else:
                    new[row] = x
                if kind != "out":
                    for s in range(slots):
                        accs[s] = accs[s] + x * weights[s]
            if kind == "t2":
                start = pl.multiple_of(p * ny + yb * un, un)
                gp[pl.ds(start, un), :] = jnp.concatenate(rows, axis=0) * (1.0 / spectral_half)
            return tuple(accs)

        zero = jnp.zeros((orb, LANES), F32)
        init = () if kind == "out" else (zero,) * slots
        sums.append(lax.fori_loop(0, ny // un, body, init))
    if kind == "out":
        total = e[...] + e_inside[...] + e_outside[...]
        for p in range(SLAB):
            rest = p * part + orb * ny
            new[rest : rest + ny, :] = gp[p * ny : (p + 1) * ny, :]
            new[rest + ny : rest + ny + 8, :] = pltpu.roll(total, LANES - (p + 1) * atom_dev, 1)
        return
    tile = coef_tile(sums, slots, atom_dev)
    if kind == "t2":
        e = tile_b1[...] * full_zero[...] + 2.0 * (tile_b2[...] * full)
        e = e + (2.0 * c3) * (full_cot[...] * tile)
        e = jnp.sum(e, axis=0, keepdims=True) * (1.0 / spectral_half)
        e = jnp.broadcast_to(e, (8, LANES))
        e_out[...] = e
        lane = lane_iota(e.shape)
        mine = (lane >= atom_dev) & (lane < 2 * atom_dev)
        e_inner[...] = jnp.where(mine, pltpu.roll(e, atom_dev, 1), 0.0)
        mine = (lane >= 2 * atom_dev) & (lane < 3 * atom_dev)
        e_outer[...] = jnp.where(mine, pltpu.roll(e, LANES - atom_dev, 1), 0.0)
        return
    tile_out[...] = tile
    put_edges(ny, atom_dev, new, tile, inner, outer)


def final_kernel(ny, orb, atom_dev, idx, *refs):
    blocks, (out, gp_out, e_out, gp, sems) = refs[:2], refs[2:]
    k = lax.rem(idx[0], GROUP)
    rows = orb * ny
    copies = []
    for n in range(2):
        first = pl.multiple_of((lax.rem(k, 2) ^ (1 - n)) * rows, rows)
        copies.append(
            pltpu.make_async_copy(
                blocks[n].at[pl.ds(0, rows)], out.at[pl.ds(first, rows)], sems.at[n]
            )
        )
    for copy in copies:
        copy.start()
    total = blocks[0][rows:, :] + blocks[1][rows:, :]
    gp[...] = total[0:ny]
    last = pltpu.make_async_copy(gp, gp_out, sems.at[2])
    last.start()
    e = total[ny : ny + 1]
    lane = lane_iota(e.shape)
    for n in range(atom_dev):
        e_out[n] = jnp.sum(jnp.where(lane == n, e, 0.0))
    for copy in copies + [last]:
        copy.wait()


def per_device(orbitals, cotangent, potential, cheb_coef, energy, proj_cell, proj_atom, proj_value):
    orb_all, _, ny, nz = orbitals.shape
    devices = lax.axis_size("grid")
    groups = devices // GROUP
    atoms = energy.shape[0]
    atom_dev = atoms // devices
    points = proj_cell.shape[0] // LANES
    orb = orb_all // 2
    assert orb % 8 == 0 and nz == LANES and devices % GROUP == 0
    idx = lax.axis_index("grid").astype(jnp.int32).reshape(1)
    block = orb * ny
    plane = SLAB * ny

    def pairs(within):
        return [(GROUP * g + a, GROUP * g + b) for g in range(groups) for a, b in within]

    enter = [(0, 2), (1, 0), (2, 3), (3, 1)]
    leave = [(b, a) for a, b in enter]
    swap = [(0, 0), (1, 2), (2, 1), (3, 3)]
    core = pairs([(0, 1), (1, 0), (2, 3), (3, 2)])
    across = []
    for g in range(groups):
        for m in range(2):
            below, above = GROUP * g + 2 * m + 1, GROUP * ((g + 1) % groups) + 2 * m
            across += [(below, above), (above, below)]

    def permute(x, to):
        return lax.ppermute(x, "grid", to)

    def halo(inner, outer):
        beyond = permute(outer, across)
        return permute(inner, core), beyond

    def exchange(blocks, first):
        return [permute(blocks[0], pairs(first)), permute(blocks[1], pairs(swap))]

    consts, *blocks = call(
        functools.partial(prep_kernel, devices, atoms),
        [(-(-(NEAR * atom_dev + 4) // 8) * 8, LANES)] + [(block + 3 * points + ny, LANES)] * 2,
        idx,
        cheb_coef,
        energy,
        proj_cell.reshape(points, LANES),
        proj_atom.reshape(points, LANES),
        proj_value.reshape(points, LANES),
        potential.reshape(ny, LANES),
        cotangent.reshape(orb_all * ny, LANES),
        micros=1.2,
        scratch=[
            pltpu.VMEM((2, points, LANES), jnp.int32),
            pltpu.SMEM(cheb_coef.shape, F32),
            pltpu.SMEM(energy.shape, F32),
            pltpu.VMEM((points, LANES), F32),
            pltpu.VMEM((ny, LANES), F32),
            pltpu.SemaphoreType.DMA((8,)),
        ],
        smem=(0,),
        hbm_args=range(1, 8),
    )
    cot_blocks = exchange(blocks, enter)
    blocks = call(
        pack_kernel,
        [(block, LANES)] * 2,
        idx,
        orbitals.reshape(orb_all * ny, LANES),
        micros=1.0,
        scratch=[pltpu.SemaphoreType.DMA((2,))],
        smem=(0,),
        hbm_args=(1,),
    )
    orb_blocks = exchange(blocks, enter)
    field_shape, tile_shape = (plane, orb, LANES), (orb, LANES)
    edge_shape, sums_shape = (ny + 1, orb, LANES), (8, LANES)
    chain = [field_shape, tile_shape, edge_shape, edge_shape]

    def relay(first, blocks, *args):
        return call(
            functools.partial(relay_kernel, ny, orb, atom_dev, first),
            ([(plane, 8, LANES)] if first else []) + chain,
            idx,
            *blocks,
            *args,
            micros=1.4 if first else 0.7,
            scratch=[pltpu.VMEM((SLAB * 3 * atom_dev, orb, LANES), F32)],
            smem=(0,),
        )

    def step(kind, outs, *args):
        return call(
            functools.partial(step_kernel, kind, ny, atom_dev),
            outs,
            consts,
            dense,
            *args,
            micros=1.0,
            scratch=[pltpu.VMEM(field_shape, F32)],
        )

    dense, cot, tile_cot, *edges = relay(True, cot_blocks)
    inner, outer = edges
    cot_halo = halo(inner, outer)
    cot_halo = (
        cot_halo[0],
        jnp.concatenate([permute(outer[:ny], across), permute(outer[ny:], across)]),
    )
    zero, tile_zero, *edges = relay(False, orb_blocks, dense)
    zero_halo = halo(*edges)
    b2, tile_b2, *edges, full_cot = step("b2", chain + [tile_shape], cot, tile_cot, *cot_halo)
    b2_halo = halo(*edges)
    t1, tile_t1, *edges, full_zero = step("t1", chain + [tile_shape], zero, tile_zero, *zero_halo)
    t1_halo = halo(*edges)
    b1, tile_b1, *edges = step("b1", chain, b2, tile_b2, *b2_halo, cot)
    b1_halo = halo(*edges)
    gp, e, *edges = step(
        "t2",
        [(plane, LANES)] + [sums_shape] * 3,
        t1,
        tile_t1,
        *t1_halo,
        zero,
        full_zero,
        b1,
        tile_b1,
        b2,
        tile_b2,
        cot,
        full_cot,
    )
    part = block + ny + 8
    (image,) = step(
        "out", [(SLAB * part, LANES)], b1, tile_b1, *b1_halo, b2, cot, gp, e, *halo(*edges)
    )
    place = first_place(lax.rem(idx[0], GROUP))
    images = exchange(
        [
            lax.dynamic_slice_in_dim(image, place * part, part, 0),
            lax.dynamic_slice_in_dim(image, (1 - place) * part, part, 0),
        ],
        leave,
    )
    out, gp, e = call(
        functools.partial(final_kernel, ny, orb, atom_dev),
        [(orb_all * ny, LANES), (ny, LANES), (atom_dev,)],
        idx,
        *images,
        micros=1.0,
        scratch=[pltpu.VMEM((ny, LANES), F32), pltpu.SemaphoreType.DMA((3,))],
        smem=(0,),
        hbm_outs=(0, 1),
        smem_outs=(2,),
    )
    return out.reshape(orbitals.shape), gp.reshape(potential.shape), e


def solution(mesh):
    placed = (
        P("sample", "grid", None, None),
        P("sample", "grid", None, None),
        P("grid", None, None),
        P(),
        P(),
        P("grid"),
        P("grid"),
        P("grid"),
    )
    return jax.shard_map(
        per_device,
        mesh=mesh,
        in_specs=placed,
        out_specs=(
            P("sample", "grid", None, None),
            P(("sample", "grid"), None, None),
            P(("sample", "grid")),
        ),
        check_vma=False,
    )
```

time: 63.6 us -> 59.5 us (0.936)
  waiting for transfers between devices: 22.1 us -> 20.3 us
  starting transfers between devices: 28.8 us -> 27.9 us
  Pallas kernels: 11 us -> 10.2 us
    ppermute x21 -> x19, waiting for transfers between devices: 22.1 us -> 20.3 us  [permute(): return lax.ppermute(x, 'grid', to)]
    ppermute x21 -> x19, starting transfers between devices: 28.8 us -> 27.9 us  [permute(): return lax.ppermute(x, 'grid', to)]
    pallas_call x9 -> x10, Pallas kernels: 11 us -> 10.2 us  [call(): pl.pallas_call(body, out_shape=out_shape, in_specs=in_specs, out_specs=ou...]
    unnamed x4 -> x0, local copies, waits for them, and re-layouts: 0.66 us -> none
  transfers between devices with their start and end apart: 21 -> 19, of which waited for: 9 -> 10; matrix products, arithmetic and copies ran while one was open for 0% -> 0% of each run, Pallas kernels for 11% -> 12%
where the time goes in v3:
time: 59.5 us; the launch traced here: 59.3 us
  starting transfers between devices  27.9 us (47%)
  waiting for transfers between devices  20.3 us (34%)
  Pallas kernels  10.2 us (17%)
  between operations  0.74 us (1%)
    ppermute x19, starting transfers between devices, permute(): return lax.ppermute(x, 'grid', to)  27.9 us
    ppermute x19, waiting for transfers between devices, permute(): return lax.ppermute(x, 'grid', to)  20.3 us
    pallas_call x10, Pallas kernels, call(): pl.pallas_call(body, out_shape=out_shape, in_specs=in_specs, out_specs=ou...  10.2 us
  transfers between devices with their start and end apart: 19, of which 10 were waited for; matrix products, arithmetic and copies ran while one was open for 0% of the time, Pallas kernels for 12%

profile of v3, /device:TPU:1, one launch (start us, length us, event | category | flops | bytes accessed | tf_op | source)
XLA Modules:
  0.0 59.3 jit_solution(10131946590348977871)
XLA Ops:
  0.6 1.1 %shard_map.103 = (f32[16,128]{1,0:T(8,128)S(1)}, f32[592,128]{1,0:T(8,128)S(1)}, f32[592,128]{1,0:T(8,128)S(1)}) custom-call(s32[1]{0:T(128)} %bitcast.idx, f32[4]{0:T(128)} %cheb.1, f32[32]{0:T(128)} %energy.1, s32[16,128]{1,0:T(8,128)} %bitcast.14, s32[16,128]{1,0:T(8,128)} %bitcast.15, f32[16,128]{1,0:T(8,128)} %bitcast.16, f32[32,128]{1,0:T(8,128)} %bitcast.13, ...), custom_call_target="tpu_custom_call" | custom-call | flops 1200000 | bytes 4428000 | tf_op jit(solution)/shard_map/pallas_call | solution.py:43
  1.8 4.5 %collective-permute-start.1 = (f32[592,128]{1,0:T(8,128)S(1)}, f32[592,128]{1,0:T(8,128)S(1)}, u32[]{:S(2)}, u32[]{:S(2)}) collective-permute-start(f32[592,128]{1,0:T(8,128)S(1)} %get-tuple-element.40), channel_id=1, source_target_pairs={{0,0},{1,2},{2,1},{3,3},{4,4},{5,6},{6,5},{7,7},{8,8},{9,10},{10,9... | collective-permute-start | bytes 909320 | tf_op jit(solution)/shard_map/ppermute | solution.py:394
  6.3 1.1 %shard_map.107 = (f32[512,128]{1,0:T(8,128)S(1)}, f32[512,128]{1,0:T(8,128)S(1)}) custom-call(s32[1]{0:T(128)} %bitcast.idx, f32[1024,128]{1,0:T(8,128)} %bitcast.12), custom_call_target="tpu_custom_call" | custom-call | flops 1000000 | bytes 3690000 | tf_op jit(solution)/shard_map/pallas_call | solution.py:43
  7.4 1.9 %collective-permute-start.10 = (f32[512,128]{1,0:T(8,128)S(1)}, f32[512,128]{1,0:T(8,128)S(1)}, u32[]{:S(2)}, u32[]{:S(2)}) collective-permute-start(f32[512,128]{1,0:T(8,128)S(1)} %get-tuple-element.55), channel_id=1, source_target_pairs={{0,0},{1,2},{2,1},{3,3},{4,4},{5,6},{6,5},{7,7},{8,8},{9,10},{10,9... | collective-permute-start | bytes 786440 | tf_op jit(solution)/shard_map/ppermute | solution.py:394
  9.3 2.6 %collective-permute-done.1.refs_1_ = f32[592,128]{1,0:T(8,128)S(1)} collective-permute-done((f32[592,128]{1,0:T(8,128)S(1)}, f32[592,128]{1,0:T(8,128)S(1)}, u32[]{:S(2)}, u32[]{:S(2)}) %collective-permute-start.1) | collective-permute-done | bytes 303136 | tf_op jit(solution)/shard_map/ppermute | solution.py:394
  11.9 1.4 %shard_map.104 = (f32[64,8,128]{2,1,0:T(8,128)S(1)}, f32[64,16,128]{2,1,0:T(8,128)S(1)}, f32[16,128]{1,0:T(8,128)S(1)}, f32[33,16,128]{2,1,0:T(8,128)S(1)}, f32[33,16,128]{2,1,0:T(8,128)S(1)}) custom-call(s32[1]{0:T(128)} %bitcast.idx, f32[592,128]{1,0:T(8,128)S(1)} %collective-permute-done.refs_0_, f32[592,128]{1,0:T(8,128)S(1)} %collective-permute-done.1.refs_1_), custom_call_target="tpu_custom_call" | custom-call | flops 1400000 | bytes 5166000 | tf_op jit(solution)/shard_map/pallas_call | solution.py:43
  13.3 0.7 %collective-permute-start.3 = (f32[32,16,128]{2,1,0:T(8,128)S(1)}, f32[32,16,128]{2,1,0:T(8,128)S(1)}, u32[]{:S(2)}, u32[]{:S(2)}) collective-permute-start(f32[32,16,128]{2,1,0:T(8,128)S(1)} %slice.6), channel_id=1, source_target_pairs={{1,4},{4,1},{3,6},{6,3},{5,8},{8,5},{7,10},{10,7},{9,12},{12,9},{1... | collective-permute-start | bytes 786440 | tf_op jit(solution)/shard_map/ppermute | solution.py:394
  14.1 3.0 %collective-permute-start.2 = (f32[33,16,128]{2,1,0:T(8,128)S(1)}, f32[33,16,128]{2,1,0:T(8,128)S(1)}, u32[]{:S(2)}, u32[]{:S(2)}) collective-permute-start(f32[33,16,128]{2,1,0:T(8,128)S(1)} %get-tuple-element.44), channel_id=1, source_target_pairs={{0,1},{1,0},{2,3},{3,2},{4,5},{5,4},{6,7},{7,6},{8,9},{9,8},{10,11... | collective-permute-start | bytes 811016 | tf_op jit(solution)/shard_map/ppermute | solution.py:394
  17.3 0.6 %shard_map.108 = (f32[64,16,128]{2,1,0:T(8,128)S(1)}, f32[16,128]{1,0:T(8,128)S(1)}, f32[33,16,128]{2,1,0:T(8,128)S(1)}, f32[33,16,128]{2,1,0:T(8,128)S(1)}) custom-call(s32[1]{0:T(128)} %bitcast.idx, f32[512,128]{1,0:T(8,128)S(1)} %collective-permute-done.9.refs_0_, f32[512,128]{1,0:T(8,128)S(1)} %collective-permute-done.10.refs_1_, ...), custom_call_target="tpu_custom_call" | custom-call | flops 700000 | bytes 2583000 | tf_op jit(solution)/shard_map/pallas_call | solution.py:43
  18.0 0.6 %collective-permute-start.11 = (f32[33,16,128]{2,1,0:T(8,128)S(1)}, f32[33,16,128]{2,1,0:T(8,128)S(1)}, u32[]{:S(2)}, u32[]{:S(2)}) collective-permute-start(f32[33,16,128]{2,1,0:T(8,128)S(1)} %get-tuple-element.58), channel_id=1, source_target_pairs={{0,1},{1,0},{2,3},{3,2},{4,5},{5,4},{6,7},{7,6},{8,9},{9,8},{10,11... | collective-permute-start | bytes 811016 | tf_op jit(solution)/shard_map/ppermute | solution.py:394
  18.6 1.9 %collective-permute-start.12 = (f32[33,16,128]{2,1,0:T(8,128)S(1)}, f32[33,16,128]{2,1,0:T(8,128)S(1)}, u32[]{:S(2)}, u32[]{:S(2)}) collective-permute-start(f32[33,16,128]{2,1,0:T(8,128)S(1)} %get-tuple-element.59), channel_id=1, source_target_pairs={{1,4},{4,1},{3,6},{6,3},{5,8},{8,5},{7,10},{10,7},{9,12},{12,9},{1... | collective-permute-start | bytes 811016 | tf_op jit(solution)/shard_map/ppermute | solution.py:394
  20.5 1.4 %collective-permute-done.4 = f32[1,16,128]{2,1,0:T(8,128)S(1)} collective-permute-done((f32[1,16,128]{2,1,0:T(8,128)S(1)}, f32[1,16,128]{2,1,0:T(8,128)S(1)}, u32[]{:S(2)}, u32[]{:S(2)}) %collective-permute-start.4) | collective-permute-done | bytes 8224 | tf_op jit(solution)/shard_map/ppermute | solution.py:394
  21.9 0.9 %shard_map.105 = (f32[64,16,128]{2,1,0:T(8,128)S(1)}, f32[16,128]{1,0:T(8,128)S(1)}, f32[33,16,128]{2,1,0:T(8,128)S(1)}, f32[33,16,128]{2,1,0:T(8,128)S(1)}, f32[16,128]{1,0:T(8,128)S(1)}) custom-call(f32[16,128]{1,0:T(8,128)S(1)} %get-tuple-element.38.refs_0_, f32[64,8,128]{2,1,0:T(8,128)S(1)} %get-tuple-element.41.refs_1_.refs_2_, ...), custom_call_target="tpu_custom_call" | custom-call | flops 1000000 | bytes 3690000 | tf_op jit(solution)/shard_map/pallas_call | solution.py:43
  22.9 1.6 %collective-permute-start.5 = (f32[33,16,128]{2,1,0:T(8,128)S(1)}, f32[33,16,128]{2,1,0:T(8,128)S(1)}, u32[]{:S(2)}, u32[]{:S(2)}) collective-permute-start(f32[33,16,128]{2,1,0:T(8,128)S(1)} %get-tuple-element.48), channel_id=1, source_target_pairs={{0,1},{1,0},{2,3},{3,2},{4,5},{5,4},{6,7},{7,6},{8,9},{9,8},{10,11... | collective-permute-start | bytes 811016 | tf_op jit(solution)/shard_map/ppermute | solution.py:394
  24.5 0.7 %collective-permute-start.6 = (f32[33,16,128]{2,1,0:T(8,128)S(1)}, f32[33,16,128]{2,1,0:T(8,128)S(1)}, u32[]{:S(2)}, u32[]{:S(2)}) collective-permute-start(f32[33,16,128]{2,1,0:T(8,128)S(1)} %get-tuple-element.49), channel_id=1, source_target_pairs={{1,4},{4,1},{3,6},{6,3},{5,8},{8,5},{7,10},{10,7},{9,12},{12,9},{1... | collective-permute-start | bytes 811016 | tf_op jit(solution)/shard_map/ppermute | solution.py:394
  25.2 2.3 %collective-permute-done.12.refs_5_ = f32[33,16,128]{2,1,0:T(8,128)S(1)} collective-permute-done((f32[33,16,128]{2,1,0:T(8,128)S(1)}, f32[33,16,128]{2,1,0:T(8,128)S(1)}, u32[]{:S(2)}, u32[]{:S(2)}) %collective-permute-start.12) | collective-permute-done | bytes 270368 | tf_op jit(solution)/shard_map/ppermute | solution.py:394
  27.5 0.9 %shard_map.109 = (f32[64,16,128]{2,1,0:T(8,128)S(1)}, f32[16,128]{1,0:T(8,128)S(1)}, f32[33,16,128]{2,1,0:T(8,128)S(1)}, f32[33,16,128]{2,1,0:T(8,128)S(1)}, f32[16,128]{1,0:T(8,128)S(1)}) custom-call(f32[16,128]{1,0:T(8,128)S(1)} %get-tuple-element.38.refs_0_, f32[64,8,128]{2,1,0:T(8,128)S(1)} %get-tuple-element.41.refs_1_.refs_2_, ...), custom_call_target="tpu_custom_call" | custom-call | flops 1000000 | bytes 3690000 | tf_op jit(solution)/shard_map/pallas_call | solution.py:43
  28.4 2.1 %collective-permute-start.13 = (f32[33,16,128]{2,1,0:T(8,128)S(1)}, f32[33,16,128]{2,1,0:T(8,128)S(1)}, u32[]{:S(2)}, u32[]{:S(2)}) collective-permute-start(f32[33,16,128]{2,1,0:T(8,128)S(1)} %get-tuple-element.62), channel_id=1, source_target_pairs={{0,1},{1,0},{2,3},{3,2},{4,5},{5,4},{6,7},{7,6},{8,9},{9,8},{10,11... | collective-permute-start | bytes 811016 | tf_op jit(solution)/shard_map/ppermute | solution.py:394
  30.5 0.5 collective-permute-start.14
  31.0 2.6 %collective-permute-done.6.refs_5_ = f32[33,16,128]{2,1,0:T(8,128)S(1)} collective-permute-done((f32[33,16,128]{2,1,0:T(8,128)S(1)}, f32[33,16,128]{2,1,0:T(8,128)S(1)}, u32[]{:S(2)}, u32[]{:S(2)}) %collective-permute-start.6) | collective-permute-done | bytes 270368 | tf_op jit(solution)/shard_map/ppermute | solution.py:394
  33.5 0.9 %shard_map.106 = (f32[64,16,128]{2,1,0:T(8,128)S(1)}, f32[16,128]{1,0:T(8,128)S(1)}, f32[33,16,128]{2,1,0:T(8,128)S(1)}, f32[33,16,128]{2,1,0:T(8,128)S(1)}) custom-call(f32[16,128]{1,0:T(8,128)S(1)} %get-tuple-element.38.refs_0_, f32[64,8,128]{2,1,0:T(8,128)S(1)} %get-tuple-element.41.refs_1_.refs_2_, ...), custom_call_target="tpu_custom_call" | custom-call | flops 1000000 | bytes 3690000 | tf_op jit(solution)/shard_map/pallas_call | solution.py:43
  34.5 1.9 %collective-permute-start.7 = (f32[33,16,128]{2,1,0:T(8,128)S(1)}, f32[33,16,128]{2,1,0:T(8,128)S(1)}, u32[]{:S(2)}, u32[]{:S(2)}) collective-permute-start(f32[33,16,128]{2,1,0:T(8,128)S(1)} %get-tuple-element.52), channel_id=1, source_target_pairs={{0,1},{1,0},{2,3},{3,2},{4,5},{5,4},{6,7},{7,6},{8,9},{9,8},{10,11... | collective-permute-start | bytes 811016 | tf_op jit(solution)/shard_map/ppermute | solution.py:394
  36.3 0.5 collective-permute-start.8
  36.8 2.8 %collective-permute-done.14.refs_5_ = f32[33,16,128]{2,1,0:T(8,128)S(1)} collective-permute-done((f32[33,16,128]{2,1,0:T(8,128)S(1)}, f32[33,16,128]{2,1,0:T(8,128)S(1)}, u32[]{:S(2)}, u32[]{:S(2)}) %collective-permute-start.14) | collective-permute-done | bytes 270368 | tf_op jit(solution)/shard_map/ppermute | solution.py:394
  39.6 1.2 %shard_map.110 = (f32[64,128]{1,0:T(8,128)S(1)}, f32[8,128]{1,0:T(8,128)S(1)}, f32[8,128]{1,0:T(8,128)S(1)}, f32[8,128]{1,0:T(8,128)S(1)}) custom-call(f32[16,128]{1,0:T(8,128)S(1)} %get-tuple-element.38.refs_0_, f32[64,8,128]{2,1,0:T(8,128)S(1)} %get-tuple-element.41.refs_1_.refs_2_, f32[64,16,128]{2,1,0:T(8,128)S(1)} %get-tuple-element.60.refs_2_, ...), custom_call_target="tpu_custom_call" | custom-call | flops 1000000 | bytes 3690000 | tf_op jit(solution)/shard_map/pallas_call | solution.py:43
  40.7 1.6 %collective-permute-start.15 = (f32[8,128]{1,0:T(8,128)S(1)}, f32[8,128]{1,0:T(8,128)S(1)}, u32[]{:S(2)}, u32[]{:S(2)}) collective-permute-start(f32[8,128]{1,0:T(8,128)S(1)} %get-tuple-element.68), channel_id=1, source_target_pairs={{0,1},{1,0},{2,3},{3,2},{4,5},{5,4},{6,7},{7,6},{8,9},{9,8},{10,11... | collective-permute-start | bytes 12296 | tf_op jit(solution)/shard_map/ppermute | solution.py:394
  43.2 2.5 %collective-permute-done.16.refs_11_ = f32[8,128]{1,0:T(8,128)S(1)} collective-permute-done((f32[8,128]{1,0:T(8,128)S(1)}, f32[8,128]{1,0:T(8,128)S(1)}, u32[]{:S(2)}, u32[]{:S(2)}) %collective-permute-start.16) | collective-permute-done | bytes 4128 | tf_op jit(solution)/shard_map/ppermute | solution.py:394
  45.7 0.8 %shard_map.111 = f32[1104,128]{1,0:T(8,128)S(1)} custom-call(f32[16,128]{1,0:T(8,128)S(1)} %get-tuple-element.38.refs_0_, f32[64,8,128]{2,1,0:T(8,128)S(1)} %get-tuple-element.41.refs_1_.refs_2_, f32[64,16,128]{2,1,0:T(8,128)S(1)} %get-tuple-element.50.refs_8_.refs_2_, f32[16,128]{1,0:T(8,128)S(1)} %get-tuple-element.51.refs_9_.refs_3_, ...), custom_call_target="tpu_custom_call" | custom-call | flops 1000000 | bytes 3690000 | tf_op jit(solution)/shard_map/pallas_call | solution.py:43
  46.6 2.6 %collective-permute-start.17 = (f32[552,128]{1,0:T(8,128)S(1)}, f32[552,128]{1,0:T(8,128)S(1)}, u32[]{:S(2)}, u32[]{:S(2)}) collective-permute-start(f32[552,128]{1,0:T(8,128)S(1)} %get-tuple-element.77), channel_id=1, source_target_pairs={{2,0},{0,1},{3,2},{1,3},{6,4},{4,5},{7,6},{5,7},{10,8},{8,9},{11,1... | collective-permute-start | bytes 847880 | tf_op jit(solution)/shard_map/ppermute | solution.py:394
  49.2 3.4 %collective-permute-start.18 = (f32[552,128]{1,0:T(8,128)S(1)}, f32[552,128]{1,0:T(8,128)S(1)}, u32[]{:S(2)}, u32[]{:S(2)}) collective-permute-start(f32[552,128]{1,0:T(8,128)S(1)} %get-tuple-element.76), channel_id=1, source_target_pairs={{0,0},{1,2},{2,1},{3,3},{4,4},{5,6},{6,5},{7,7},{8,8},{9,10},{10,9... | collective-permute-start | bytes 847880 | tf_op jit(solution)/shard_map/ppermute | solution.py:394
  52.7 5.2 %collective-permute-done.18.refs_1_ = f32[552,128]{1,0:T(8,128)S(1)} collective-permute-done((f32[552,128]{1,0:T(8,128)S(1)}, f32[552,128]{1,0:T(8,128)S(1)}, u32[]{:S(2)}, u32[]{:S(2)}) %collective-permute-start.18) | collective-permute-done | bytes 282656 | tf_op jit(solution)/shard_map/ppermute | solution.py:394
  58.0 1.3 %shard_map.112 = (f32[1024,128]{1,0:T(8,128)}, f32[32,128]{1,0:T(8,128)}, f32[2]{0:T(128)}) custom-call(s32[1]{0:T(128)} %bitcast.idx, f32[552,128]{1,0:T(8,128)S(1)} %collective-permute-done.17.refs_0_, f32[552,128]{1,0:T(8,128)S(1)} %collective-permute-done.18.refs_1_), custom_call_target="tpu_custom_call" | custom-call | flops 1000000 | bytes 3690000 | tf_op jit(solution)/shard_map/pallas_call | solution.py:43
  (20 shorter events, 1.4 us)
Async XLA Ops:
  1.8 7.6 %collective-permute-start = (f32[592,128]{1,0:T(8,128)S(1)}, f32[592,128]{1,0:T(8,128)S(1)}, u32[]{:S(2)}, u32[]{:S(2)}) collective-permute-start(f32[592,128]{1,0:T(8,128)S(1)} %get-tuple-element.39), channel_id=1, source_target_pairs={{0,2},{1,0},{2,3},{3,1},{4,6},{5,4},{6,7},{7,5},{8,10},{9,8},{10,1... | collective-permute-start | bytes 909320 | tf_op jit(solution)/shard_map/ppermute | solution.py:394
  1.8 10.1 %collective-permute-start.1 = (f32[592,128]{1,0:T(8,128)S(1)}, f32[592,128]{1,0:T(8,128)S(1)}, u32[]{:S(2)}, u32[]{:S(2)}) collective-permute-start(f32[592,128]{1,0:T(8,128)S(1)} %get-tuple-element.40), channel_id=1, source_target_pairs={{0,0},{1,2},{2,1},{3,3},{4,4},{5,6},{6,5},{7,7},{8,8},{9,10},{10,9... | collective-permute-start | bytes 909320 | tf_op jit(solution)/shard_map/ppermute | solution.py:394
  7.4 10.0 %collective-permute-start.10 = (f32[512,128]{1,0:T(8,128)S(1)}, f32[512,128]{1,0:T(8,128)S(1)}, u32[]{:S(2)}, u32[]{:S(2)}) collective-permute-start(f32[512,128]{1,0:T(8,128)S(1)} %get-tuple-element.55), channel_id=1, source_target_pairs={{0,0},{1,2},{2,1},{3,3},{4,4},{5,6},{6,5},{7,7},{8,8},{9,10},{10,9... | collective-permute-start | bytes 786440 | tf_op jit(solution)/shard_map/ppermute | solution.py:394
  9.3 8.0 %collective-permute-start.9 = (f32[512,128]{1,0:T(8,128)S(1)}, f32[512,128]{1,0:T(8,128)S(1)}, u32[]{:S(2)}, u32[]{:S(2)}) collective-permute-start(f32[512,128]{1,0:T(8,128)S(1)} %get-tuple-element.54), channel_id=1, source_target_pairs={{0,2},{1,0},{2,3},{3,1},{4,6},{5,4},{6,7},{7,5},{8,10},{9,8},{10,1... | collective-permute-start | bytes 786440 | tf_op jit(solution)/shard_map/ppermute | solution.py:394
  13.3 8.6 %collective-permute-start.3 = (f32[32,16,128]{2,1,0:T(8,128)S(1)}, f32[32,16,128]{2,1,0:T(8,128)S(1)}, u32[]{:S(2)}, u32[]{:S(2)}) collective-permute-start(f32[32,16,128]{2,1,0:T(8,128)S(1)} %slice.6), channel_id=1, source_target_pairs={{1,4},{4,1},{3,6},{6,3},{5,8},{8,5},{7,10},{10,7},{9,12},{12,9},{1... | collective-permute-start | bytes 786440 | tf_op jit(solution)/shard_map/ppermute | solution.py:394
  14.1 7.9 %collective-permute-start.2 = (f32[33,16,128]{2,1,0:T(8,128)S(1)}, f32[33,16,128]{2,1,0:T(8,128)S(1)}, u32[]{:S(2)}, u32[]{:S(2)}) collective-permute-start(f32[33,16,128]{2,1,0:T(8,128)S(1)} %get-tuple-element.44), channel_id=1, source_target_pairs={{0,1},{1,0},{2,3},{3,2},{4,5},{5,4},{6,7},{7,6},{8,9},{9,8},{10,11... | collective-permute-start | bytes 811016 | tf_op jit(solution)/shard_map/ppermute | solution.py:394
  17.1 4.8 %collective-permute-start.4 = (f32[1,16,128]{2,1,0:T(8,128)S(1)}, f32[1,16,128]{2,1,0:T(8,128)S(1)}, u32[]{:S(2)}, u32[]{:S(2)}) collective-permute-start(f32[1,16,128]{2,1,0:T(8,128)S(1)} %slice.7), channel_id=1, source_target_pairs={{1,4},{4,1},{3,6},{6,3},{5,8},{8,5},{7,10},{10,7},{9,12},{12,9},{1... | collective-permute-start | bytes 24584 | tf_op jit(solution)/shard_map/ppermute | solution.py:394
  18.0 7.2 %collective-permute-start.11 = (f32[33,16,128]{2,1,0:T(8,128)S(1)}, f32[33,16,128]{2,1,0:T(8,128)S(1)}, u32[]{:S(2)}, u32[]{:S(2)}) collective-permute-start(f32[33,16,128]{2,1,0:T(8,128)S(1)} %get-tuple-element.58), channel_id=1, source_target_pairs={{0,1},{1,0},{2,3},{3,2},{4,5},{5,4},{6,7},{7,6},{8,9},{9,8},{10,11... | collective-permute-start | bytes 811016 | tf_op jit(solution)/shard_map/ppermute | solution.py:394
  18.6 8.9 %collective-permute-start.12 = (f32[33,16,128]{2,1,0:T(8,128)S(1)}, f32[33,16,128]{2,1,0:T(8,128)S(1)}, u32[]{:S(2)}, u32[]{:S(2)}) collective-permute-start(f32[33,16,128]{2,1,0:T(8,128)S(1)} %get-tuple-element.59), channel_id=1, source_target_pairs={{1,4},{4,1},{3,6},{6,3},{5,8},{8,5},{7,10},{10,7},{9,12},{12,9},{1... | collective-permute-start | bytes 811016 | tf_op jit(solution)/shard_map/ppermute | solution.py:394
  22.9 8.1 %collective-permute-start.5 = (f32[33,16,128]{2,1,0:T(8,128)S(1)}, f32[33,16,128]{2,1,0:T(8,128)S(1)}, u32[]{:S(2)}, u32[]{:S(2)}) collective-permute-start(f32[33,16,128]{2,1,0:T(8,128)S(1)} %get-tuple-element.48), channel_id=1, source_target_pairs={{0,1},{1,0},{2,3},{3,2},{4,5},{5,4},{6,7},{7,6},{8,9},{9,8},{10,11... | collective-permute-start | bytes 811016 | tf_op jit(solution)/shard_map/ppermute | solution.py:394
  24.5 9.1 %collective-permute-start.6 = (f32[33,16,128]{2,1,0:T(8,128)S(1)}, f32[33,16,128]{2,1,0:T(8,128)S(1)}, u32[]{:S(2)}, u32[]{:S(2)}) collective-permute-start(f32[33,16,128]{2,1,0:T(8,128)S(1)} %get-tuple-element.49), channel_id=1, source_target_pairs={{1,4},{4,1},{3,6},{6,3},{5,8},{8,5},{7,10},{10,7},{9,12},{12,9},{1... | collective-permute-start | bytes 811016 | tf_op jit(solution)/shard_map/ppermute | solution.py:394
  28.4 8.4 %collective-permute-start.13 = (f32[33,16,128]{2,1,0:T(8,128)S(1)}, f32[33,16,128]{2,1,0:T(8,128)S(1)}, u32[]{:S(2)}, u32[]{:S(2)}) collective-permute-start(f32[33,16,128]{2,1,0:T(8,128)S(1)} %get-tuple-element.62), channel_id=1, source_target_pairs={{0,1},{1,0},{2,3},{3,2},{4,5},{5,4},{6,7},{7,6},{8,9},{9,8},{10,11... | collective-permute-start | bytes 811016 | tf_op jit(solution)/shard_map/ppermute | solution.py:394
  30.5 9.1 %collective-permute-start.14 = (f32[33,16,128]{2,1,0:T(8,128)S(1)}, f32[33,16,128]{2,1,0:T(8,128)S(1)}, u32[]{:S(2)}, u32[]{:S(2)}) collective-permute-start(f32[33,16,128]{2,1,0:T(8,128)S(1)} %get-tuple-element.63), channel_id=1, source_target_pairs={{1,4},{4,1},{3,6},{6,3},{5,8},{8,5},{7,10},{10,7},{9,12},{12,9},{1... | collective-permute-start | bytes 811016 | tf_op jit(solution)/shard_map/ppermute | solution.py:394
  34.5 11.3 %collective-permute-start.7 = (f32[33,16,128]{2,1,0:T(8,128)S(1)}, f32[33,16,128]{2,1,0:T(8,128)S(1)}, u32[]{:S(2)}, u32[]{:S(2)}) collective-permute-start(f32[33,16,128]{2,1,0:T(8,128)S(1)} %get-tuple-element.52), channel_id=1, source_target_pairs={{0,1},{1,0},{2,3},{3,2},{4,5},{5,4},{6,7},{7,6},{8,9},{9,8},{10,11... | collective-permute-start | bytes 811016 | tf_op jit(solution)/shard_map/ppermute | solution.py:394
  36.3 9.4 %collective-permute-start.8 = (f32[33,16,128]{2,1,0:T(8,128)S(1)}, f32[33,16,128]{2,1,0:T(8,128)S(1)}, u32[]{:S(2)}, u32[]{:S(2)}) collective-permute-start(f32[33,16,128]{2,1,0:T(8,128)S(1)} %get-tuple-element.53), channel_id=1, source_target_pairs={{1,4},{4,1},{3,6},{6,3},{5,8},{8,5},{7,10},{10,7},{9,12},{12,9},{1... | collective-permute-start | bytes 811016 | tf_op jit(solution)/shard_map/ppermute | solution.py:394
  40.7 2.4 %collective-permute-start.15 = (f32[8,128]{1,0:T(8,128)S(1)}, f32[8,128]{1,0:T(8,128)S(1)}, u32[]{:S(2)}, u32[]{:S(2)}) collective-permute-start(f32[8,128]{1,0:T(8,128)S(1)} %get-tuple-element.68), channel_id=1, source_target_pairs={{0,1},{1,0},{2,3},{3,2},{4,5},{5,4},{6,7},{7,6},{8,9},{9,8},{10,11... | collective-permute-start | bytes 12296 | tf_op jit(solution)/shard_map/ppermute | solution.py:394
  42.3 3.4 %collective-permute-start.16 = (f32[8,128]{1,0:T(8,128)S(1)}, f32[8,128]{1,0:T(8,128)S(1)}, u32[]{:S(2)}, u32[]{:S(2)}) collective-permute-start(f32[8,128]{1,0:T(8,128)S(1)} %get-tuple-element.69), channel_id=1, source_target_pairs={{1,4},{4,1},{3,6},{6,3},{5,8},{8,5},{7,10},{10,7},{9,12},{12,9},{1... | collective-permute-start | bytes 12296 | tf_op jit(solution)/shard_map/ppermute | solution.py:394
  46.6 6.2 %collective-permute-start.17 = (f32[552,128]{1,0:T(8,128)S(1)}, f32[552,128]{1,0:T(8,128)S(1)}, u32[]{:S(2)}, u32[]{:S(2)}) collective-permute-start(f32[552,128]{1,0:T(8,128)S(1)} %get-tuple-element.77), channel_id=1, source_target_pairs={{2,0},{0,1},{3,2},{1,3},{6,4},{4,5},{7,6},{5,7},{10,8},{8,9},{11,1... | collective-permute-start | bytes 847880 | tf_op jit(solution)/shard_map/ppermute | solution.py:394
  49.2 8.7 %collective-permute-start.18 = (f32[552,128]{1,0:T(8,128)S(1)}, f32[552,128]{1,0:T(8,128)S(1)}, u32[]{:S(2)}, u32[]{:S(2)}) collective-permute-start(f32[552,128]{1,0:T(8,128)S(1)} %get-tuple-element.76), channel_id=1, source_target_pairs={{0,0},{1,2},{2,1},{3,3},{4,4},{5,6},{6,5},{7,7},{8,8},{9,10},{10,9... | collective-permute-start | bytes 847880 | tf_op jit(solution)/shard_map/ppermute | solution.py:394

commit v4 on v3

--- a/solution.py
+++ b/solution.py
@@ -339,7 +339,7 @@
 
 
 def final_kernel(ny, orb, atom_dev, idx, *refs):
-    blocks, (out, gp_out, e_out, gp, sems) = refs[:2], refs[2:]
+    blocks, (out, gp_out, e_out, gp, e_box, sems) = refs[:2], refs[2:]
     k = lax.rem(idx[0], GROUP)
     rows = orb * ny
     copies = []
@@ -359,8 +359,10 @@
     e = total[ny : ny + 1]
     lane = lane_iota(e.shape)
     for n in range(atom_dev):
-        e_out[n] = jnp.sum(jnp.where(lane == n, e, 0.0))
-    for copy in copies + [last]:
+        e_box[n] = jnp.sum(jnp.where(lane == n, e, 0.0))
+    ends = [last, pltpu.make_async_copy(e_box, e_out, sems.at[3])]
+    ends[1].start()
+    for copy in copies + ends:
         copy.wait()
 
 
@@ -466,8 +468,8 @@
     inner, outer = edges
     cot_halo = halo(inner, outer)
     cot_halo = (
-        cot_halo[0],
-        jnp.concatenate([permute(outer[:ny], across), permute(outer[ny:], across)]),
+        jnp.concatenate([permute(inner[:ny], core), permute(inner[ny:], core)]),
+        cot_halo[1],
     )
     zero, tile_zero, *edges = relay(False, orb_blocks, dense)
     zero_halo = halo(*edges)
@@ -510,10 +512,13 @@
         idx,
         *images,
         micros=1.0,
-        scratch=[pltpu.VMEM((ny, LANES), F32), pltpu.SemaphoreType.DMA((3,))],
+        scratch=[
+            pltpu.VMEM((ny, LANES), F32),
+            pltpu.SMEM((atom_dev,), F32),
+            pltpu.SemaphoreType.DMA((4,)),
+        ],
         smem=(0,),
-        hbm_outs=(0, 1),
-        smem_outs=(2,),
+        hbm_outs=(0, 1, 2),
     )
     return out.reshape(orbitals.shape), gp.reshape(potential.shape), e
 

time: 59.5 us -> 58.8 us (0.988)
  starting transfers between devices: 27.9 us -> 26.3 us
  waiting for transfers between devices: 20.3 us -> 21.7 us
    ppermute x19, starting transfers between devices: 27.9 us -> 26.3 us  [permute(): return lax.ppermute(x, 'grid', to)]
    ppermute x19, waiting for transfers between devices: 20.3 us -> 21.7 us  [permute(): return lax.ppermute(x, 'grid', to)]
where the time goes in v4:
time: 58.8 us; the launch traced here: 58.6 us
  starting transfers between devices  26.3 us (45%)
  waiting for transfers between devices  21.7 us (37%)
  Pallas kernels  9.67 us (16%)
  between operations  0.74 us (1%)
    ppermute x19, starting transfers between devices, permute(): return lax.ppermute(x, 'grid', to)  26.3 us
    ppermute x19, waiting for transfers between devices, permute(): return lax.ppermute(x, 'grid', to)  21.7 us
    pallas_call x10, Pallas kernels, call(): pl.pallas_call(body, out_shape=out_shape, in_specs=in_specs, out_specs=ou...  9.67 us
  transfers between devices with their start and end apart: 19, of which 10 were waited for; matrix products, arithmetic and copies ran while one was open for 0% of the time, Pallas kernels for 12%

profile of v4, /device:TPU:1, one launch (start us, length us, event | category | flops | bytes accessed | tf_op | source)
XLA Modules:
  0.0 58.6 jit_solution(886551674395565449)
XLA Ops:
  0.6 1.1 %shard_map.103 = (f32[16,128]{1,0:T(8,128)S(1)}, f32[592,128]{1,0:T(8,128)S(1)}, f32[592,128]{1,0:T(8,128)S(1)}) custom-call(s32[1]{0:T(128)} %bitcast.idx, f32[4]{0:T(128)} %cheb.1, f32[32]{0:T(128)} %energy.1, s32[16,128]{1,0:T(8,128)} %bitcast.14, s32[16,128]{1,0:T(8,128)} %bitcast.15, f32[16,128]{1,0:T(8,128)} %bitcast.16, f32[32,128]{1,0:T(8,128)} %bitcast.13, ...), custom_call_target="tpu_custom_call" | custom-call | flops 1200000 | bytes 4428000 | tf_op jit(solution)/shard_map/pallas_call | solution.py:43
  1.8 4.5 %collective-permute-start.1 = (f32[592,128]{1,0:T(8,128)S(1)}, f32[592,128]{1,0:T(8,128)S(1)}, u32[]{:S(2)}, u32[]{:S(2)}) collective-permute-start(f32[592,128]{1,0:T(8,128)S(1)} %get-tuple-element.40), channel_id=1, source_target_pairs={{0,0},{1,2},{2,1},{3,3},{4,4},{5,6},{6,5},{7,7},{8,8},{9,10},{10,9... | collective-permute-start | bytes 909320 | tf_op jit(solution)/shard_map/ppermute | solution.py:396
  6.3 1.1 %shard_map.107 = (f32[512,128]{1,0:T(8,128)S(1)}, f32[512,128]{1,0:T(8,128)S(1)}) custom-call(s32[1]{0:T(128)} %bitcast.idx, f32[1024,128]{1,0:T(8,128)} %bitcast.12), custom_call_target="tpu_custom_call" | custom-call | flops 1000000 | bytes 3690000 | tf_op jit(solution)/shard_map/pallas_call | solution.py:43
  7.4 1.9 %collective-permute-start.10 = (f32[512,128]{1,0:T(8,128)S(1)}, f32[512,128]{1,0:T(8,128)S(1)}, u32[]{:S(2)}, u32[]{:S(2)}) collective-permute-start(f32[512,128]{1,0:T(8,128)S(1)} %get-tuple-element.55), channel_id=1, source_target_pairs={{0,0},{1,2},{2,1},{3,3},{4,4},{5,6},{6,5},{7,7},{8,8},{9,10},{10,9... | collective-permute-start | bytes 786440 | tf_op jit(solution)/shard_map/ppermute | solution.py:396
  9.3 2.6 %collective-permute-done.1.refs_1_ = f32[592,128]{1,0:T(8,128)S(1)} collective-permute-done((f32[592,128]{1,0:T(8,128)S(1)}, f32[592,128]{1,0:T(8,128)S(1)}, u32[]{:S(2)}, u32[]{:S(2)}) %collective-permute-start.1) | collective-permute-done | bytes 303136 | tf_op jit(solution)/shard_map/ppermute | solution.py:396
  11.9 1.4 %shard_map.104 = (f32[64,8,128]{2,1,0:T(8,128)S(1)}, f32[64,16,128]{2,1,0:T(8,128)S(1)}, f32[16,128]{1,0:T(8,128)S(1)}, f32[33,16,128]{2,1,0:T(8,128)S(1)}, f32[33,16,128]{2,1,0:T(8,128)S(1)}) custom-call(s32[1]{0:T(128)} %bitcast.idx, f32[592,128]{1,0:T(8,128)S(1)} %collective-permute-done.refs_0_, f32[592,128]{1,0:T(8,128)S(1)} %collective-permute-done.1.refs_1_), custom_call_target="tpu_custom_call" | custom-call | flops 1400000 | bytes 5166000 | tf_op jit(solution)/shard_map/pallas_call | solution.py:43
  13.4 1.7 %collective-permute-start.4 = (f32[33,16,128]{2,1,0:T(8,128)S(1)}, f32[33,16,128]{2,1,0:T(8,128)S(1)}, u32[]{:S(2)}, u32[]{:S(2)}) collective-permute-start(f32[33,16,128]{2,1,0:T(8,128)S(1)} %get-tuple-element.45), channel_id=1, source_target_pairs={{1,4},{4,1},{3,6},{6,3},{5,8},{8,5},{7,10},{10,7},{9,12},{12,9},{1... | collective-permute-start | bytes 811016 | tf_op jit(solution)/shard_map/ppermute | solution.py:396
  15.1 2.1 %collective-permute-start.3 = (f32[1,16,128]{2,1,0:T(8,128)S(1)}, f32[1,16,128]{2,1,0:T(8,128)S(1)}, u32[]{:S(2)}, u32[]{:S(2)}) collective-permute-start(f32[1,16,128]{2,1,0:T(8,128)S(1)} %slice.7), channel_id=1, source_target_pairs={{0,1},{1,0},{2,3},{3,2},{4,5},{5,4},{6,7},{7,6},{8,9},{9,8},{10,11... | collective-permute-start | bytes 24584 | tf_op jit(solution)/shard_map/ppermute | solution.py:396
  17.2 0.1 collective-permute-done.10.refs_1_
  17.3 0.6 %shard_map.108 = (f32[64,16,128]{2,1,0:T(8,128)S(1)}, f32[16,128]{1,0:T(8,128)S(1)}, f32[33,16,128]{2,1,0:T(8,128)S(1)}, f32[33,16,128]{2,1,0:T(8,128)S(1)}) custom-call(s32[1]{0:T(128)} %bitcast.idx, f32[512,128]{1,0:T(8,128)S(1)} %collective-permute-done.9.refs_0_, f32[512,128]{1,0:T(8,128)S(1)} %collective-permute-done.10.refs_1_, ...), custom_call_target="tpu_custom_call" | custom-call | flops 700000 | bytes 2583000 | tf_op jit(solution)/shard_map/pallas_call | solution.py:43
  18.0 0.6 %collective-permute-start.11 = (f32[33,16,128]{2,1,0:T(8,128)S(1)}, f32[33,16,128]{2,1,0:T(8,128)S(1)}, u32[]{:S(2)}, u32[]{:S(2)}) collective-permute-start(f32[33,16,128]{2,1,0:T(8,128)S(1)} %get-tuple-element.58), channel_id=1, source_target_pairs={{0,1},{1,0},{2,3},{3,2},{4,5},{5,4},{6,7},{7,6},{8,9},{9,8},{10,11... | collective-permute-start | bytes 811016 | tf_op jit(solution)/shard_map/ppermute | solution.py:396
  18.6 1.9 %collective-permute-start.12 = (f32[33,16,128]{2,1,0:T(8,128)S(1)}, f32[33,16,128]{2,1,0:T(8,128)S(1)}, u32[]{:S(2)}, u32[]{:S(2)}) collective-permute-start(f32[33,16,128]{2,1,0:T(8,128)S(1)} %get-tuple-element.59), channel_id=1, source_target_pairs={{1,4},{4,1},{3,6},{6,3},{5,8},{8,5},{7,10},{10,7},{9,12},{12,9},{1... | collective-permute-start | bytes 811016 | tf_op jit(solution)/shard_map/ppermute | solution.py:396
  20.5 0.9 %collective-permute-done.4.refs_5_ = f32[33,16,128]{2,1,0:T(8,128)S(1)} collective-permute-done((f32[33,16,128]{2,1,0:T(8,128)S(1)}, f32[33,16,128]{2,1,0:T(8,128)S(1)}, u32[]{:S(2)}, u32[]{:S(2)}) %collective-permute-start.4) | collective-permute-done | bytes 270368 | tf_op jit(solution)/shard_map/ppermute | solution.py:396
  21.4 0.9 %shard_map.105 = (f32[64,16,128]{2,1,0:T(8,128)S(1)}, f32[16,128]{1,0:T(8,128)S(1)}, f32[33,16,128]{2,1,0:T(8,128)S(1)}, f32[33,16,128]{2,1,0:T(8,128)S(1)}, f32[16,128]{1,0:T(8,128)S(1)}) custom-call(f32[16,128]{1,0:T(8,128)S(1)} %get-tuple-element.38.refs_0_, f32[64,8,128]{2,1,0:T(8,128)S(1)} %get-tuple-element.41.refs_1_.refs_2_, ...), custom_call_target="tpu_custom_call" | custom-call | flops 1000000 | bytes 3690000 | tf_op jit(solution)/shard_map/pallas_call | solution.py:43
  22.3 2.7 %collective-permute-start.5 = (f32[33,16,128]{2,1,0:T(8,128)S(1)}, f32[33,16,128]{2,1,0:T(8,128)S(1)}, u32[]{:S(2)}, u32[]{:S(2)}) collective-permute-start(f32[33,16,128]{2,1,0:T(8,128)S(1)} %get-tuple-element.48), channel_id=1, source_target_pairs={{0,1},{1,0},{2,3},{3,2},{4,5},{5,4},{6,7},{7,6},{8,9},{9,8},{10,11... | collective-permute-start | bytes 811016 | tf_op jit(solution)/shard_map/ppermute | solution.py:396
  25.0 2.8 %collective-permute-done.12.refs_5_ = f32[33,16,128]{2,1,0:T(8,128)S(1)} collective-permute-done((f32[33,16,128]{2,1,0:T(8,128)S(1)}, f32[33,16,128]{2,1,0:T(8,128)S(1)}, u32[]{:S(2)}, u32[]{:S(2)}) %collective-permute-start.12) | collective-permute-done | bytes 270368 | tf_op jit(solution)/shard_map/ppermute | solution.py:396
  27.8 0.9 %shard_map.109 = (f32[64,16,128]{2,1,0:T(8,128)S(1)}, f32[16,128]{1,0:T(8,128)S(1)}, f32[33,16,128]{2,1,0:T(8,128)S(1)}, f32[33,16,128]{2,1,0:T(8,128)S(1)}, f32[16,128]{1,0:T(8,128)S(1)}) custom-call(f32[16,128]{1,0:T(8,128)S(1)} %get-tuple-element.38.refs_0_, f32[64,8,128]{2,1,0:T(8,128)S(1)} %get-tuple-element.41.refs_1_.refs_2_, ...), custom_call_target="tpu_custom_call" | custom-call | flops 1000000 | bytes 3690000 | tf_op jit(solution)/shard_map/pallas_call | solution.py:43
  28.7 2.1 %collective-permute-start.13 = (f32[33,16,128]{2,1,0:T(8,128)S(1)}, f32[33,16,128]{2,1,0:T(8,128)S(1)}, u32[]{:S(2)}, u32[]{:S(2)}) collective-permute-start(f32[33,16,128]{2,1,0:T(8,128)S(1)} %get-tuple-element.62), channel_id=1, source_target_pairs={{0,1},{1,0},{2,3},{3,2},{4,5},{5,4},{6,7},{7,6},{8,9},{9,8},{10,11... | collective-permute-start | bytes 811016 | tf_op jit(solution)/shard_map/ppermute | solution.py:396
  30.8 3.3 %collective-permute-done.6.refs_5_ = f32[33,16,128]{2,1,0:T(8,128)S(1)} collective-permute-done((f32[33,16,128]{2,1,0:T(8,128)S(1)}, f32[33,16,128]{2,1,0:T(8,128)S(1)}, u32[]{:S(2)}, u32[]{:S(2)}) %collective-permute-start.6) | collective-permute-done | bytes 270368 | tf_op jit(solution)/shard_map/ppermute | solution.py:396
  34.1 0.9 %shard_map.106 = (f32[64,16,128]{2,1,0:T(8,128)S(1)}, f32[16,128]{1,0:T(8,128)S(1)}, f32[33,16,128]{2,1,0:T(8,128)S(1)}, f32[33,16,128]{2,1,0:T(8,128)S(1)}) custom-call(f32[16,128]{1,0:T(8,128)S(1)} %get-tuple-element.38.refs_0_, f32[64,8,128]{2,1,0:T(8,128)S(1)} %get-tuple-element.41.refs_1_.refs_2_, ...), custom_call_target="tpu_custom_call" | custom-call | flops 1000000 | bytes 3690000 | tf_op jit(solution)/shard_map/pallas_call | solution.py:43
  35.0 1.6 %collective-permute-start.7 = (f32[33,16,128]{2,1,0:T(8,128)S(1)}, f32[33,16,128]{2,1,0:T(8,128)S(1)}, u32[]{:S(2)}, u32[]{:S(2)}) collective-permute-start(f32[33,16,128]{2,1,0:T(8,128)S(1)} %get-tuple-element.52), channel_id=1, source_target_pairs={{0,1},{1,0},{2,3},{3,2},{4,5},{5,4},{6,7},{7,6},{8,9},{9,8},{10,11... | collective-permute-start | bytes 811016 | tf_op jit(solution)/shard_map/ppermute | solution.py:396
  36.6 3.3 %collective-permute-done.14.refs_5_ = f32[33,16,128]{2,1,0:T(8,128)S(1)} collective-permute-done((f32[33,16,128]{2,1,0:T(8,128)S(1)}, f32[33,16,128]{2,1,0:T(8,128)S(1)}, u32[]{:S(2)}, u32[]{:S(2)}) %collective-permute-start.14) | collective-permute-done | bytes 270368 | tf_op jit(solution)/shard_map/ppermute | solution.py:396
  39.9 1.2 %shard_map.110 = (f32[64,128]{1,0:T(8,128)S(1)}, f32[8,128]{1,0:T(8,128)S(1)}, f32[8,128]{1,0:T(8,128)S(1)}, f32[8,128]{1,0:T(8,128)S(1)}) custom-call(f32[16,128]{1,0:T(8,128)S(1)} %get-tuple-element.38.refs_0_, f32[64,8,128]{2,1,0:T(8,128)S(1)} %get-tuple-element.41.refs_1_.refs_2_, f32[64,16,128]{2,1,0:T(8,128)S(1)} %get-tuple-element.60.refs_2_, ...), custom_call_target="tpu_custom_call" | custom-call | flops 1000000 | bytes 3690000 | tf_op jit(solution)/shard_map/pallas_call | solution.py:43
  41.1 1.6 %collective-permute-start.15 = (f32[8,128]{1,0:T(8,128)S(1)}, f32[8,128]{1,0:T(8,128)S(1)}, u32[]{:S(2)}, u32[]{:S(2)}) collective-permute-start(f32[8,128]{1,0:T(8,128)S(1)} %get-tuple-element.68), channel_id=1, source_target_pairs={{0,1},{1,0},{2,3},{3,2},{4,5},{5,4},{6,7},{7,6},{8,9},{9,8},{10,11... | collective-permute-start | bytes 12296 | tf_op jit(solution)/shard_map/ppermute | solution.py:396
  42.7 0.8 %collective-permute-done.15.refs_10_ = f32[8,128]{1,0:T(8,128)S(1)} collective-permute-done((f32[8,128]{1,0:T(8,128)S(1)}, f32[8,128]{1,0:T(8,128)S(1)}, u32[]{:S(2)}, u32[]{:S(2)}) %collective-permute-start.15) | collective-permute-done | bytes 4128 | tf_op jit(solution)/shard_map/ppermute | solution.py:396
  43.5 2.5 %collective-permute-done.16.refs_11_ = f32[8,128]{1,0:T(8,128)S(1)} collective-permute-done((f32[8,128]{1,0:T(8,128)S(1)}, f32[8,128]{1,0:T(8,128)S(1)}, u32[]{:S(2)}, u32[]{:S(2)}) %collective-permute-start.16) | collective-permute-done | bytes 4128 | tf_op jit(solution)/shard_map/ppermute | solution.py:396
  46.0 0.8 %shard_map.111 = f32[1104,128]{1,0:T(8,128)S(1)} custom-call(f32[16,128]{1,0:T(8,128)S(1)} %get-tuple-element.38.refs_0_, f32[64,8,128]{2,1,0:T(8,128)S(1)} %get-tuple-element.41.refs_1_.refs_2_, f32[64,16,128]{2,1,0:T(8,128)S(1)} %get-tuple-element.50.refs_8_.refs_2_, f32[16,128]{1,0:T(8,128)S(1)} %get-tuple-element.51.refs_9_.refs_3_, ...), custom_call_target="tpu_custom_call" | custom-call | flops 1000000 | bytes 3690000 | tf_op jit(solution)/shard_map/pallas_call | solution.py:43
  46.8 0.1 constant_dynamic-slice_fusion
  46.9 2.0 %collective-permute-start.17 = (f32[552,128]{1,0:T(8,128)S(1)}, f32[552,128]{1,0:T(8,128)S(1)}, u32[]{:S(2)}, u32[]{:S(2)}) collective-permute-start(f32[552,128]{1,0:T(8,128)S(1)} %get-tuple-element.77), channel_id=1, source_target_pairs={{2,0},{0,1},{3,2},{1,3},{6,4},{4,5},{7,6},{5,7},{10,8},{8,9},{11,1... | collective-permute-start | bytes 847880 | tf_op jit(solution)/shard_map/ppermute | solution.py:396
  48.9 3.5 %collective-permute-start.18 = (f32[552,128]{1,0:T(8,128)S(1)}, f32[552,128]{1,0:T(8,128)S(1)}, u32[]{:S(2)}, u32[]{:S(2)}) collective-permute-start(f32[552,128]{1,0:T(8,128)S(1)} %get-tuple-element.76), channel_id=1, source_target_pairs={{0,0},{1,2},{2,1},{3,3},{4,4},{5,6},{6,5},{7,7},{8,8},{9,10},{10,9... | collective-permute-start | bytes 847880 | tf_op jit(solution)/shard_map/ppermute | solution.py:396
  52.4 5.3 %collective-permute-done.18.refs_1_ = f32[552,128]{1,0:T(8,128)S(1)} collective-permute-done((f32[552,128]{1,0:T(8,128)S(1)}, f32[552,128]{1,0:T(8,128)S(1)}, u32[]{:S(2)}, u32[]{:S(2)}) %collective-permute-start.18) | collective-permute-done | bytes 282656 | tf_op jit(solution)/shard_map/ppermute | solution.py:396
  57.7 0.8 %shard_map.112 = (f32[1024,128]{1,0:T(8,128)}, f32[32,128]{1,0:T(8,128)}, f32[2]{0:T(128)}) custom-call(s32[1]{0:T(128)} %bitcast.idx, f32[552,128]{1,0:T(8,128)S(1)} %collective-permute-done.17.refs_0_, f32[552,128]{1,0:T(8,128)S(1)} %collective-permute-done.18.refs_1_), custom_call_target="tpu_custom_call" | custom-call | flops 1000000 | bytes 3690000 | tf_op jit(solution)/shard_map/pallas_call | solution.py:43
  (20 shorter events, 0.3 us)
Async XLA Ops:
  1.8 7.6 %collective-permute-start = (f32[592,128]{1,0:T(8,128)S(1)}, f32[592,128]{1,0:T(8,128)S(1)}, u32[]{:S(2)}, u32[]{:S(2)}) collective-permute-start(f32[592,128]{1,0:T(8,128)S(1)} %get-tuple-element.39), channel_id=1, source_target_pairs={{0,2},{1,0},{2,3},{3,1},{4,6},{5,4},{6,7},{7,5},{8,10},{9,8},{10,1... | collective-permute-start | bytes 909320 | tf_op jit(solution)/shard_map/ppermute | solution.py:396
  1.8 10.1 %collective-permute-start.1 = (f32[592,128]{1,0:T(8,128)S(1)}, f32[592,128]{1,0:T(8,128)S(1)}, u32[]{:S(2)}, u32[]{:S(2)}) collective-permute-start(f32[592,128]{1,0:T(8,128)S(1)} %get-tuple-element.40), channel_id=1, source_target_pairs={{0,0},{1,2},{2,1},{3,3},{4,4},{5,6},{6,5},{7,7},{8,8},{9,10},{10,9... | collective-permute-start | bytes 909320 | tf_op jit(solution)/shard_map/ppermute | solution.py:396
  7.4 10.0 %collective-permute-start.10 = (f32[512,128]{1,0:T(8,128)S(1)}, f32[512,128]{1,0:T(8,128)S(1)}, u32[]{:S(2)}, u32[]{:S(2)}) collective-permute-start(f32[512,128]{1,0:T(8,128)S(1)} %get-tuple-element.55), channel_id=1, source_target_pairs={{0,0},{1,2},{2,1},{3,3},{4,4},{5,6},{6,5},{7,7},{8,8},{9,10},{10,9... | collective-permute-start | bytes 786440 | tf_op jit(solution)/shard_map/ppermute | solution.py:396
  9.3 8.0 %collective-permute-start.9 = (f32[512,128]{1,0:T(8,128)S(1)}, f32[512,128]{1,0:T(8,128)S(1)}, u32[]{:S(2)}, u32[]{:S(2)}) collective-permute-start(f32[512,128]{1,0:T(8,128)S(1)} %get-tuple-element.54), channel_id=1, source_target_pairs={{0,2},{1,0},{2,3},{3,1},{4,6},{5,4},{6,7},{7,5},{8,10},{9,8},{10,1... | collective-permute-start | bytes 786440 | tf_op jit(solution)/shard_map/ppermute | solution.py:396
  13.3 7.1 %collective-permute-start.2 = (f32[32,16,128]{2,1,0:T(8,128)S(1)}, f32[32,16,128]{2,1,0:T(8,128)S(1)}, u32[]{:S(2)}, u32[]{:S(2)}) collective-permute-start(f32[32,16,128]{2,1,0:T(8,128)S(1)} %slice.6), channel_id=1, source_target_pairs={{0,1},{1,0},{2,3},{3,2},{4,5},{5,4},{6,7},{7,6},{8,9},{9,8},{10,11... | collective-permute-start | bytes 786440 | tf_op jit(solution)/shard_map/ppermute | solution.py:396
  13.4 8.0 %collective-permute-start.4 = (f32[33,16,128]{2,1,0:T(8,128)S(1)}, f32[33,16,128]{2,1,0:T(8,128)S(1)}, u32[]{:S(2)}, u32[]{:S(2)}) collective-permute-start(f32[33,16,128]{2,1,0:T(8,128)S(1)} %get-tuple-element.45), channel_id=1, source_target_pairs={{1,4},{4,1},{3,6},{6,3},{5,8},{8,5},{7,10},{10,7},{9,12},{12,9},{1... | collective-permute-start | bytes 811016 | tf_op jit(solution)/shard_map/ppermute | solution.py:396
  15.1 5.4 %collective-permute-start.3 = (f32[1,16,128]{2,1,0:T(8,128)S(1)}, f32[1,16,128]{2,1,0:T(8,128)S(1)}, u32[]{:S(2)}, u32[]{:S(2)}) collective-permute-start(f32[1,16,128]{2,1,0:T(8,128)S(1)} %slice.7), channel_id=1, source_target_pairs={{0,1},{1,0},{2,3},{3,2},{4,5},{5,4},{6,7},{7,6},{8,9},{9,8},{10,11... | collective-permute-start | bytes 24584 | tf_op jit(solution)/shard_map/ppermute | solution.py:396
  18.0 7.1 %collective-permute-start.11 = (f32[33,16,128]{2,1,0:T(8,128)S(1)}, f32[33,16,128]{2,1,0:T(8,128)S(1)}, u32[]{:S(2)}, u32[]{:S(2)}) collective-permute-start(f32[33,16,128]{2,1,0:T(8,128)S(1)} %get-tuple-element.58), channel_id=1, source_target_pairs={{0,1},{1,0},{2,3},{3,2},{4,5},{5,4},{6,7},{7,6},{8,9},{9,8},{10,11... | collective-permute-start | bytes 811016 | tf_op jit(solution)/shard_map/ppermute | solution.py:396
  18.6 9.2 %collective-permute-start.12 = (f32[33,16,128]{2,1,0:T(8,128)S(1)}, f32[33,16,128]{2,1,0:T(8,128)S(1)}, u32[]{:S(2)}, u32[]{:S(2)}) collective-permute-start(f32[33,16,128]{2,1,0:T(8,128)S(1)} %get-tuple-element.59), channel_id=1, source_target_pairs={{1,4},{4,1},{3,6},{6,3},{5,8},{8,5},{7,10},{10,7},{9,12},{12,9},{1... | collective-permute-start | bytes 811016 | tf_op jit(solution)/shard_map/ppermute | solution.py:396
  22.3 8.5 %collective-permute-start.5 = (f32[33,16,128]{2,1,0:T(8,128)S(1)}, f32[33,16,128]{2,1,0:T(8,128)S(1)}, u32[]{:S(2)}, u32[]{:S(2)}) collective-permute-start(f32[33,16,128]{2,1,0:T(8,128)S(1)} %get-tuple-element.48), channel_id=1, source_target_pairs={{0,1},{1,0},{2,3},{3,2},{4,5},{5,4},{6,7},{7,6},{8,9},{9,8},{10,11... | collective-permute-start | bytes 811016 | tf_op jit(solution)/shard_map/ppermute | solution.py:396
  25.0 9.1 %collective-permute-start.6 = (f32[33,16,128]{2,1,0:T(8,128)S(1)}, f32[33,16,128]{2,1,0:T(8,128)S(1)}, u32[]{:S(2)}, u32[]{:S(2)}) collective-permute-start(f32[33,16,128]{2,1,0:T(8,128)S(1)} %get-tuple-element.49), channel_id=1, source_target_pairs={{1,4},{4,1},{3,6},{6,3},{5,8},{8,5},{7,10},{10,7},{9,12},{12,9},{1... | collective-permute-start | bytes 811016 | tf_op jit(solution)/shard_map/ppermute | solution.py:396
  28.7 7.9 %collective-permute-start.13 = (f32[33,16,128]{2,1,0:T(8,128)S(1)}, f32[33,16,128]{2,1,0:T(8,128)S(1)}, u32[]{:S(2)}, u32[]{:S(2)}) collective-permute-start(f32[33,16,128]{2,1,0:T(8,128)S(1)} %get-tuple-element.62), channel_id=1, source_target_pairs={{0,1},{1,0},{2,3},{3,2},{4,5},{5,4},{6,7},{7,6},{8,9},{9,8},{10,11... | collective-permute-start | bytes 811016 | tf_op jit(solution)/shard_map/ppermute | solution.py:396
  30.8 9.1 %collective-permute-start.14 = (f32[33,16,128]{2,1,0:T(8,128)S(1)}, f32[33,16,128]{2,1,0:T(8,128)S(1)}, u32[]{:S(2)}, u32[]{:S(2)}) collective-permute-start(f32[33,16,128]{2,1,0:T(8,128)S(1)} %get-tuple-element.63), channel_id=1, source_target_pairs={{1,4},{4,1},{3,6},{6,3},{5,8},{8,5},{7,10},{10,7},{9,12},{12,9},{1... | collective-permute-start | bytes 811016 | tf_op jit(solution)/shard_map/ppermute | solution.py:396
  35.0 11.0 %collective-permute-start.7 = (f32[33,16,128]{2,1,0:T(8,128)S(1)}, f32[33,16,128]{2,1,0:T(8,128)S(1)}, u32[]{:S(2)}, u32[]{:S(2)}) collective-permute-start(f32[33,16,128]{2,1,0:T(8,128)S(1)} %get-tuple-element.52), channel_id=1, source_target_pairs={{0,1},{1,0},{2,3},{3,2},{4,5},{5,4},{6,7},{7,6},{8,9},{9,8},{10,11... | collective-permute-start | bytes 811016 | tf_op jit(solution)/shard_map/ppermute | solution.py:396
  36.6 9.4 %collective-permute-start.8 = (f32[33,16,128]{2,1,0:T(8,128)S(1)}, f32[33,16,128]{2,1,0:T(8,128)S(1)}, u32[]{:S(2)}, u32[]{:S(2)}) collective-permute-start(f32[33,16,128]{2,1,0:T(8,128)S(1)} %get-tuple-element.53), channel_id=1, source_target_pairs={{1,4},{4,1},{3,6},{6,3},{5,8},{8,5},{7,10},{10,7},{9,12},{12,9},{1... | collective-permute-start | bytes 811016 | tf_op jit(solution)/shard_map/ppermute | solution.py:396
  41.1 2.4 %collective-permute-start.15 = (f32[8,128]{1,0:T(8,128)S(1)}, f32[8,128]{1,0:T(8,128)S(1)}, u32[]{:S(2)}, u32[]{:S(2)}) collective-permute-start(f32[8,128]{1,0:T(8,128)S(1)} %get-tuple-element.68), channel_id=1, source_target_pairs={{0,1},{1,0},{2,3},{3,2},{4,5},{5,4},{6,7},{7,6},{8,9},{9,8},{10,11... | collective-permute-start | bytes 12296 | tf_op jit(solution)/shard_map/ppermute | solution.py:396
  42.6 3.4 %collective-permute-start.16 = (f32[8,128]{1,0:T(8,128)S(1)}, f32[8,128]{1,0:T(8,128)S(1)}, u32[]{:S(2)}, u32[]{:S(2)}) collective-permute-start(f32[8,128]{1,0:T(8,128)S(1)} %get-tuple-element.69), channel_id=1, source_target_pairs={{1,4},{4,1},{3,6},{6,3},{5,8},{8,5},{7,10},{10,7},{9,12},{12,9},{1... | collective-permute-start | bytes 12296 | tf_op jit(solution)/shard_map/ppermute | solution.py:396
  46.9 5.5 %collective-permute-start.17 = (f32[552,128]{1,0:T(8,128)S(1)}, f32[552,128]{1,0:T(8,128)S(1)}, u32[]{:S(2)}, u32[]{:S(2)}) collective-permute-start(f32[552,128]{1,0:T(8,128)S(1)} %get-tuple-element.77), channel_id=1, source_target_pairs={{2,0},{0,1},{3,2},{1,3},{6,4},{4,5},{7,6},{5,7},{10,8},{8,9},{11,1... | collective-permute-start | bytes 847880 | tf_op jit(solution)/shard_map/ppermute | solution.py:396
  48.9 8.9 %collective-permute-start.18 = (f32[552,128]{1,0:T(8,128)S(1)}, f32[552,128]{1,0:T(8,128)S(1)}, u32[]{:S(2)}, u32[]{:S(2)}) collective-permute-start(f32[552,128]{1,0:T(8,128)S(1)} %get-tuple-element.76), channel_id=1, source_target_pairs={{0,0},{1,2},{2,1},{3,3},{4,4},{5,6},{6,5},{7,7},{8,8},{9,10},{10,9... | collective-permute-start | bytes 847880 | tf_op jit(solution)/shard_map/ppermute | solution.py:396

commit v5 on v4

--- a/solution.py
+++ b/solution.py
@@ -112,7 +112,6 @@
         )
     for copy in copies:
         copy.start()
-    for copy in copies:
         copy.wait()
 
 

time: 58.8 us -> 58.8 us (level)
  waiting for transfers between devices: 21.7 us -> 19.3 us
  starting transfers between devices: 26.3 us -> 27.8 us
  Pallas kernels: 9.67 us -> 10.5 us
    ppermute x19, waiting for transfers between devices: 21.7 us -> 19.3 us  [permute(): return lax.ppermute(x, 'grid', to)]
    ppermute x19, starting transfers between devices: 26.3 us -> 27.8 us  [permute(): return lax.ppermute(x, 'grid', to)]
    pallas_call x10, Pallas kernels: 9.67 us -> 10.5 us  [call(): pl.pallas_call(body, out_shape=out_shape, in_specs=in_specs, out_specs=ou...]
  transfers between devices with their start and end apart: 19 -> 19, of which waited for: 10 -> 9; matrix products, arithmetic and copies ran while one was open for 0% -> 0% of each run, Pallas kernels for 12% -> 13%
where the time goes in v5:
time: 58.8 us; the launch traced here: 58.6 us
  starting transfers between devices  27.8 us (47%)
  waiting for transfers between devices  19.3 us (33%)
  Pallas kernels  10.5 us (18%)
  between operations  0.74 us (1%)
    ppermute x19, starting transfers between devices, permute(): return lax.ppermute(x, 'grid', to)  27.8 us
    ppermute x19, waiting for transfers between devices, permute(): return lax.ppermute(x, 'grid', to)  19.3 us
    pallas_call x10, Pallas kernels, call(): pl.pallas_call(body, out_shape=out_shape, in_specs=in_specs, out_specs=ou...  10.5 us
  transfers between devices with their start and end apart: 19, of which 9 were waited for; matrix products, arithmetic and copies ran while one was open for 0% of the time, Pallas kernels for 13%

profile of v5, /device:TPU:1, one launch (start us, length us, event | category | flops | bytes accessed | tf_op | source)
XLA Modules:
  0.0 58.6 jit_solution(11069033724032237661)
XLA Ops:
  0.6 1.1 %shard_map.103 = (f32[16,128]{1,0:T(8,128)S(1)}, f32[592,128]{1,0:T(8,128)S(1)}, f32[592,128]{1,0:T(8,128)S(1)}) custom-call(s32[1]{0:T(128)} %bitcast.idx, f32[4]{0:T(128)} %cheb.1, f32[32]{0:T(128)} %energy.1, s32[16,128]{1,0:T(8,128)} %bitcast.14, s32[16,128]{1,0:T(8,128)} %bitcast.15, f32[16,128]{1,0:T(8,128)} %bitcast.16, f32[32,128]{1,0:T(8,128)} %bitcast.13, ...), custom_call_target="tpu_custom_call" | custom-call | flops 1200000 | bytes 4428000 | tf_op jit(solution)/shard_map/pallas_call | solution.py:43
  1.8 4.5 %collective-permute-start.1 = (f32[592,128]{1,0:T(8,128)S(1)}, f32[592,128]{1,0:T(8,128)S(1)}, u32[]{:S(2)}, u32[]{:S(2)}) collective-permute-start(f32[592,128]{1,0:T(8,128)S(1)} %get-tuple-element.40), channel_id=1, source_target_pairs={{0,0},{1,2},{2,1},{3,3},{4,4},{5,6},{6,5},{7,7},{8,8},{9,10},{10,9... | collective-permute-start | bytes 909320 | tf_op jit(solution)/shard_map/ppermute | solution.py:395
  6.3 1.9 %shard_map.107 = (f32[512,128]{1,0:T(8,128)S(1)}, f32[512,128]{1,0:T(8,128)S(1)}) custom-call(s32[1]{0:T(128)} %bitcast.idx, f32[1024,128]{1,0:T(8,128)} %bitcast.12), custom_call_target="tpu_custom_call" | custom-call | flops 1000000 | bytes 3690000 | tf_op jit(solution)/shard_map/pallas_call | solution.py:43
  8.2 1.9 %collective-permute-start.10 = (f32[512,128]{1,0:T(8,128)S(1)}, f32[512,128]{1,0:T(8,128)S(1)}, u32[]{:S(2)}, u32[]{:S(2)}) collective-permute-start(f32[512,128]{1,0:T(8,128)S(1)} %get-tuple-element.55), channel_id=1, source_target_pairs={{0,0},{1,2},{2,1},{3,3},{4,4},{5,6},{6,5},{7,7},{8,8},{9,10},{10,9... | collective-permute-start | bytes 786440 | tf_op jit(solution)/shard_map/ppermute | solution.py:395
  10.2 1.7 %collective-permute-done.1.refs_1_ = f32[592,128]{1,0:T(8,128)S(1)} collective-permute-done((f32[592,128]{1,0:T(8,128)S(1)}, f32[592,128]{1,0:T(8,128)S(1)}, u32[]{:S(2)}, u32[]{:S(2)}) %collective-permute-start.1) | collective-permute-done | bytes 303136 | tf_op jit(solution)/shard_map/ppermute | solution.py:395
  11.9 1.4 %shard_map.104 = (f32[64,8,128]{2,1,0:T(8,128)S(1)}, f32[64,16,128]{2,1,0:T(8,128)S(1)}, f32[16,128]{1,0:T(8,128)S(1)}, f32[33,16,128]{2,1,0:T(8,128)S(1)}, f32[33,16,128]{2,1,0:T(8,128)S(1)}) custom-call(s32[1]{0:T(128)} %bitcast.idx, f32[592,128]{1,0:T(8,128)S(1)} %collective-permute-done.refs_0_, f32[592,128]{1,0:T(8,128)S(1)} %collective-permute-done.1.refs_1_), custom_call_target="tpu_custom_call" | custom-call | flops 1400000 | bytes 5166000 | tf_op jit(solution)/shard_map/pallas_call | solution.py:43
  13.8 1.3 %collective-permute-start.4 = (f32[33,16,128]{2,1,0:T(8,128)S(1)}, f32[33,16,128]{2,1,0:T(8,128)S(1)}, u32[]{:S(2)}, u32[]{:S(2)}) collective-permute-start(f32[33,16,128]{2,1,0:T(8,128)S(1)} %get-tuple-element.45), channel_id=1, source_target_pairs={{1,4},{4,1},{3,6},{6,3},{5,8},{8,5},{7,10},{10,7},{9,12},{12,9},{1... | collective-permute-start | bytes 811016 | tf_op jit(solution)/shard_map/ppermute | solution.py:395
  15.1 2.4 %collective-permute-start.3 = (f32[1,16,128]{2,1,0:T(8,128)S(1)}, f32[1,16,128]{2,1,0:T(8,128)S(1)}, u32[]{:S(2)}, u32[]{:S(2)}) collective-permute-start(f32[1,16,128]{2,1,0:T(8,128)S(1)} %slice.7), channel_id=1, source_target_pairs={{0,1},{1,0},{2,3},{3,2},{4,5},{5,4},{6,7},{7,6},{8,9},{9,8},{10,11... | collective-permute-start | bytes 24584 | tf_op jit(solution)/shard_map/ppermute | solution.py:395
  17.5 1.0 %collective-permute-done.10.refs_1_ = f32[512,128]{1,0:T(8,128)S(1)} collective-permute-done((f32[512,128]{1,0:T(8,128)S(1)}, f32[512,128]{1,0:T(8,128)S(1)}, u32[]{:S(2)}, u32[]{:S(2)}) %collective-permute-start.10) | collective-permute-done | bytes 262176 | tf_op jit(solution)/shard_map/ppermute | solution.py:395
  19.1 2.2 %collective-permute-start.12 = (f32[33,16,128]{2,1,0:T(8,128)S(1)}, f32[33,16,128]{2,1,0:T(8,128)S(1)}, u32[]{:S(2)}, u32[]{:S(2)}) collective-permute-start(f32[33,16,128]{2,1,0:T(8,128)S(1)} %get-tuple-element.59), channel_id=1, source_target_pairs={{1,4},{4,1},{3,6},{6,3},{5,8},{8,5},{7,10},{10,7},{9,12},{12,9},{1... | collective-permute-start | bytes 811016 | tf_op jit(solution)/shard_map/ppermute | solution.py:395
  21.4 0.9 %collective-permute-done.4.refs_5_ = f32[33,16,128]{2,1,0:T(8,128)S(1)} collective-permute-done((f32[33,16,128]{2,1,0:T(8,128)S(1)}, f32[33,16,128]{2,1,0:T(8,128)S(1)}, u32[]{:S(2)}, u32[]{:S(2)}) %collective-permute-start.4) | collective-permute-done | bytes 270368 | tf_op jit(solution)/shard_map/ppermute | solution.py:395
  22.2 0.9 %shard_map.105 = (f32[64,16,128]{2,1,0:T(8,128)S(1)}, f32[16,128]{1,0:T(8,128)S(1)}, f32[33,16,128]{2,1,0:T(8,128)S(1)}, f32[33,16,128]{2,1,0:T(8,128)S(1)}, f32[16,128]{1,0:T(8,128)S(1)}) custom-call(f32[16,128]{1,0:T(8,128)S(1)} %get-tuple-element.38.refs_0_, f32[64,8,128]{2,1,0:T(8,128)S(1)} %get-tuple-element.41.refs_1_.refs_2_, ...), custom_call_target="tpu_custom_call" | custom-call | flops 1000000 | bytes 3690000 | tf_op jit(solution)/shard_map/pallas_call | solution.py:43
  23.2 1.6 %collective-permute-start.5 = (f32[33,16,128]{2,1,0:T(8,128)S(1)}, f32[33,16,128]{2,1,0:T(8,128)S(1)}, u32[]{:S(2)}, u32[]{:S(2)}) collective-permute-start(f32[33,16,128]{2,1,0:T(8,128)S(1)} %get-tuple-element.48), channel_id=1, source_target_pairs={{0,1},{1,0},{2,3},{3,2},{4,5},{5,4},{6,7},{7,6},{8,9},{9,8},{10,11... | collective-permute-start | bytes 811016 | tf_op jit(solution)/shard_map/ppermute | solution.py:395
  24.8 0.7 %collective-permute-start.6 = (f32[33,16,128]{2,1,0:T(8,128)S(1)}, f32[33,16,128]{2,1,0:T(8,128)S(1)}, u32[]{:S(2)}, u32[]{:S(2)}) collective-permute-start(f32[33,16,128]{2,1,0:T(8,128)S(1)} %get-tuple-element.49), channel_id=1, source_target_pairs={{1,4},{4,1},{3,6},{6,3},{5,8},{8,5},{7,10},{10,7},{9,12},{12,9},{1... | collective-permute-start | bytes 811016 | tf_op jit(solution)/shard_map/ppermute | solution.py:395
  25.5 3.0 %collective-permute-done.12.refs_5_ = f32[33,16,128]{2,1,0:T(8,128)S(1)} collective-permute-done((f32[33,16,128]{2,1,0:T(8,128)S(1)}, f32[33,16,128]{2,1,0:T(8,128)S(1)}, u32[]{:S(2)}, u32[]{:S(2)}) %collective-permute-start.12) | collective-permute-done | bytes 270368 | tf_op jit(solution)/shard_map/ppermute | solution.py:395
  28.5 0.9 %shard_map.109 = (f32[64,16,128]{2,1,0:T(8,128)S(1)}, f32[16,128]{1,0:T(8,128)S(1)}, f32[33,16,128]{2,1,0:T(8,128)S(1)}, f32[33,16,128]{2,1,0:T(8,128)S(1)}, f32[16,128]{1,0:T(8,128)S(1)}) custom-call(f32[16,128]{1,0:T(8,128)S(1)} %get-tuple-element.38.refs_0_, f32[64,8,128]{2,1,0:T(8,128)S(1)} %get-tuple-element.41.refs_1_.refs_2_, ...), custom_call_target="tpu_custom_call" | custom-call | flops 1000000 | bytes 3690000 | tf_op jit(solution)/shard_map/pallas_call | solution.py:43
  29.4 1.3 %collective-permute-start.13 = (f32[33,16,128]{2,1,0:T(8,128)S(1)}, f32[33,16,128]{2,1,0:T(8,128)S(1)}, u32[]{:S(2)}, u32[]{:S(2)}) collective-permute-start(f32[33,16,128]{2,1,0:T(8,128)S(1)} %get-tuple-element.62), channel_id=1, source_target_pairs={{0,1},{1,0},{2,3},{3,2},{4,5},{5,4},{6,7},{7,6},{8,9},{9,8},{10,11... | collective-permute-start | bytes 811016 | tf_op jit(solution)/shard_map/ppermute | solution.py:395
  30.7 1.1 %collective-permute-start.14 = (f32[33,16,128]{2,1,0:T(8,128)S(1)}, f32[33,16,128]{2,1,0:T(8,128)S(1)}, u32[]{:S(2)}, u32[]{:S(2)}) collective-permute-start(f32[33,16,128]{2,1,0:T(8,128)S(1)} %get-tuple-element.63), channel_id=1, source_target_pairs={{1,4},{4,1},{3,6},{6,3},{5,8},{8,5},{7,10},{10,7},{9,12},{12,9},{1... | collective-permute-start | bytes 811016 | tf_op jit(solution)/shard_map/ppermute | solution.py:395
  31.8 2.5 %collective-permute-done.6.refs_5_ = f32[33,16,128]{2,1,0:T(8,128)S(1)} collective-permute-done((f32[33,16,128]{2,1,0:T(8,128)S(1)}, f32[33,16,128]{2,1,0:T(8,128)S(1)}, u32[]{:S(2)}, u32[]{:S(2)}) %collective-permute-start.6) | collective-permute-done | bytes 270368 | tf_op jit(solution)/shard_map/ppermute | solution.py:395
  34.3 0.9 %shard_map.106 = (f32[64,16,128]{2,1,0:T(8,128)S(1)}, f32[16,128]{1,0:T(8,128)S(1)}, f32[33,16,128]{2,1,0:T(8,128)S(1)}, f32[33,16,128]{2,1,0:T(8,128)S(1)}) custom-call(f32[16,128]{1,0:T(8,128)S(1)} %get-tuple-element.38.refs_0_, f32[64,8,128]{2,1,0:T(8,128)S(1)} %get-tuple-element.41.refs_1_.refs_2_, ...), custom_call_target="tpu_custom_call" | custom-call | flops 1000000 | bytes 3690000 | tf_op jit(solution)/shard_map/pallas_call | solution.py:43
  35.2 1.3 %collective-permute-start.7 = (f32[33,16,128]{2,1,0:T(8,128)S(1)}, f32[33,16,128]{2,1,0:T(8,128)S(1)}, u32[]{:S(2)}, u32[]{:S(2)}) collective-permute-start(f32[33,16,128]{2,1,0:T(8,128)S(1)} %get-tuple-element.52), channel_id=1, source_target_pairs={{0,1},{1,0},{2,3},{3,2},{4,5},{5,4},{6,7},{7,6},{8,9},{9,8},{10,11... | collective-permute-start | bytes 811016 | tf_op jit(solution)/shard_map/ppermute | solution.py:395
  36.5 1.1 %collective-permute-start.8 = (f32[33,16,128]{2,1,0:T(8,128)S(1)}, f32[33,16,128]{2,1,0:T(8,128)S(1)}, u32[]{:S(2)}, u32[]{:S(2)}) collective-permute-start(f32[33,16,128]{2,1,0:T(8,128)S(1)} %get-tuple-element.53), channel_id=1, source_target_pairs={{1,4},{4,1},{3,6},{6,3},{5,8},{8,5},{7,10},{10,7},{9,12},{12,9},{1... | collective-permute-start | bytes 811016 | tf_op jit(solution)/shard_map/ppermute | solution.py:395
  37.6 2.4 %collective-permute-done.14.refs_5_ = f32[33,16,128]{2,1,0:T(8,128)S(1)} collective-permute-done((f32[33,16,128]{2,1,0:T(8,128)S(1)}, f32[33,16,128]{2,1,0:T(8,128)S(1)}, u32[]{:S(2)}, u32[]{:S(2)}) %collective-permute-start.14) | collective-permute-done | bytes 270368 | tf_op jit(solution)/shard_map/ppermute | solution.py:395
  40.0 1.2 %shard_map.110 = (f32[64,128]{1,0:T(8,128)S(1)}, f32[8,128]{1,0:T(8,128)S(1)}, f32[8,128]{1,0:T(8,128)S(1)}, f32[8,128]{1,0:T(8,128)S(1)}) custom-call(f32[16,128]{1,0:T(8,128)S(1)} %get-tuple-element.38.refs_0_, f32[64,8,128]{2,1,0:T(8,128)S(1)} %get-tuple-element.41.refs_1_.refs_2_, f32[64,16,128]{2,1,0:T(8,128)S(1)} %get-tuple-element.60.refs_2_, ...), custom_call_target="tpu_custom_call" | custom-call | flops 1000000 | bytes 3690000 | tf_op jit(solution)/shard_map/pallas_call | solution.py:43
  41.2 1.4 %collective-permute-start.15 = (f32[8,128]{1,0:T(8,128)S(1)}, f32[8,128]{1,0:T(8,128)S(1)}, u32[]{:S(2)}, u32[]{:S(2)}) collective-permute-start(f32[8,128]{1,0:T(8,128)S(1)} %get-tuple-element.68), channel_id=1, source_target_pairs={{0,1},{1,0},{2,3},{3,2},{4,5},{5,4},{6,7},{7,6},{8,9},{9,8},{10,11... | collective-permute-start | bytes 12296 | tf_op jit(solution)/shard_map/ppermute | solution.py:395
  42.6 1.0 %collective-permute-start.16 = (f32[8,128]{1,0:T(8,128)S(1)}, f32[8,128]{1,0:T(8,128)S(1)}, u32[]{:S(2)}, u32[]{:S(2)}) collective-permute-start(f32[8,128]{1,0:T(8,128)S(1)} %get-tuple-element.69), channel_id=1, source_target_pairs={{1,4},{4,1},{3,6},{6,3},{5,8},{8,5},{7,10},{10,7},{9,12},{12,9},{1... | collective-permute-start | bytes 12296 | tf_op jit(solution)/shard_map/ppermute | solution.py:395
  43.6 2.4 %collective-permute-done.16.refs_11_ = f32[8,128]{1,0:T(8,128)S(1)} collective-permute-done((f32[8,128]{1,0:T(8,128)S(1)}, f32[8,128]{1,0:T(8,128)S(1)}, u32[]{:S(2)}, u32[]{:S(2)}) %collective-permute-start.16) | collective-permute-done | bytes 4128 | tf_op jit(solution)/shard_map/ppermute | solution.py:395
  46.0 0.8 %shard_map.111 = f32[1104,128]{1,0:T(8,128)S(1)} custom-call(f32[16,128]{1,0:T(8,128)S(1)} %get-tuple-element.38.refs_0_, f32[64,8,128]{2,1,0:T(8,128)S(1)} %get-tuple-element.41.refs_1_.refs_2_, f32[64,16,128]{2,1,0:T(8,128)S(1)} %get-tuple-element.50.refs_8_.refs_2_, f32[16,128]{1,0:T(8,128)S(1)} %get-tuple-element.51.refs_9_.refs_3_, ...), custom_call_target="tpu_custom_call" | custom-call | flops 1000000 | bytes 3690000 | tf_op jit(solution)/shard_map/pallas_call | solution.py:43
  46.8 2.0 %collective-permute-start.17 = (f32[552,128]{1,0:T(8,128)S(1)}, f32[552,128]{1,0:T(8,128)S(1)}, u32[]{:S(2)}, u32[]{:S(2)}) collective-permute-start(f32[552,128]{1,0:T(8,128)S(1)} %get-tuple-element.77), channel_id=1, source_target_pairs={{2,0},{0,1},{3,2},{1,3},{6,4},{4,5},{7,6},{5,7},{10,8},{8,9},{11,1... | collective-permute-start | bytes 847880 | tf_op jit(solution)/shard_map/ppermute | solution.py:395
  48.9 3.5 %collective-permute-start.18 = (f32[552,128]{1,0:T(8,128)S(1)}, f32[552,128]{1,0:T(8,128)S(1)}, u32[]{:S(2)}, u32[]{:S(2)}) collective-permute-start(f32[552,128]{1,0:T(8,128)S(1)} %get-tuple-element.76), channel_id=1, source_target_pairs={{0,0},{1,2},{2,1},{3,3},{4,4},{5,6},{6,5},{7,7},{8,8},{9,10},{10,9... | collective-permute-start | bytes 847880 | tf_op jit(solution)/shard_map/ppermute | solution.py:395
  52.4 5.3 %collective-permute-done.18.refs_1_ = f32[552,128]{1,0:T(8,128)S(1)} collective-permute-done((f32[552,128]{1,0:T(8,128)S(1)}, f32[552,128]{1,0:T(8,128)S(1)}, u32[]{:S(2)}, u32[]{:S(2)}) %collective-permute-start.18) | collective-permute-done | bytes 282656 | tf_op jit(solution)/shard_map/ppermute | solution.py:395
  57.7 0.8 %shard_map.112 = (f32[1024,128]{1,0:T(8,128)}, f32[32,128]{1,0:T(8,128)}, f32[2]{0:T(128)}) custom-call(s32[1]{0:T(128)} %bitcast.idx, f32[552,128]{1,0:T(8,128)S(1)} %collective-permute-done.17.refs_0_, f32[552,128]{1,0:T(8,128)S(1)} %collective-permute-done.18.refs_1_), custom_call_target="tpu_custom_call" | custom-call | flops 1000000 | bytes 3690000 | tf_op jit(solution)/shard_map/pallas_call | solution.py:43
  (20 shorter events, 1.3 us)
Async XLA Ops:
  1.8 8.4 %collective-permute-start = (f32[592,128]{1,0:T(8,128)S(1)}, f32[592,128]{1,0:T(8,128)S(1)}, u32[]{:S(2)}, u32[]{:S(2)}) collective-permute-start(f32[592,128]{1,0:T(8,128)S(1)} %get-tuple-element.39), channel_id=1, source_target_pairs={{0,2},{1,0},{2,3},{3,1},{4,6},{5,4},{6,7},{7,5},{8,10},{9,8},{10,1... | collective-permute-start | bytes 909320 | tf_op jit(solution)/shard_map/ppermute | solution.py:395
  1.8 10.1 %collective-permute-start.1 = (f32[592,128]{1,0:T(8,128)S(1)}, f32[592,128]{1,0:T(8,128)S(1)}, u32[]{:S(2)}, u32[]{:S(2)}) collective-permute-start(f32[592,128]{1,0:T(8,128)S(1)} %get-tuple-element.40), channel_id=1, source_target_pairs={{0,0},{1,2},{2,1},{3,3},{4,4},{5,6},{6,5},{7,7},{8,8},{9,10},{10,9... | collective-permute-start | bytes 909320 | tf_op jit(solution)/shard_map/ppermute | solution.py:395
  8.2 10.3 %collective-permute-start.10 = (f32[512,128]{1,0:T(8,128)S(1)}, f32[512,128]{1,0:T(8,128)S(1)}, u32[]{:S(2)}, u32[]{:S(2)}) collective-permute-start(f32[512,128]{1,0:T(8,128)S(1)} %get-tuple-element.55), channel_id=1, source_target_pairs={{0,0},{1,2},{2,1},{3,3},{4,4},{5,6},{6,5},{7,7},{8,8},{9,10},{10,9... | collective-permute-start | bytes 786440 | tf_op jit(solution)/shard_map/ppermute | solution.py:395
  10.2 8.3 %collective-permute-start.9 = (f32[512,128]{1,0:T(8,128)S(1)}, f32[512,128]{1,0:T(8,128)S(1)}, u32[]{:S(2)}, u32[]{:S(2)}) collective-permute-start(f32[512,128]{1,0:T(8,128)S(1)} %get-tuple-element.54), channel_id=1, source_target_pairs={{0,2},{1,0},{2,3},{3,1},{4,6},{5,4},{6,7},{7,5},{8,10},{9,8},{10,1... | collective-permute-start | bytes 786440 | tf_op jit(solution)/shard_map/ppermute | solution.py:395
  13.3 8.0 %collective-permute-start.2 = (f32[32,16,128]{2,1,0:T(8,128)S(1)}, f32[32,16,128]{2,1,0:T(8,128)S(1)}, u32[]{:S(2)}, u32[]{:S(2)}) collective-permute-start(f32[32,16,128]{2,1,0:T(8,128)S(1)} %slice.6), channel_id=1, source_target_pairs={{0,1},{1,0},{2,3},{3,2},{4,5},{5,4},{6,7},{7,6},{8,9},{9,8},{10,11... | collective-permute-start | bytes 786440 | tf_op jit(solution)/shard_map/ppermute | solution.py:395
  13.8 8.5 %collective-permute-start.4 = (f32[33,16,128]{2,1,0:T(8,128)S(1)}, f32[33,16,128]{2,1,0:T(8,128)S(1)}, u32[]{:S(2)}, u32[]{:S(2)}) collective-permute-start(f32[33,16,128]{2,1,0:T(8,128)S(1)} %get-tuple-element.45), channel_id=1, source_target_pairs={{1,4},{4,1},{3,6},{6,3},{5,8},{8,5},{7,10},{10,7},{9,12},{12,9},{1... | collective-permute-start | bytes 811016 | tf_op jit(solution)/shard_map/ppermute | solution.py:395
  15.1 6.3 %collective-permute-start.3 = (f32[1,16,128]{2,1,0:T(8,128)S(1)}, f32[1,16,128]{2,1,0:T(8,128)S(1)}, u32[]{:S(2)}, u32[]{:S(2)}) collective-permute-start(f32[1,16,128]{2,1,0:T(8,128)S(1)} %slice.7), channel_id=1, source_target_pairs={{0,1},{1,0},{2,3},{3,2},{4,5},{5,4},{6,7},{7,6},{8,9},{9,8},{10,11... | collective-permute-start | bytes 24584 | tf_op jit(solution)/shard_map/ppermute | solution.py:395
  19.1 6.3 %collective-permute-start.11 = (f32[33,16,128]{2,1,0:T(8,128)S(1)}, f32[33,16,128]{2,1,0:T(8,128)S(1)}, u32[]{:S(2)}, u32[]{:S(2)}) collective-permute-start(f32[33,16,128]{2,1,0:T(8,128)S(1)} %get-tuple-element.58), channel_id=1, source_target_pairs={{0,1},{1,0},{2,3},{3,2},{4,5},{5,4},{6,7},{7,6},{8,9},{9,8},{10,11... | collective-permute-start | bytes 811016 | tf_op jit(solution)/shard_map/ppermute | solution.py:395
  19.1 9.4 %collective-permute-start.12 = (f32[33,16,128]{2,1,0:T(8,128)S(1)}, f32[33,16,128]{2,1,0:T(8,128)S(1)}, u32[]{:S(2)}, u32[]{:S(2)}) collective-permute-start(f32[33,16,128]{2,1,0:T(8,128)S(1)} %get-tuple-element.59), channel_id=1, source_target_pairs={{1,4},{4,1},{3,6},{6,3},{5,8},{8,5},{7,10},{10,7},{9,12},{12,9},{1... | collective-permute-start | bytes 811016 | tf_op jit(solution)/shard_map/ppermute | solution.py:395
  23.2 8.7 %collective-permute-start.5 = (f32[33,16,128]{2,1,0:T(8,128)S(1)}, f32[33,16,128]{2,1,0:T(8,128)S(1)}, u32[]{:S(2)}, u32[]{:S(2)}) collective-permute-start(f32[33,16,128]{2,1,0:T(8,128)S(1)} %get-tuple-element.48), channel_id=1, source_target_pairs={{0,1},{1,0},{2,3},{3,2},{4,5},{5,4},{6,7},{7,6},{8,9},{9,8},{10,11... | collective-permute-start | bytes 811016 | tf_op jit(solution)/shard_map/ppermute | solution.py:395
  24.8 9.5 %collective-permute-start.6 = (f32[33,16,128]{2,1,0:T(8,128)S(1)}, f32[33,16,128]{2,1,0:T(8,128)S(1)}, u32[]{:S(2)}, u32[]{:S(2)}) collective-permute-start(f32[33,16,128]{2,1,0:T(8,128)S(1)} %get-tuple-element.49), channel_id=1, source_target_pairs={{1,4},{4,1},{3,6},{6,3},{5,8},{8,5},{7,10},{10,7},{9,12},{12,9},{1... | collective-permute-start | bytes 811016 | tf_op jit(solution)/shard_map/ppermute | solution.py:395
  29.4 8.2 %collective-permute-start.13 = (f32[33,16,128]{2,1,0:T(8,128)S(1)}, f32[33,16,128]{2,1,0:T(8,128)S(1)}, u32[]{:S(2)}, u32[]{:S(2)}) collective-permute-start(f32[33,16,128]{2,1,0:T(8,128)S(1)} %get-tuple-element.62), channel_id=1, source_target_pairs={{0,1},{1,0},{2,3},{3,2},{4,5},{5,4},{6,7},{7,6},{8,9},{9,8},{10,11... | collective-permute-start | bytes 811016 | tf_op jit(solution)/shard_map/ppermute | solution.py:395
  30.7 9.3 %collective-permute-start.14 = (f32[33,16,128]{2,1,0:T(8,128)S(1)}, f32[33,16,128]{2,1,0:T(8,128)S(1)}, u32[]{:S(2)}, u32[]{:S(2)}) collective-permute-start(f32[33,16,128]{2,1,0:T(8,128)S(1)} %get-tuple-element.63), channel_id=1, source_target_pairs={{1,4},{4,1},{3,6},{6,3},{5,8},{8,5},{7,10},{10,7},{9,12},{12,9},{1... | collective-permute-start | bytes 811016 | tf_op jit(solution)/shard_map/ppermute | solution.py:395
  35.2 10.8 %collective-permute-start.7 = (f32[33,16,128]{2,1,0:T(8,128)S(1)}, f32[33,16,128]{2,1,0:T(8,128)S(1)}, u32[]{:S(2)}, u32[]{:S(2)}) collective-permute-start(f32[33,16,128]{2,1,0:T(8,128)S(1)} %get-tuple-element.52), channel_id=1, source_target_pairs={{0,1},{1,0},{2,3},{3,2},{4,5},{5,4},{6,7},{7,6},{8,9},{9,8},{10,11... | collective-permute-start | bytes 811016 | tf_op jit(solution)/shard_map/ppermute | solution.py:395
  36.5 9.5 %collective-permute-start.8 = (f32[33,16,128]{2,1,0:T(8,128)S(1)}, f32[33,16,128]{2,1,0:T(8,128)S(1)}, u32[]{:S(2)}, u32[]{:S(2)}) collective-permute-start(f32[33,16,128]{2,1,0:T(8,128)S(1)} %get-tuple-element.53), channel_id=1, source_target_pairs={{1,4},{4,1},{3,6},{6,3},{5,8},{8,5},{7,10},{10,7},{9,12},{12,9},{1... | collective-permute-start | bytes 811016 | tf_op jit(solution)/shard_map/ppermute | solution.py:395
  41.2 2.4 %collective-permute-start.15 = (f32[8,128]{1,0:T(8,128)S(1)}, f32[8,128]{1,0:T(8,128)S(1)}, u32[]{:S(2)}, u32[]{:S(2)}) collective-permute-start(f32[8,128]{1,0:T(8,128)S(1)} %get-tuple-element.68), channel_id=1, source_target_pairs={{0,1},{1,0},{2,3},{3,2},{4,5},{5,4},{6,7},{7,6},{8,9},{9,8},{10,11... | collective-permute-start | bytes 12296 | tf_op jit(solution)/shard_map/ppermute | solution.py:395
  42.6 3.4 %collective-permute-start.16 = (f32[8,128]{1,0:T(8,128)S(1)}, f32[8,128]{1,0:T(8,128)S(1)}, u32[]{:S(2)}, u32[]{:S(2)}) collective-permute-start(f32[8,128]{1,0:T(8,128)S(1)} %get-tuple-element.69), channel_id=1, source_target_pairs={{1,4},{4,1},{3,6},{6,3},{5,8},{8,5},{7,10},{10,7},{9,12},{12,9},{1... | collective-permute-start | bytes 12296 | tf_op jit(solution)/shard_map/ppermute | solution.py:395
  46.8 5.6 %collective-permute-start.17 = (f32[552,128]{1,0:T(8,128)S(1)}, f32[552,128]{1,0:T(8,128)S(1)}, u32[]{:S(2)}, u32[]{:S(2)}) collective-permute-start(f32[552,128]{1,0:T(8,128)S(1)} %get-tuple-element.77), channel_id=1, source_target_pairs={{2,0},{0,1},{3,2},{1,3},{6,4},{4,5},{7,6},{5,7},{10,8},{8,9},{11,1... | collective-permute-start | bytes 847880 | tf_op jit(solution)/shard_map/ppermute | solution.py:395
  48.9 8.9 %collective-permute-start.18 = (f32[552,128]{1,0:T(8,128)S(1)}, f32[552,128]{1,0:T(8,128)S(1)}, u32[]{:S(2)}, u32[]{:S(2)}) collective-permute-start(f32[552,128]{1,0:T(8,128)S(1)} %get-tuple-element.76), channel_id=1, source_target_pairs={{0,0},{1,2},{2,1},{3,3},{4,4},{5,6},{6,5},{7,7},{8,8},{9,10},{10,9... | collective-permute-start | bytes 847880 | tf_op jit(solution)/shard_map/ppermute | solution.py:395
